TPU v7x, 128 devices: a whole 4x4x4 slice. The times are simulated.
128 devices in a mesh: expert: 8 (over z, x_hi), replica: 16 (over y, x_lo, core).
Axes of the slice: x: 4 (x_hi: 2, x_lo: 2; x = x_hi * 2 + x_lo), y: 4, z: 4, core: 2. Of those that a mesh axis runs over, the one named last changes fastest.
Arguments:
- tokens: bfloat16 [32768, 512], P(('expert', 'replica')), may hold values from -6 to 6
- expert_ids: int32 [32768, 2], P(('expert', 'replica')), may hold values from 0 to 23, all different within a row; in each aligned block of 256 rows (0 to 255, 256 to 511, ...) at most 48 rows name the same one
- gates: float32 [32768, 2], P(('expert', 'replica')), may hold values from 0.2 to 1
- cotangent: bfloat16 [32768, 512], P(('expert', 'replica')), may hold values from -3 to 3
- w_gate: bfloat16 [24, 512, 2048], P('expert'), may hold values from -0.25 to 0.25
- w_up: bfloat16 [24, 512, 2048], P('expert'), may hold values from -0.25 to 0.25
- w_down: bfloat16 [24, 2048, 512], P('expert'), may hold values from -0.125 to 0.125
Outputs:
- mixed: bfloat16 [32768, 512], P(('expert', 'replica'))
- token_grad: bfloat16 [32768, 512], P(('expert', 'replica'))
- gate_grad: bfloat16 [24, 512, 2048], P('expert', None, 'replica')
- up_grad: bfloat16 [24, 512, 2048], P('expert', None, 'replica')
- down_grad: bfloat16 [24, 2048, 512], P('expert', 'replica')
Inputs may be any that keep to these rules, and one draw needn't show every extreme that they name: `expert_ids`: each token names two different experts. Among the 512 entries of one device's tokens, no expert is named more than 48 times, and in some devices some expert is named exactly 48 times.
All inputs are finite; a program needn't handle non-finite values.
Results may differ from a plain program's by a relative error of at most 0.022.
Values may be sent and summed in bfloat16 or wider, within the bound.
No kernel may reach another device: no remote copies, remote signals or barrier semaphores. Data moves between devices by JAX's collectives and lax.ppermute only.
A program may use at most 128 MiB of HBM per device.

v0:
```python
import functools

import jax
import jax.numpy as jnp
from jax import lax
from jax.experimental import pallas as pl
from jax.experimental.pallas import tpu as pltpu
from jax.sharding import PartitionSpec as P

CAP = 48
LOCAL = 3
SOURCES = 8
ROWS = SOURCES * CAP
D = 512
TOK = 256
BLK = 128
META = 16
F32 = jnp.float32
BF16 = jnp.bfloat16
VMEM_LIMIT = 48 * 1024 * 1024
VMEM = pl.BlockSpec(memory_space=pltpu.VMEM)
SMEM = pl.BlockSpec(memory_space=pltpu.SMEM)


def dot(a, b, ca=1, cb=0):
    return lax.dot_general(a, b, (((ca,), (cb,)), ((), ())), preferred_element_type=F32)


def bf16_like(*shape):
    return jax.ShapeDtypeStruct(shape, BF16)


def call(kernel, name, in_specs, out_shape, args, nbytes=10**6, scratch=()):
    return pl.pallas_call(
        kernel,
        in_specs=in_specs,
        out_specs=jax.tree.map(lambda _: VMEM, out_shape),
        out_shape=out_shape,
        scratch_shapes=list(scratch),
        compiler_params=pltpu.CompilerParams(vmem_limit_bytes=VMEM_LIMIT),
        cost_estimate=pl.CostEstimate(flops=0, bytes_accessed=nbytes, transcendentals=0),
        name=name,
    )(*args)


def along_z(dz):
    return [(z * 2 + h, ((z + dz) % 4) * 2 + h) for z in range(4) for h in range(2)]


PARTNER = [(e, e ^ 1) for e in range(8)]
CORE = [(r, r ^ 1) for r in range(16)]
ACROSS = [(r, r ^ 2) for r in range(16)]
RING = [(r, (r + (4 if r % 2 == 0 else 12)) % 16) for r in range(16)]


def pack_kernel(tokens_ref, cot_ref, ids_ref, gates_ref, out_ref):
    out_ref[0:TOK] = tokens_ref[...]
    out_ref[TOK : 2 * TOK] = cot_ref[...]
    gates = gates_ref[...]
    high = gates.astype(BF16).astype(F32)
    middle = (gates - high).astype(BF16).astype(F32)
    low = gates - high - middle
    meta = jnp.concatenate(
        [ids_ref[...].astype(F32), high, middle, low, jnp.zeros((META - 8, TOK), F32)], axis=0
    )
    out_ref[2 * TOK :] = jnp.concatenate([meta, jnp.zeros_like(meta)], axis=1).astype(BF16)


def read_meta(packed_ref):
    meta = packed_ref[2 * TOK :, 0:TOK].astype(F32)
    gates = meta[2:4] + meta[4:6] + meta[6:8]
    return meta[0:2], gates


def dispatch_kernel(me_ref, packed_ref, *out_refs):
    z, h = me_ref[0] >> 1, me_ref[0] & 1
    ids, gates = read_meta(packed_ref)
    count = 4 * LOCAL
    index = lax.broadcasted_iota(jnp.int32, (16, TOK), 0)
    want = (((z + (index & 3)) & 3) * 2 + h) * LOCAL + (index >> 2)
    want = jnp.where(index < count, want, -1).astype(F32)
    hit0 = ids[0:1] == want
    hit1 = ids[1:2] == want
    hit = jnp.where(hit0 | hit1, 1.0, 0.0).astype(F32)
    gate = jnp.where(hit0, gates[0:1], jnp.where(hit1, gates[1:2], 0.0))
    earlier = lax.broadcasted_iota(jnp.int32, (TOK, TOK), 0) < lax.broadcasted_iota(
        jnp.int32, (TOK, TOK), 1
    )
    before = dot(hit.astype(BF16), jnp.where(earlier, 1.0, 0.0).astype(BF16))
    place = jnp.where(hit > 0.0, before, -1.0).astype(jnp.int32)
    slot = lax.broadcasted_iota(jnp.int32, (CAP, TOK), 0)
    for j in range(LOCAL):
        picks, weights = [], []
        for n in range(j * 4, j * 4 + 4):
            sel = slot == place[n : n + 1]
            picks.append(jnp.where(sel, 1.0, 0.0).astype(BF16))
            weights.append(jnp.sum(jnp.where(sel, gate[n : n + 1], 0.0), axis=1, keepdims=True))
        pick = jnp.concatenate(picks, axis=0)
        weight = jnp.concatenate(weights, axis=0)
        rows = dot(pick, packed_ref[0:TOK]).astype(BF16)
        grads = (weight * dot(pick, packed_ref[TOK : 2 * TOK])).astype(BF16)
        for dz in range(4):
            part = slice(dz * CAP, (dz + 1) * CAP)
            if j == 0:
                out_refs[dz][0] = rows[part]
                out_refs[dz][1] = grads[part]
            else:
                out_refs[4 + dz][j - 1, 0] = rows[part]
                out_refs[4 + dz][j - 1, 1] = grads[part]


def dispatch(name, me, packed):
    out = [bf16_like(2, CAP, D)] * 4 + [bf16_like(2, 2, CAP, D)] * 4
    return call(dispatch_kernel, name, [SMEM, VMEM], out, (me, packed), 3 * 10**6)


def join_first_kernel(*refs):
    for n, ref in enumerate(refs[:-1]):
        refs[-1][n] = ref[...]


def join_rest_kernel(*refs):
    for n, ref in enumerate(refs[:-2]):
        refs[-2][n] = ref[0]
        refs[-1][n] = ref[1]


def expert_kernel(
    tbl_ref, own_ref, oth_ref, after_ref, wg0, wg1, wu0, wu1, wd0, wd1,
    far, mid, near, home0, home1, ret_own, ret_oth,
    x_s, g_s, xt_s, gt_s, eo_s, ig_s,
):
    i = pl.program_id(0)

    @pl.when(i == 0)
    def _():
        for k, ref in enumerate((own_ref, oth_ref)):
            x_s[k * ROWS : (k + 1) * ROWS, :] = ref[:, 0].reshape(ROWS, D)
            g_s[k * ROWS : (k + 1) * ROWS, :] = ref[:, 1].reshape(ROWS, D)
        xt_s[...] = x_s[...].T
        gt_s[...] = g_s[...].T
        eo_s[...] = jnp.zeros_like(eo_s)
        ig_s[...] = jnp.zeros_like(ig_s)

    wg = jnp.concatenate([wg0[...], wg1[...]], axis=1)
    wu = jnp.concatenate([wu0[...], wu1[...]], axis=1)
    wd = jnp.concatenate([wd0[...], wd1[...]], axis=0)
    x = x_s[...]
    g = g_s[...]
    pre_gate = dot(x, wg)
    pre_up = dot(x, wu)
    grad_hidden = dot(g, wd, 1, 1)
    sig = jax.nn.sigmoid(pre_gate)
    silu = pre_gate * sig
    hidden = (silu * pre_up).astype(BF16)
    grad_gate = (grad_hidden * pre_up * sig * (1.0 + pre_gate * (1.0 - sig))).astype(BF16)
    grad_up = (grad_hidden * silu).astype(BF16)
    part_gate = dot(xt_s[...], grad_gate).astype(BF16)
    part_up = dot(xt_s[...], grad_up).astype(BF16)
    part_down = dot(gt_s[...], hidden).astype(BF16)

    def keep(ref, lane):
        for k, part in enumerate((part_gate, part_up, part_down)):
            ref[k * D : (k + 1) * D, :] = part[:, lane * BLK : (lane + 1) * BLK]

    homes = (far.at[0], far.at[1]), (mid.at[0], mid.at[1]), (near.at[0], near.at[1]), (home0, home1)
    for step, (a, b) in enumerate(homes):

        @pl.when(i == step)
        def _(a=a, b=b):
            keep(a, 0)
            keep(b, 1)

    eo_s[...] += dot(hidden, wd)
    ig_s[...] += dot(grad_gate, wg, 1, 1) + dot(grad_up, wu, 1, 1)

    @pl.when(i == 3)
    def _():
        for k, ref in enumerate((ret_own, ret_oth)):
            ref[0] = eo_s[k * ROWS : (k + 1) * ROWS, :].astype(BF16)
            ref[1] = ig_s[k * ROWS : (k + 1) * ROWS, :].astype(BF16)


def expert(j, tbl, own, oth, after, w_gate, w_up, w_down):
    rows = 2 * ROWS

    def fixed(shape):
        return pl.BlockSpec(shape, lambda i, tbl: (0,) * len(shape))

    def columns(k):
        return pl.BlockSpec((None, D, BLK), lambda i, tbl: (j, 0, tbl[2 * i + k]))

    def lines(k):
        return pl.BlockSpec((None, BLK, D), lambda i, tbl: (j, tbl[2 * i + k], 0))

    chunk, ret = (3 * D, BLK), (2, ROWS, D)
    out_shapes = [(2,) + chunk] * 3 + [chunk] * 2 + [ret] * 2
    return pl.pallas_call(
        expert_kernel,
        grid_spec=pltpu.PrefetchScalarGridSpec(
            num_scalar_prefetch=1,
            grid=(4,),
            in_specs=[fixed(own.shape), fixed(oth.shape), pl.BlockSpec(memory_space=pl.ANY)]
            + [columns(0), columns(1), columns(0), columns(1), lines(0), lines(1)],
            out_specs=[fixed(s) for s in out_shapes],
            scratch_shapes=[
                pltpu.VMEM((rows, D), BF16),
                pltpu.VMEM((rows, D), BF16),
                pltpu.VMEM((D, rows), BF16),
                pltpu.VMEM((D, rows), BF16),
                pltpu.VMEM((rows, D), F32),
                pltpu.VMEM((rows, D), F32),
            ],
        ),
        out_shape=[bf16_like(*s) for s in out_shapes],
        compiler_params=pltpu.CompilerParams(
            dimension_semantics=("arbitrary",), vmem_limit_bytes=VMEM_LIMIT
        ),
        cost_estimate=pl.CostEstimate(flops=0, bytes_accessed=2 * 10**6, transcendentals=0),
        name=f"expert{j}",
    )(tbl, own, oth, after, w_gate, w_gate, w_up, w_up, w_down, w_down)


def back_kernel(count, *refs):
    ins, outs = refs[: 2 * count], refs[2 * count :]
    for j in range(count):
        own_ref, oth_ref = ins[2 * j : 2 * j + 2]
        for n in range(SOURCES):
            for k in range(2):
                rows = slice(n * CAP, (n + 1) * CAP)
                total = own_ref[k, rows].astype(F32) + oth_ref[k, rows].astype(F32)
                outs[n & 3][j, n >> 2, k] = total.astype(BF16)


def back(name, pairs):
    count = len(pairs) // 2
    out = [bf16_like(count, 2, 2, CAP, D)] * 4
    return call(
        functools.partial(back_kernel, count), name, [VMEM] * len(pairs), out, pairs, 3 * 10**6
    )


def token_sums(side, me_ref, packed_ref, rows, out_s, in_s):
    z, h = me_ref[0] >> 1, me_ref[0] & 1
    for dz in range(4):
        first, last = rows[dz], rows[4 + dz]
        for j in range(LOCAL):
            ref, at = (first, j) if j < LOCAL - 1 else (last, 0)
            n = j * 4 + dz
            out_s[n * CAP : (n + 1) * CAP, :] = ref[at, side, 0]
            in_s[n * CAP : (n + 1) * CAP, :] = ref[at, side, 1]
    ids, gates = read_meta(packed_ref)
    columns = jnp.concatenate([ids, gates, jnp.zeros((4, TOK), F32)], axis=0).T
    lane = lax.broadcasted_iota(jnp.int32, (TOK, 128), 1)
    want = (((z + (lane & 3)) & 3) * 2 + h) * LOCAL + (lane >> 2)
    want = jnp.where(lane < 4 * LOCAL, want, -1).astype(F32)
    hits = [columns[:, k : k + 1] == want for k in range(2)]
    either = jnp.where(hits[0] | hits[1], 1.0, 0.0).astype(BF16)
    earlier = lax.broadcasted_iota(jnp.int32, (TOK, TOK), 1) < lax.broadcasted_iota(
        jnp.int32, (TOK, TOK), 0
    )
    before = dot(jnp.where(earlier, 1.0, 0.0).astype(BF16), either)
    code = before + (lane * CAP + 1).astype(F32)
    slots = lax.broadcasted_iota(jnp.int32, (TOK, 4 * LOCAL * CAP), 1)
    picks = []
    for k in range(2):
        slot = jnp.sum(jnp.where(hits[k], code, 0.0), axis=1, keepdims=True).astype(jnp.int32) - 1
        picks.append(jnp.where(slots == slot, 1.0, 0.0).astype(BF16))
    mixed = columns[:, 2:3] * dot(picks[0], out_s[...]) + columns[:, 3:4] * dot(picks[1], out_s[...])
    return mixed, dot(picks[0] + picks[1], in_s[...])


def partner_kernel(me_ref, packed_ref, *refs):
    rows, (out_ref, out_s, in_s) = refs[:-3], refs[-3:]
    mixed, grad = token_sums(1, me_ref, packed_ref, rows, out_s, in_s)
    out_ref[0] = mixed.astype(BF16)
    out_ref[1] = grad.astype(BF16)


def combine_kernel(me_ref, packed_ref, other_ref, *refs):
    rows, (mixed_ref, grad_ref, out_s, in_s) = refs[:-4], refs[-4:]
    mixed, grad = token_sums(0, me_ref, packed_ref, rows, out_s, in_s)
    mixed_ref[...] = (mixed + other_ref[0].astype(F32)).astype(BF16)
    grad_ref[...] = (grad + other_ref[1].astype(F32)).astype(BF16)


def finish_kernel(*refs):
    ins, outs = refs[: 2 * LOCAL], refs[2 * LOCAL :]
    for j in range(LOCAL):
        total = (ins[2 * j][...].astype(F32) + ins[2 * j + 1][...].astype(F32)).astype(BF16)
        outs[0][j] = total[0:D]
        outs[1][j] = total[D : 2 * D]
        outs[2][j] = total[2 * D :].T


def add(*terms):
    return functools.reduce(lambda a, b: a + b, [t.astype(F32) for t in terms]).astype(BF16)


def local(tokens, expert_ids, gates, cotangent, w_gate, w_up, w_down):
    me = lax.axis_index("expert").astype(jnp.int32).reshape(1)
    rep = lax.axis_index("replica").astype(jnp.int32)
    y, x, core = rep >> 2, (rep >> 1) & 1, rep & 1
    step = jnp.arange(8, dtype=jnp.int32)
    away = (3 - (step >> 1)) * (1 - 2 * core)
    tbl = ((y + away) & 3) * 4 + (x ^ (step & 1)) * 2 + core

    def over_replica(value, perm):
        return lax.ppermute(value, "replica", perm)

    def to_z(value, dz):
        return lax.ppermute(value, "expert", along_z(dz))

    packed = call(
        pack_kernel,
        "pack",
        [VMEM] * 4,
        bf16_like(2 * TOK + META, D),
        (tokens, cotangent, expert_ids.T, gates.T),
    )
    partner = lax.ppermute(packed, "expert", PARTNER)
    firsts, rests = [], []
    for name, source in (("own_slots", packed), ("partner_slots", partner)):
        sent = dispatch(name, me, source)
        firsts += [sent[0]] + [to_z(sent[dz], dz) for dz in range(1, 4)]
        rests += [sent[4]] + [to_z(sent[4 + dz], dz) for dz in range(1, 4)]
    joined = bf16_like(SOURCES, 2, CAP, D)
    received = [call(join_first_kernel, "join0", [VMEM] * 8, joined, firsts)]
    received += call(join_rest_kernel, "join12", [VMEM] * 8, [joined] * 2, rests)

    parts, pairs = [], []
    after = me
    for j in range(LOCAL):
        own = received[j]
        oth = over_replica(own, CORE)
        far, mid, near, home0, home1, ret_own, ret_oth = expert(
            j, tbl, own, oth, after, w_gate, w_up, w_down
        )
        after = home0
        total = over_replica(far, RING)
        total = over_replica(add(mid, total), RING)
        total = over_replica(add(near, total), RING)
        across = over_replica(add(home1, total[1]), ACROSS)
        parts += [add(home0, total[0]), across]
        pairs += [ret_own, over_replica(ret_oth, CORE)]

    rows = []
    for name, some in (("back01", pairs[:4]), ("back2", pairs[4:])):
        sums = back(name, some)
        rows += [sums[0]] + [to_z(sums[dz], 4 - dz) for dz in range(1, 4)]
    scratch = [pltpu.VMEM((4 * LOCAL * CAP, D), BF16)] * 2
    theirs = call(
        partner_kernel, "partner_sums", [SMEM] + [VMEM] * 9, bf16_like(2, TOK, D),
        (me, partner, *rows), 3 * 10**6, scratch,
    )
    mixed, token_grad = call(
        combine_kernel, "combine", [SMEM] + [VMEM] * 10, [bf16_like(TOK, D)] * 2,
        (me, packed, lax.ppermute(theirs, "expert", PARTNER), *rows), 3 * 10**6, scratch,
    )
    gate_grad, up_grad, down_grad = call(
        finish_kernel, "finish", [VMEM] * len(parts),
        [bf16_like(LOCAL, D, BLK), bf16_like(LOCAL, D, BLK), bf16_like(LOCAL, BLK, D)],
        parts, 4 * 10**6,
    )
    return mixed, token_grad, gate_grad, up_grad, down_grad


def solution(mesh):
    tokens = P(("expert", "replica"), None)
    return jax.shard_map(
        local,
        mesh=mesh,
        in_specs=(tokens,) * 4 + (P("expert", None, None),) * 3,
        out_specs=(tokens,) * 2
        + (P("expert", None, "replica"), P("expert", None, "replica"), P("expert", "replica", None)),
        check_vma=False,
    )
```

profile of v0, /device:TPU:0, one launch (start us, length us, event | category | flops | bytes accessed | tf_op | source)
XLA Modules:
  0.0 190.1 jit_solution(2788473255296733599)
XLA Ops:
  0.6 0.9 copy-done.4
  1.6 0.9 copy-done.5
  2.5 0.7 copy-done.6
  3.2 0.7 copy-done.7
  4.0 3.2 %collective-permute-start = (bf16[528,512]{1,0:T(8,128)(2,1)S(1)}, bf16[528,512]{1,0:T(8,128)(2,1)S(1)}, u32[]{:S(2)}, u32[]{:S(2)}) collective-permute-start(bf16[528,512]{1,0:T(8,128)(2,1)S(1)} %pack.1.packed_ref), channel_id=1, source_target_pairs={{0,16},{16,0},{32,48},{48,32},{64,80},{80,64},{96,112},{112,96},{1... | collective-permute-start | bytes 1622024 | tf_op jit(solution)/shard_map/ppermute | solution.py:321
  7.1 0.7 own_slots.1
  7.9 2.0 %collective-permute-start.1 = (bf16[2,48,512]{2,1,0:T(8,128)(2,1)S(1)}, bf16[2,48,512]{2,1,0:T(8,128)(2,1)S(1)}, u32[]{:S(2)}, u32[]{:S(2)}) collective-permute-start(bf16[2,48,512]{2,1,0:T(8,128)(2,1)S(1)} %get-tuple-element.58), channel_id=1, source_target_pairs={{0,32},{16,48},{32,64},{48,80},{64,96},{80,112},{96,0},{112,16},{1... | collective-permute-start | bytes 294920 | tf_op jit(solution)/shard_map/ppermute | solution.py:312
  9.8 3.6 %collective-permute-start.2 = (bf16[2,48,512]{2,1,0:T(8,128)(2,1)S(1)}, bf16[2,48,512]{2,1,0:T(8,128)(2,1)S(1)}, u32[]{:S(2)}, u32[]{:S(2)}) collective-permute-start(bf16[2,48,512]{2,1,0:T(8,128)(2,1)S(1)} %get-tuple-element.59), channel_id=1, source_target_pairs={{0,64},{16,80},{32,96},{48,112},{64,0},{80,16},{96,32},{112,48},{1... | collective-permute-start | bytes 294920 | tf_op jit(solution)/shard_map/ppermute | solution.py:312
  13.4 1.0 collective-permute-start.3
  14.4 5.0 %collective-permute-done.packed_ref = bf16[528,512]{1,0:T(8,128)(2,1)S(1)} collective-permute-done((bf16[528,512]{1,0:T(8,128)(2,1)S(1)}, bf16[528,512]{1,0:T(8,128)(2,1)S(1)}, u32[]{:S(2)}, u32[]{:S(2)}) %collective-permute-start) | collective-permute-done | bytes 540704 | tf_op jit(solution)/shard_map/ppermute | solution.py:321
  19.4 0.7 partner_slots.1
  20.1 2.2 %collective-permute-start.4 = (bf16[2,48,512]{2,1,0:T(8,128)(2,1)S(1)}, bf16[2,48,512]{2,1,0:T(8,128)(2,1)S(1)}, u32[]{:S(2)}, u32[]{:S(2)}) collective-permute-start(bf16[2,48,512]{2,1,0:T(8,128)(2,1)S(1)} %get-tuple-element.62), channel_id=1, source_target_pairs={{0,32},{16,48},{32,64},{48,80},{64,96},{80,112},{96,0},{112,16},{1... | collective-permute-start | bytes 294920 | tf_op jit(solution)/shard_map/ppermute | solution.py:312
  22.3 3.6 %collective-permute-start.5 = (bf16[2,48,512]{2,1,0:T(8,128)(2,1)S(1)}, bf16[2,48,512]{2,1,0:T(8,128)(2,1)S(1)}, u32[]{:S(2)}, u32[]{:S(2)}) collective-permute-start(bf16[2,48,512]{2,1,0:T(8,128)(2,1)S(1)} %get-tuple-element.63), channel_id=1, source_target_pairs={{0,64},{16,80},{32,96},{48,112},{64,0},{80,16},{96,32},{112,48},{1... | collective-permute-start | bytes 294920 | tf_op jit(solution)/shard_map/ppermute | solution.py:312
  25.9 1.0 collective-permute-start.6
  26.9 1.2 collective-permute-done.4.refs_5_
  28.1 1.6 collective-permute-done.5.refs_6_
  29.7 0.8 collective-permute-done.6.refs_7_
  30.7 0.6 collective-permute-start.9
  31.3 3.1 %collective-permute-start.10 = (bf16[2,2,48,512]{3,2,1,0:T(8,128)(2,1)S(1)}, bf16[2,2,48,512]{3,2,1,0:T(8,128)(2,1)S(1)}, u32[]{:S(2)}, u32[]{:S(2)}) collective-permute-start(bf16[2,2,48,512]{3,2,1,0:T(8,128)(2,1)S(1)} %get-tuple-element.69), channel_id=1, source_target_pairs={{0,64},{16,80},{32,96},{48,112},{64,0},{80,16},{96,32},{112,48},{1... | collective-permute-start | bytes 589832 | tf_op jit(solution)/shard_map/ppermute | solution.py:312
  34.4 0.5 collective-permute-start.11
  34.9 1.5 collective-permute-start.12
  36.5 3.7 %collective-permute-done.9.refs_1_ = bf16[2,2,48,512]{3,2,1,0:T(8,128)(2,1)S(1)} collective-permute-done((bf16[2,2,48,512]{3,2,1,0:T(8,128)(2,1)S(1)}, bf16[2,2,48,512]{3,2,1,0:T(8,128)(2,1)S(1)}, u32[]{:S(2)}, u32[]{:S(2)}) %collective-permute-start.9) | collective-permute-done | bytes 196640 | tf_op jit(solution)/shard_map/ppermute | solution.py:312
  40.2 4.2 %collective-permute-done.10.refs_2_ = bf16[2,2,48,512]{3,2,1,0:T(8,128)(2,1)S(1)} collective-permute-done((bf16[2,2,48,512]{3,2,1,0:T(8,128)(2,1)S(1)}, bf16[2,2,48,512]{3,2,1,0:T(8,128)(2,1)S(1)}, u32[]{:S(2)}, u32[]{:S(2)}) %collective-permute-start.10) | collective-permute-done | bytes 196640 | tf_op jit(solution)/shard_map/ppermute | solution.py:312
  44.4 0.4 collective-permute-done.11.refs_3_
  44.8 2.8 %collective-permute-done.12.refs_5_ = bf16[2,2,48,512]{3,2,1,0:T(8,128)(2,1)S(1)} collective-permute-done((bf16[2,2,48,512]{3,2,1,0:T(8,128)(2,1)S(1)}, bf16[2,2,48,512]{3,2,1,0:T(8,128)(2,1)S(1)}, u32[]{:S(2)}, u32[]{:S(2)}) %collective-permute-start.12) | collective-permute-done | bytes 196640 | tf_op jit(solution)/shard_map/ppermute | solution.py:312
  47.6 4.7 %collective-permute-done.13.refs_6_ = bf16[2,2,48,512]{3,2,1,0:T(8,128)(2,1)S(1)} collective-permute-done((bf16[2,2,48,512]{3,2,1,0:T(8,128)(2,1)S(1)}, bf16[2,2,48,512]{3,2,1,0:T(8,128)(2,1)S(1)}, u32[]{:S(2)}, u32[]{:S(2)}) %collective-permute-start.13) | collective-permute-done | bytes 196640 | tf_op jit(solution)/shard_map/ppermute | solution.py:312
  52.5 1.0 join12.1
  53.5 0.5 collective-permute-start.20
  54.0 14.1 %expert0.1 = (bf16[2,1536,128]{2,1,0:T(8,128)(2,1)S(1)}, bf16[2,1536,128]{2,1,0:T(8,128)(2,1)S(1)}, bf16[2,1536,128]{2,1,0:T(8,128)(2,1)S(1)}, bf16[1536,128]{1,...) custom-call(s32[8]{0:T(128)S(1)} %add_add_fusion.tbl_ref, ...), custom_call_target="tpu_custom_call" | custom-call | bytes 2000000 | tf_op jit(solution)/shard_map/expert0/pallas_call | solution.py:198
  68.2 1.8 collective-permute-start.26
  70.0 15.5 %expert1.1 = (bf16[2,1536,128]{2,1,0:T(8,128)(2,1)}, bf16[2,1536,128]{2,1,0:T(8,128)(2,1)S(1)}, bf16[2,1536,128]{2,1,0:T(8,128)(2,1)S(1)}, bf16[1536,128]{1,0:T(...) custom-call(s32[8]{0:T(128)S(1)} %add_add_fusion.tbl_ref, ...), custom_call_target="tpu_custom_call" | custom-call | bytes 2000000 | tf_op jit(solution)/shard_map/expert1/pallas_call | solution.py:198
  85.5 14.9 %expert2.1 = (bf16[2,1536,128]{2,1,0:T(8,128)(2,1)}, bf16[2,1536,128]{2,1,0:T(8,128)(2,1)S(1)}, bf16[2,1536,128]{2,1,0:T(8,128)(2,1)S(1)}, bf16[1536,128]{1,0:T(...) custom-call(s32[8]{0:T(128)S(1)} %add_add_fusion.tbl_ref, ...), custom_call_target="tpu_custom_call" | custom-call | bytes 2000000 | tf_op jit(solution)/shard_map/expert2/pallas_call | solution.py:198
  100.4 1.2 collective-permute-start.21
  101.7 0.4 collective-permute-start.16
  102.1 0.5 collective-permute-start.30
  102.7 1.3 collective-permute-start.34
  104.0 1.3 add_convert_fusion.5
  105.3 0.4 collective-permute-start.27
  105.9 2.7 %collective-permute-start.22 = (bf16[1,2,2,48,512]{4,3,2,1,0:T(8,128)(2,1)S(1)}, bf16[1,2,2,48,512]{4,3,2,1,0:T(8,128)(2,1)S(1)}, u32[]{:S(2)}, u32[]{:S(2)}) collective-permute-start(bf16[1,2,2,48,512]{4,3,2,1,0:T(8,128)(2,1)S(1)} %get-tuple-element.88), channel_id=1, source_target_pairs={{0,96},{16,112},{32,0},{48,16},{64,32},{80,48},{96,64},{112,80},{1... | collective-permute-start | bytes 589832 | tf_op jit(solution)/shard_map/ppermute | solution.py:312
  108.9 6.7 %collective-permute-done.30 = bf16[2,1536,128]{2,1,0:T(8,128)(2,1)} collective-permute-done((bf16[2,1536,128]{2,1,0:T(8,128)(2,1)}, bf16[2,1536,128]{2,1,0:T(8,128)(2,1)}, u32[]{:S(2)}, u32[]{:S(2)}) %collective-permute-start.30) | collective-permute-done | bytes 786464 | tf_op jit(solution)/shard_map/ppermute | solution.py:309
  115.7 0.9 collective-permute-start.24
  116.5 2.2 %add_convert_fusion.3 = bf16[2,1536,128]{2,1,0:T(8,128)(2,1)} fusion(bf16[2,1536,128]{2,1,0:T(8,128)(2,1)} %collective-permute-done.30, bf16[2,1536,128]{2,1,0:T(8,128)(2,1)S(1)} %get-tuple-element.98), kind=kLoop, calls=%fused_computation.3 | loop fusion | flops 1572864 | bytes 2359296 | tf_op jit(solution)/shard_map/convert_element_type | solution.py:297
  118.7 0.4 back01.1
  119.1 5.0 %collective-permute-done.34 = bf16[2,1536,128]{2,1,0:T(8,128)(2,1)} collective-permute-done((bf16[2,1536,128]{2,1,0:T(8,128)(2,1)}, bf16[2,1536,128]{2,1,0:T(8,128)(2,1)}, u32[]{:S(2)}, u32[]{:S(2)}) %collective-permute-start.34) | collective-permute-done | bytes 786464 | tf_op jit(solution)/shard_map/ppermute | solution.py:309
  124.1 2.6 %collective-permute-start.17 = (bf16[2,2,2,48,512]{4,3,2,1,0:T(8,128)(2,1)S(1)}, bf16[2,2,2,48,512]{4,3,2,1,0:T(8,128)(2,1)S(1)}, u32[]{:S(2)}, u32[]{:S(2)}) collective-permute-start(bf16[2,2,2,48,512]{4,3,2,1,0:T(8,128)(2,1)S(1)} %get-tuple-element.80), channel_id=1, source_target_pairs={{0,96},{16,112},{32,0},{48,16},{64,32},{80,48},{96,64},{112,80},{1... | collective-permute-start | bytes 1179656 | tf_op jit(solution)/shard_map/ppermute | solution.py:312
  127.0 0.6 collective-permute-start.19
  127.6 1.3 add_convert_fusion.1
  128.9 12.8 %collective-permute-done.17.refs_1_ = bf16[2,2,2,48,512]{4,3,2,1,0:T(8,128)(2,1)S(1)} collective-permute-done((bf16[2,2,2,48,512]{4,3,2,1,0:T(8,128)(2,1)S(1)}, bf16[2,2,2,48,512]{4,3,2,1,0:T(8,128)(2,1)S(1)}, u32[]{:S(2)}, u32[]{:S(2)}) %collective-permute-start.17) | collective-permute-done | bytes 393248 | tf_op jit(solution)/shard_map/ppermute | solution.py:312
  141.8 0.8 collective-permute-start.35
  142.6 2.6 %collective-permute-done.19.refs_3_ = bf16[2,2,2,48,512]{4,3,2,1,0:T(8,128)(2,1)S(1)} collective-permute-done((bf16[2,2,2,48,512]{4,3,2,1,0:T(8,128)(2,1)S(1)}, bf16[2,2,2,48,512]{4,3,2,1,0:T(8,128)(2,1)S(1)}, u32[]{:S(2)}, u32[]{:S(2)}) %collective-permute-start.19) | collective-permute-done | bytes 393248 | tf_op jit(solution)/shard_map/ppermute | solution.py:312
  145.2 1.4 partner_sums.1
  146.7 3.1 %collective-permute-start.25 = (bf16[2,256,512]{2,1,0:T(8,128)(2,1)S(1)}, bf16[2,256,512]{2,1,0:T(8,128)(2,1)S(1)}, u32[]{:S(2)}, u32[]{:S(2)}) collective-permute-start(bf16[2,256,512]{2,1,0:T(8,128)(2,1)S(1)} %partner_sums.1), channel_id=1, source_target_pairs={{0,16},{16,0},{32,48},{48,32},{64,80},{80,64},{96,112},{112,96},{1... | collective-permute-start | bytes 1572872 | tf_op jit(solution)/shard_map/ppermute | solution.py:358
  150.0 0.9 collective-permute-start.28
  151.1 1.4 collective-permute-start.32
  152.4 2.5 %collective-permute-done.35 = bf16[2,1536,128]{2,1,0:T(8,128)(2,1)S(1)} collective-permute-done((bf16[2,1536,128]{2,1,0:T(8,128)(2,1)S(1)}, bf16[2,1536,128]{2,1,0:T(8,128)(2,1)S(1)}, u32[]{:S(2)}, u32[]{:S(2)}) %collective-permute-start.35) | collective-permute-done | bytes 786464 | tf_op jit(solution)/shard_map/ppermute | solution.py:309
  155.3 8.1 %collective-permute-done.28 = bf16[2,1536,128]{2,1,0:T(8,128)(2,1)S(1)} collective-permute-done((bf16[2,1536,128]{2,1,0:T(8,128)(2,1)S(1)}, bf16[2,1536,128]{2,1,0:T(8,128)(2,1)S(1)}, u32[]{:S(2)}, u32[]{:S(2)}) %collective-permute-start.28) | collective-permute-done | bytes 786464 | tf_op jit(solution)/shard_map/ppermute | solution.py:309
  163.6 1.6 collective-permute-start.29
  165.2 6.6 %collective-permute-done.32 = bf16[2,1536,128]{2,1,0:T(8,128)(2,1)S(1)} collective-permute-done((bf16[2,1536,128]{2,1,0:T(8,128)(2,1)S(1)}, bf16[2,1536,128]{2,1,0:T(8,128)(2,1)S(1)}, u32[]{:S(2)}, u32[]{:S(2)}) %collective-permute-start.32) | collective-permute-done | bytes 786464 | tf_op jit(solution)/shard_map/ppermute | solution.py:309
  172.0 1.6 collective-permute-start.33
  173.6 6.6 %collective-permute-done.36 = bf16[2,1536,128]{2,1,0:T(8,128)(2,1)S(1)} collective-permute-done((bf16[2,1536,128]{2,1,0:T(8,128)(2,1)S(1)}, bf16[2,1536,128]{2,1,0:T(8,128)(2,1)S(1)}, u32[]{:S(2)}, u32[]{:S(2)}) %collective-permute-start.36) | collective-permute-done | bytes 786464 | tf_op jit(solution)/shard_map/ppermute | solution.py:309
  180.4 1.6 collective-permute-start.37
  182.0 2.2 %combine.1 = (bf16[256,512]{1,0:T(8,128)(2,1)}, bf16[256,512]{1,0:T(8,128)(2,1)}) custom-call(s32[1]{0:T(128)} %bitcast.me_ref.after_ref, bf16[528,512]{1,0:T(8,128)(2,1)S(1)} %pack.1.packed_ref, bf16[2,256,512]{2,1,0:T(8,128)(2,1)S(1)} %collective-permute-done.25.other_ref, bf16[2,2,2,48,512]{4,3,2,1,0:T(8,128)(2,1)S(1)} %get-tuple-element.79.refs_0_, ...), custom_call_target="tpu_custom_call" | custom-call | bytes 3000000 | tf_op jit(solution)/shard_map/combine/pallas_call | solution.py:34
  184.2 4.7 %collective-permute-done.37.refs_5_ = bf16[1536,128]{1,0:T(8,128)(2,1)S(1)} collective-permute-done((bf16[1536,128]{1,0:T(8,128)(2,1)S(1)}, bf16[1536,128]{1,0:T(8,128)(2,1)S(1)}, u32[]{:S(2)}, u32[]{:S(2)}) %collective-permute-start.37) | collective-permute-done | bytes 393248 | tf_op jit(solution)/shard_map/ppermute | solution.py:309
  188.9 1.3 finish.1
  (51 shorter events, 2.7 us)
Async XLA Ops:
  0.6 1.0 copy-start.4
  1.6 0.9 copy-start.5
  2.5 0.7 copy-start.6
  3.2 0.7 copy-start.7
  4.0 15.5 %collective-permute-start = (bf16[528,512]{1,0:T(8,128)(2,1)S(1)}, bf16[528,512]{1,0:T(8,128)(2,1)S(1)}, u32[]{:S(2)}, u32[]{:S(2)}) collective-permute-start(bf16[528,512]{1,0:T(8,128)(2,1)S(1)} %pack.1.packed_ref), channel_id=1, source_target_pairs={{0,16},{16,0},{32,48},{48,32},{64,80},{80,64},{96,112},{112,96},{1... | collective-permute-start | bytes 1622024 | tf_op jit(solution)/shard_map/ppermute | solution.py:321
  7.9 18.1 %collective-permute-start.1 = (bf16[2,48,512]{2,1,0:T(8,128)(2,1)S(1)}, bf16[2,48,512]{2,1,0:T(8,128)(2,1)S(1)}, u32[]{:S(2)}, u32[]{:S(2)}) collective-permute-start(bf16[2,48,512]{2,1,0:T(8,128)(2,1)S(1)} %get-tuple-element.58), channel_id=1, source_target_pairs={{0,32},{16,48},{32,64},{48,80},{64,96},{80,112},{96,0},{112,16},{1... | collective-permute-start | bytes 294920 | tf_op jit(solution)/shard_map/ppermute | solution.py:312
  9.8 17.1 %collective-permute-start.2 = (bf16[2,48,512]{2,1,0:T(8,128)(2,1)S(1)}, bf16[2,48,512]{2,1,0:T(8,128)(2,1)S(1)}, u32[]{:S(2)}, u32[]{:S(2)}) collective-permute-start(bf16[2,48,512]{2,1,0:T(8,128)(2,1)S(1)} %get-tuple-element.59), channel_id=1, source_target_pairs={{0,64},{16,80},{32,96},{48,112},{64,0},{80,16},{96,32},{112,48},{1... | collective-permute-start | bytes 294920 | tf_op jit(solution)/shard_map/ppermute | solution.py:312
  13.4 13.5 %collective-permute-start.3 = (bf16[2,48,512]{2,1,0:T(8,128)(2,1)S(1)}, bf16[2,48,512]{2,1,0:T(8,128)(2,1)S(1)}, u32[]{:S(2)}, u32[]{:S(2)}) collective-permute-start(bf16[2,48,512]{2,1,0:T(8,128)(2,1)S(1)} %get-tuple-element.60), channel_id=1, source_target_pairs={{0,96},{16,112},{32,0},{48,16},{64,32},{80,48},{96,64},{112,80},{1... | collective-permute-start | bytes 294920 | tf_op jit(solution)/shard_map/ppermute | solution.py:312
  20.1 8.0 %collective-permute-start.4 = (bf16[2,48,512]{2,1,0:T(8,128)(2,1)S(1)}, bf16[2,48,512]{2,1,0:T(8,128)(2,1)S(1)}, u32[]{:S(2)}, u32[]{:S(2)}) collective-permute-start(bf16[2,48,512]{2,1,0:T(8,128)(2,1)S(1)} %get-tuple-element.62), channel_id=1, source_target_pairs={{0,32},{16,48},{32,64},{48,80},{64,96},{80,112},{96,0},{112,16},{1... | collective-permute-start | bytes 294920 | tf_op jit(solution)/shard_map/ppermute | solution.py:312
  22.3 7.4 %collective-permute-start.5 = (bf16[2,48,512]{2,1,0:T(8,128)(2,1)S(1)}, bf16[2,48,512]{2,1,0:T(8,128)(2,1)S(1)}, u32[]{:S(2)}, u32[]{:S(2)}) collective-permute-start(bf16[2,48,512]{2,1,0:T(8,128)(2,1)S(1)} %get-tuple-element.63), channel_id=1, source_target_pairs={{0,64},{16,80},{32,96},{48,112},{64,0},{80,16},{96,32},{112,48},{1... | collective-permute-start | bytes 294920 | tf_op jit(solution)/shard_map/ppermute | solution.py:312
  25.9 4.6 %collective-permute-start.6 = (bf16[2,48,512]{2,1,0:T(8,128)(2,1)S(1)}, bf16[2,48,512]{2,1,0:T(8,128)(2,1)S(1)}, u32[]{:S(2)}, u32[]{:S(2)}) collective-permute-start(bf16[2,48,512]{2,1,0:T(8,128)(2,1)S(1)} %get-tuple-element.64), channel_id=1, source_target_pairs={{0,96},{16,112},{32,0},{48,16},{64,32},{80,48},{96,64},{112,80},{1... | collective-permute-start | bytes 294920 | tf_op jit(solution)/shard_map/ppermute | solution.py:312
  30.6 23.4 %collective-permute-start.7 = (bf16[8,2,48,512]{3,2,1,0:T(8,128)(2,1)S(1)}, bf16[8,2,48,512]{3,2,1,0:T(8,128)(2,1)}, u32[]{:S(2)}, u32[]{:S(2)}) collective-permute-start(bf16[8,2,48,512]{3,2,1,0:T(8,128)(2,1)S(1)} %join0.1.own_ref), channel_id=1, source_target_pairs={{0,1},{1,0},{2,3},{3,2},{4,5},{5,4},{6,7},{7,6},{8,9},{9,8},{10,11... | collective-permute-start | bytes 2359304 | tf_op jit(solution)/shard_map/ppermute | solution.py:309
  30.7 9.5 %collective-permute-start.9 = (bf16[2,2,48,512]{3,2,1,0:T(8,128)(2,1)S(1)}, bf16[2,2,48,512]{3,2,1,0:T(8,128)(2,1)S(1)}, u32[]{:S(2)}, u32[]{:S(2)}) collective-permute-start(bf16[2,2,48,512]{3,2,1,0:T(8,128)(2,1)S(1)} %get-tuple-element.68), channel_id=1, source_target_pairs={{0,32},{16,48},{32,64},{48,80},{64,96},{80,112},{96,0},{112,16},{1... | collective-permute-start | bytes 589832 | tf_op jit(solution)/shard_map/ppermute | solution.py:312
  31.3 13.1 %collective-permute-start.10 = (bf16[2,2,48,512]{3,2,1,0:T(8,128)(2,1)S(1)}, bf16[2,2,48,512]{3,2,1,0:T(8,128)(2,1)S(1)}, u32[]{:S(2)}, u32[]{:S(2)}) collective-permute-start(bf16[2,2,48,512]{3,2,1,0:T(8,128)(2,1)S(1)} %get-tuple-element.69), channel_id=1, source_target_pairs={{0,64},{16,80},{32,96},{48,112},{64,0},{80,16},{96,32},{112,48},{1... | collective-permute-start | bytes 589832 | tf_op jit(solution)/shard_map/ppermute | solution.py:312
  34.4 10.4 %collective-permute-start.11 = (bf16[2,2,48,512]{3,2,1,0:T(8,128)(2,1)S(1)}, bf16[2,2,48,512]{3,2,1,0:T(8,128)(2,1)S(1)}, u32[]{:S(2)}, u32[]{:S(2)}) collective-permute-start(bf16[2,2,48,512]{3,2,1,0:T(8,128)(2,1)S(1)} %get-tuple-element.70), channel_id=1, source_target_pairs={{0,96},{16,112},{32,0},{48,16},{64,32},{80,48},{96,64},{112,80},{1... | collective-permute-start | bytes 589832 | tf_op jit(solution)/shard_map/ppermute | solution.py:312
  34.9 12.7 %collective-permute-start.12 = (bf16[2,2,48,512]{3,2,1,0:T(8,128)(2,1)S(1)}, bf16[2,2,48,512]{3,2,1,0:T(8,128)(2,1)S(1)}, u32[]{:S(2)}, u32[]{:S(2)}) collective-permute-start(bf16[2,2,48,512]{3,2,1,0:T(8,128)(2,1)S(1)} %get-tuple-element.72), channel_id=1, source_target_pairs={{0,32},{16,48},{32,64},{48,80},{64,96},{80,112},{96,0},{112,16},{1... | collective-permute-start | bytes 589832 | tf_op jit(solution)/shard_map/ppermute | solution.py:312
  40.1 12.2 %collective-permute-start.13 = (bf16[2,2,48,512]{3,2,1,0:T(8,128)(2,1)S(1)}, bf16[2,2,48,512]{3,2,1,0:T(8,128)(2,1)S(1)}, u32[]{:S(2)}, u32[]{:S(2)}) collective-permute-start(bf16[2,2,48,512]{3,2,1,0:T(8,128)(2,1)S(1)} %get-tuple-element.73), channel_id=1, source_target_pairs={{0,64},{16,80},{32,96},{48,112},{64,0},{80,16},{96,32},{112,48},{1... | collective-permute-start | bytes 589832 | tf_op jit(solution)/shard_map/ppermute | solution.py:312
  44.4 8.1 %collective-permute-start.14 = (bf16[2,2,48,512]{3,2,1,0:T(8,128)(2,1)S(1)}, bf16[2,2,48,512]{3,2,1,0:T(8,128)(2,1)S(1)}, u32[]{:S(2)}, u32[]{:S(2)}) collective-permute-start(bf16[2,2,48,512]{3,2,1,0:T(8,128)(2,1)S(1)} %get-tuple-element.74), channel_id=1, source_target_pairs={{0,96},{16,112},{32,0},{48,16},{64,32},{80,48},{96,64},{112,80},{1... | collective-permute-start | bytes 589832 | tf_op jit(solution)/shard_map/ppermute | solution.py:312
  53.5 16.5 %collective-permute-start.15 = (bf16[8,2,48,512]{3,2,1,0:T(8,128)(2,1)}, bf16[8,2,48,512]{3,2,1,0:T(8,128)(2,1)}, u32[]{:S(2)}, u32[]{:S(2)}) collective-permute-start(bf16[8,2,48,512]{3,2,1,0:T(8,128)(2,1)} %get-tuple-element.75.own_ref), channel_id=1, source_target_pairs={{0,1},{1,0},{2,3},{3,2},{4,5},{5,4},{6,7},{7,6},{8,9},{9,8},{10,11... | collective-permute-start | bytes 2359304 | tf_op jit(solution)/shard_map/ppermute | solution.py:309
  53.5 31.9 %collective-permute-start.20 = (bf16[8,2,48,512]{3,2,1,0:T(8,128)(2,1)S(1)}, bf16[8,2,48,512]{3,2,1,0:T(8,128)(2,1)}, u32[]{:S(2)}, u32[]{:S(2)}) collective-permute-start(bf16[8,2,48,512]{3,2,1,0:T(8,128)(2,1)S(1)} %get-tuple-element.83.own_ref), channel_id=1, source_target_pairs={{0,1},{1,0},{2,3},{3,2},{4,5},{5,4},{6,7},{7,6},{8,9},{9,8},{10,11... | collective-permute-start | bytes 2359304 | tf_op jit(solution)/shard_map/ppermute | solution.py:309
  68.2 34.5 %collective-permute-start.26 = (bf16[2,1536,128]{2,1,0:T(8,128)(2,1)S(1)}, bf16[2,1536,128]{2,1,0:T(8,128)(2,1)}, u32[]{:S(2)}, u32[]{:S(2)}) collective-permute-start(bf16[2,1536,128]{2,1,0:T(8,128)(2,1)S(1)} %get-tuple-element.95), channel_id=1, source_target_pairs={{0,4},{1,13},{2,6},{3,15},{4,8},{5,1},{6,10},{7,3},{8,12},{9,5},{1... | collective-permute-start | bytes 2359304 | tf_op jit(solution)/shard_map/ppermute | solution.py:309
  85.5 14.9 %copy-start.2 = (bf16[1536,128]{1,0:T(8,128)(2,1)}, bf16[1536,128]{1,0:T(8,128)(2,1)S(1)}, u32[]{:S(2)}) copy-start(bf16[1536,128]{1,0:T(8,128)(2,1)S(1)} %get-tuple-element.100) | copy-start | bytes 1179652
  100.4 5.5 %copy-start = (bf16[1536,128]{1,0:T(8,128)(2,1)}, bf16[1536,128]{1,0:T(8,128)(2,1)S(1)}, u32[]{:S(2)}) copy-start(bf16[1536,128]{1,0:T(8,128)(2,1)S(1)} %get-tuple-element.105) | copy-start | bytes 1179652
  100.4 4.9 %collective-permute-start.21 = (bf16[2,384,512]{2,1,0:T(8,128)(2,1)S(1)}, bf16[2,384,512]{2,1,0:T(8,128)(2,1)S(1)}, u32[]{:S(2)}, u32[]{:S(2)}) collective-permute-start(bf16[2,384,512]{2,1,0:T(8,128)(2,1)S(1)} %get-tuple-element.86), channel_id=1, source_target_pairs={{0,1},{1,0},{2,3},{3,2},{4,5},{5,4},{6,7},{7,6},{8,9},{9,8},{10,11... | collective-permute-start | bytes 2359304 | tf_op jit(solution)/shard_map/ppermute | solution.py:309
  101.6 4.3 %collective-permute-start.8 = (bf16[2,384,512]{2,1,0:T(8,128)(2,1)S(1)}, bf16[2,384,512]{2,1,0:T(8,128)(2,1)S(1)}, u32[]{:S(2)}, u32[]{:S(2)}) collective-permute-start(bf16[2,384,512]{2,1,0:T(8,128)(2,1)S(1)} %get-tuple-element.66), channel_id=1, source_target_pairs={{0,1},{1,0},{2,3},{3,2},{4,5},{5,4},{6,7},{7,6},{8,9},{9,8},{10,11... | collective-permute-start | bytes 2359304 | tf_op jit(solution)/shard_map/ppermute | solution.py:309
  101.7 6.9 %collective-permute-start.16 = (bf16[2,384,512]{2,1,0:T(8,128)(2,1)}, bf16[2,384,512]{2,1,0:T(8,128)(2,1)S(1)}, u32[]{:S(2)}, u32[]{:S(2)}) collective-permute-start(bf16[2,384,512]{2,1,0:T(8,128)(2,1)} %get-tuple-element.78), channel_id=1, source_target_pairs={{0,1},{1,0},{2,3},{3,2},{4,5},{5,4},{6,7},{7,6},{8,9},{9,8},{10,11... | collective-permute-start | bytes 2359304 | tf_op jit(solution)/shard_map/ppermute | solution.py:309
  102.1 13.5 %collective-permute-start.30 = (bf16[2,1536,128]{2,1,0:T(8,128)(2,1)}, bf16[2,1536,128]{2,1,0:T(8,128)(2,1)}, u32[]{:S(2)}, u32[]{:S(2)}) collective-permute-start(bf16[2,1536,128]{2,1,0:T(8,128)(2,1)} %get-tuple-element.99), channel_id=1, source_target_pairs={{0,4},{1,13},{2,6},{3,15},{4,8},{5,1},{6,10},{7,3},{8,12},{9,5},{1... | collective-permute-start | bytes 2359304 | tf_op jit(solution)/shard_map/ppermute | solution.py:309
  102.7 21.4 %collective-permute-start.34 = (bf16[2,1536,128]{2,1,0:T(8,128)(2,1)}, bf16[2,1536,128]{2,1,0:T(8,128)(2,1)}, u32[]{:S(2)}, u32[]{:S(2)}) collective-permute-start(bf16[2,1536,128]{2,1,0:T(8,128)(2,1)} %get-tuple-element.104), channel_id=1, source_target_pairs={{0,4},{1,13},{2,6},{3,15},{4,8},{5,1},{6,10},{7,3},{8,12},{9,5},{1... | collective-permute-start | bytes 2359304 | tf_op jit(solution)/shard_map/ppermute | solution.py:309
  105.3 44.5 %collective-permute-start.27 = (bf16[2,1536,128]{2,1,0:T(8,128)(2,1)S(1)}, bf16[2,1536,128]{2,1,0:T(8,128)(2,1)S(1)}, u32[]{:S(2)}, u32[]{:S(2)}) collective-permute-start(bf16[2,1536,128]{2,1,0:T(8,128)(2,1)S(1)} %add_convert_fusion.5), channel_id=1, source_target_pairs={{0,4},{1,13},{2,6},{3,15},{4,8},{5,1},{6,10},{7,3},{8,12},{9,5},{1... | collective-permute-start | bytes 2359304 | tf_op jit(solution)/shard_map/ppermute | solution.py:309
  105.9 20.8 %collective-permute-start.22 = (bf16[1,2,2,48,512]{4,3,2,1,0:T(8,128)(2,1)S(1)}, bf16[1,2,2,48,512]{4,3,2,1,0:T(8,128)(2,1)S(1)}, u32[]{:S(2)}, u32[]{:S(2)}) collective-permute-start(bf16[1,2,2,48,512]{4,3,2,1,0:T(8,128)(2,1)S(1)} %get-tuple-element.88), channel_id=1, source_target_pairs={{0,96},{16,112},{32,0},{48,16},{64,32},{80,48},{96,64},{112,80},{1... | collective-permute-start | bytes 589832 | tf_op jit(solution)/shard_map/ppermute | solution.py:312
  108.6 18.4 %collective-permute-start.23 = (bf16[1,2,2,48,512]{4,3,2,1,0:T(8,128)(2,1)S(1)}, bf16[1,2,2,48,512]{4,3,2,1,0:T(8,128)(2,1)S(1)}, u32[]{:S(2)}, u32[]{:S(2)}) collective-permute-start(bf16[1,2,2,48,512]{4,3,2,1,0:T(8,128)(2,1)S(1)} %get-tuple-element.89), channel_id=1, source_target_pairs={{0,64},{16,80},{32,96},{48,112},{64,0},{80,16},{96,32},{112,48},{1... | collective-permute-start | bytes 589832 | tf_op jit(solution)/shard_map/ppermute | solution.py:312
  115.7 11.9 %collective-permute-start.24 = (bf16[1,2,2,48,512]{4,3,2,1,0:T(8,128)(2,1)S(1)}, bf16[1,2,2,48,512]{4,3,2,1,0:T(8,128)(2,1)S(1)}, u32[]{:S(2)}, u32[]{:S(2)}) collective-permute-start(bf16[1,2,2,48,512]{4,3,2,1,0:T(8,128)(2,1)S(1)} %get-tuple-element.90), channel_id=1, source_target_pairs={{0,32},{16,48},{32,64},{48,80},{64,96},{80,112},{96,0},{112,16},{1... | collective-permute-start | bytes 589832 | tf_op jit(solution)/shard_map/ppermute | solution.py:312
  124.1 17.7 %collective-permute-start.17 = (bf16[2,2,2,48,512]{4,3,2,1,0:T(8,128)(2,1)S(1)}, bf16[2,2,2,48,512]{4,3,2,1,0:T(8,128)(2,1)S(1)}, u32[]{:S(2)}, u32[]{:S(2)}) collective-permute-start(bf16[2,2,2,48,512]{4,3,2,1,0:T(8,128)(2,1)S(1)} %get-tuple-element.80), channel_id=1, source_target_pairs={{0,96},{16,112},{32,0},{48,16},{64,32},{80,48},{96,64},{112,80},{1... | collective-permute-start | bytes 1179656 | tf_op jit(solution)/shard_map/ppermute | solution.py:312
  126.7 15.9 %collective-permute-start.18 = (bf16[2,2,2,48,512]{4,3,2,1,0:T(8,128)(2,1)S(1)}, bf16[2,2,2,48,512]{4,3,2,1,0:T(8,128)(2,1)S(1)}, u32[]{:S(2)}, u32[]{:S(2)}) collective-permute-start(bf16[2,2,2,48,512]{4,3,2,1,0:T(8,128)(2,1)S(1)} %get-tuple-element.81), channel_id=1, source_target_pairs={{0,64},{16,80},{32,96},{48,112},{64,0},{80,16},{96,32},{112,48},{1... | collective-permute-start | bytes 1179656 | tf_op jit(solution)/shard_map/ppermute | solution.py:312
  127.0 18.2 %collective-permute-start.19 = (bf16[2,2,2,48,512]{4,3,2,1,0:T(8,128)(2,1)S(1)}, bf16[2,2,2,48,512]{4,3,2,1,0:T(8,128)(2,1)S(1)}, u32[]{:S(2)}, u32[]{:S(2)}) collective-permute-start(bf16[2,2,2,48,512]{4,3,2,1,0:T(8,128)(2,1)S(1)} %get-tuple-element.82), channel_id=1, source_target_pairs={{0,32},{16,48},{32,64},{48,80},{64,96},{80,112},{96,0},{112,16},{1... | collective-permute-start | bytes 1179656 | tf_op jit(solution)/shard_map/ppermute | solution.py:312
  127.6 23.3 %collective-permute-start.31 = (bf16[2,1536,128]{2,1,0:T(8,128)(2,1)}, bf16[2,1536,128]{2,1,0:T(8,128)(2,1)S(1)}, u32[]{:S(2)}, u32[]{:S(2)}) collective-permute-start(bf16[2,1536,128]{2,1,0:T(8,128)(2,1)} %add_convert_fusion.3), channel_id=1, source_target_pairs={{0,4},{1,13},{2,6},{3,15},{4,8},{5,1},{6,10},{7,3},{8,12},{9,5},{1... | collective-permute-start | bytes 2359304 | tf_op jit(solution)/shard_map/ppermute | solution.py:309
  141.8 13.2 %collective-permute-start.35 = (bf16[2,1536,128]{2,1,0:T(8,128)(2,1)S(1)}, bf16[2,1536,128]{2,1,0:T(8,128)(2,1)S(1)}, u32[]{:S(2)}, u32[]{:S(2)}) collective-permute-start(bf16[2,1536,128]{2,1,0:T(8,128)(2,1)S(1)} %add_convert_fusion.1), channel_id=1, source_target_pairs={{0,4},{1,13},{2,6},{3,15},{4,8},{5,1},{6,10},{7,3},{8,12},{9,5},{1... | collective-permute-start | bytes 2359304 | tf_op jit(solution)/shard_map/ppermute | solution.py:309
  146.7 35.4 %collective-permute-start.25 = (bf16[2,256,512]{2,1,0:T(8,128)(2,1)S(1)}, bf16[2,256,512]{2,1,0:T(8,128)(2,1)S(1)}, u32[]{:S(2)}, u32[]{:S(2)}) collective-permute-start(bf16[2,256,512]{2,1,0:T(8,128)(2,1)S(1)} %partner_sums.1), channel_id=1, source_target_pairs={{0,16},{16,0},{32,48},{48,32},{64,80},{80,64},{96,112},{112,96},{1... | collective-permute-start | bytes 1572872 | tf_op jit(solution)/shard_map/ppermute | solution.py:358
  150.0 13.4 %collective-permute-start.28 = (bf16[2,1536,128]{2,1,0:T(8,128)(2,1)S(1)}, bf16[2,1536,128]{2,1,0:T(8,128)(2,1)S(1)}, u32[]{:S(2)}, u32[]{:S(2)}) collective-permute-start(bf16[2,1536,128]{2,1,0:T(8,128)(2,1)S(1)} %add_convert_fusion.4), channel_id=1, source_target_pairs={{0,4},{1,13},{2,6},{3,15},{4,8},{5,1},{6,10},{7,3},{8,12},{9,5},{1... | collective-permute-start | bytes 2359304 | tf_op jit(solution)/shard_map/ppermute | solution.py:309
  151.1 20.7 %collective-permute-start.32 = (bf16[2,1536,128]{2,1,0:T(8,128)(2,1)S(1)}, bf16[2,1536,128]{2,1,0:T(8,128)(2,1)S(1)}, u32[]{:S(2)}, u32[]{:S(2)}) collective-permute-start(bf16[2,1536,128]{2,1,0:T(8,128)(2,1)S(1)} %add_convert_fusion.2), channel_id=1, source_target_pairs={{0,4},{1,13},{2,6},{3,15},{4,8},{5,1},{6,10},{7,3},{8,12},{9,5},{1... | collective-permute-start | bytes 2359304 | tf_op jit(solution)/shard_map/ppermute | solution.py:309
  155.2 16.6 %copy-start.3 = (bf16[1536,128]{1,0:T(8,128)(2,1)S(1)}, bf16[1536,128]{1,0:T(8,128)(2,1)}, u32[]{:S(2)}) copy-start(bf16[1536,128]{1,0:T(8,128)(2,1)} %copy-done.2) | copy-start | bytes 1179652
  155.2 25.1 %collective-permute-start.36 = (bf16[2,1536,128]{2,1,0:T(8,128)(2,1)S(1)}, bf16[2,1536,128]{2,1,0:T(8,128)(2,1)S(1)}, u32[]{:S(2)}, u32[]{:S(2)}) collective-permute-start(bf16[2,1536,128]{2,1,0:T(8,128)(2,1)S(1)} %add_convert_fusion), channel_id=1, source_target_pairs={{0,4},{1,13},{2,6},{3,15},{4,8},{5,1},{6,10},{7,3},{8,12},{9,5},{1... | collective-permute-start | bytes 2359304 | tf_op jit(solution)/shard_map/ppermute | solution.py:309
  163.6 16.6 %copy-start.1 = (bf16[1536,128]{1,0:T(8,128)(2,1)S(1)}, bf16[1536,128]{1,0:T(8,128)(2,1)}, u32[]{:S(2)}) copy-start(bf16[1536,128]{1,0:T(8,128)(2,1)} %copy-done) | copy-start | bytes 1179652
  163.6 20.6 %collective-permute-start.29 = (bf16[1536,128]{1,0:T(8,128)(2,1)S(1)}, bf16[1536,128]{1,0:T(8,128)(2,1)S(1)}, u32[]{:S(2)}, u32[]{:S(2)}) collective-permute-start(bf16[1536,128]{1,0:T(8,128)(2,1)S(1)} %get-tuple-element.113), channel_id=1, source_target_pairs={{0,2},{1,3},{2,0},{3,1},{4,6},{5,7},{6,4},{7,5},{8,10},{9,11},{10,... | collective-permute-start | bytes 1179656 | tf_op jit(solution)/shard_map/ppermute | solution.py:309
  172.0 12.2 %collective-permute-start.33 = (bf16[1536,128]{1,0:T(8,128)(2,1)S(1)}, bf16[1536,128]{1,0:T(8,128)(2,1)S(1)}, u32[]{:S(2)}, u32[]{:S(2)}) collective-permute-start(bf16[1536,128]{1,0:T(8,128)(2,1)S(1)} %get-tuple-element.111), channel_id=1, source_target_pairs={{0,2},{1,3},{2,0},{3,1},{4,6},{5,7},{6,4},{7,5},{8,10},{9,11},{10,... | collective-permute-start | bytes 1179656 | tf_op jit(solution)/shard_map/ppermute | solution.py:309
  180.4 8.4 %collective-permute-start.37 = (bf16[1536,128]{1,0:T(8,128)(2,1)S(1)}, bf16[1536,128]{1,0:T(8,128)(2,1)S(1)}, u32[]{:S(2)}, u32[]{:S(2)}) collective-permute-start(bf16[1536,128]{1,0:T(8,128)(2,1)S(1)} %get-tuple-element.109), channel_id=1, source_target_pairs={{0,2},{1,3},{2,0},{3,1},{4,6},{5,7},{6,4},{7,5},{8,10},{9,11},{10,... | collective-permute-start | bytes 1179656 | tf_op jit(solution)/shard_map/ppermute | solution.py:309
where the time goes:
time: 191 us; the launch traced here: 190 us
  waiting for transfers between devices  80.3 us (42%)
  Pallas kernels  52.5 us (27%)
  starting transfers between devices  47.1 us (25%)
  other arithmetic  6.15 us (3%)
  local copies, waits for them, and re-layouts  3.27 us (2%)
    pallas_call x3, Pallas kernels, expert(): pl.pallas_call(expert_kernel, grid_spec=pltpu.PrefetchScalarGridSpec(num_...  44.5 us
    ppermute x18, waiting for transfers between devices, over_replica(): return lax.ppermute(value, 'replica', perm)  40.3 us
    ppermute x18, waiting for transfers between devices, to_z(): return lax.ppermute(value, 'expert', along_z(dz))  35 us
    ppermute x18, starting transfers between devices, to_z(): return lax.ppermute(value, 'expert', along_z(dz))  26.6 us
    ppermute x18, starting transfers between devices, over_replica(): return lax.ppermute(value, 'replica', perm)  14.3 us
    pallas_call x10, Pallas kernels, call(): pl.pallas_call(kernel, in_specs=in_specs, out_specs=jax.tree.map(lambda _...  7.96 us
    convert_element_type x9, other arithmetic, add(): functools.reduce(lambda a, b: a + b, [t.astype(F32) for t in terms])  6.14 us
    ppermute x1, waiting for transfers between devices, local(): partner = lax.ppermute(packed, 'expert', PARTNER)  4.98 us
  transfers between devices with their start and end apart: 38, of which 19 were waited for; matrix products, arithmetic and copies ran while one was open for 3% of the time, Pallas kernels for 27%

commit v1 on v0

--- a/solution.py
+++ b/solution.py
@@ -17,7 +17,7 @@
 META = 16
 F32 = jnp.float32
 BF16 = jnp.bfloat16
-VMEM_LIMIT = 48 * 1024 * 1024
+VMEM_LIMIT = 34 * 1024 * 1024
 VMEM = pl.BlockSpec(memory_space=pltpu.VMEM)
 SMEM = pl.BlockSpec(memory_space=pltpu.SMEM)
 
@@ -53,17 +53,32 @@
 RING = [(r, (r + (4 if r % 2 == 0 else 12)) % 16) for r in range(16)]
 
 
-def pack_kernel(tokens_ref, cot_ref, ids_ref, gates_ref, out_ref):
-    out_ref[0:TOK] = tokens_ref[...]
-    out_ref[TOK : 2 * TOK] = cot_ref[...]
-    gates = gates_ref[...]
+def pack_kernel(tokens_ref, cot_ref, ids_ref, gates_ref, out_ref, ids_s, gates_s, sems):
+    copies = [
+        pltpu.make_async_copy(src, dst, sems.at[n])
+        for n, (src, dst) in enumerate(
+            (
+                (ids_ref, ids_s),
+                (gates_ref, gates_s),
+                (tokens_ref, out_ref.at[pl.ds(0, TOK)]),
+                (cot_ref, out_ref.at[pl.ds(TOK, TOK)]),
+            )
+        )
+    ]
+    for copy in copies:
+        copy.start()
+    copies[0].wait()
+    copies[1].wait()
+    gates = gates_s[...]
     high = gates.astype(BF16).astype(F32)
     middle = (gates - high).astype(BF16).astype(F32)
     low = gates - high - middle
     meta = jnp.concatenate(
-        [ids_ref[...].astype(F32), high, middle, low, jnp.zeros((META - 8, TOK), F32)], axis=0
+        [ids_s[...].astype(F32), high, middle, low, jnp.zeros((META - 8, TOK), F32)], axis=0
     )
     out_ref[2 * TOK :] = jnp.concatenate([meta, jnp.zeros_like(meta)], axis=1).astype(BF16)
+    copies[2].wait()
+    copies[3].wait()
 
 
 def read_meta(packed_ref):
@@ -72,7 +87,7 @@
     return meta[0:2], gates
 
 
-def dispatch_kernel(me_ref, packed_ref, *out_refs):
+def dispatch_kernel(split, me_ref, packed_ref, *out_refs):
     z, h = me_ref[0] >> 1, me_ref[0] & 1
     ids, gates = read_meta(packed_ref)
     count = 4 * LOCAL
@@ -101,50 +116,37 @@
         grads = (weight * dot(pick, packed_ref[TOK : 2 * TOK])).astype(BF16)
         for dz in range(4):
             part = slice(dz * CAP, (dz + 1) * CAP)
-            if j == 0:
-                out_refs[dz][0] = rows[part]
-                out_refs[dz][1] = grads[part]
-            else:
-                out_refs[4 + dz][j - 1, 0] = rows[part]
-                out_refs[4 + dz][j - 1, 1] = grads[part]
-
-
-def dispatch(name, me, packed):
-    out = [bf16_like(2, CAP, D)] * 4 + [bf16_like(2, 2, CAP, D)] * 4
-    return call(dispatch_kernel, name, [SMEM, VMEM], out, (me, packed), 3 * 10**6)
-
-
-def join_first_kernel(*refs):
-    for n, ref in enumerate(refs[:-1]):
-        refs[-1][n] = ref[...]
-
-
-def join_rest_kernel(*refs):
-    for n, ref in enumerate(refs[:-2]):
-        refs[-2][n] = ref[0]
-        refs[-1][n] = ref[1]
-
-
-def expert_kernel(
-    tbl_ref, own_ref, oth_ref, after_ref, wg0, wg1, wu0, wu1, wd0, wd1,
-    far, mid, near, home0, home1, ret_own, ret_oth,
-    x_s, g_s, xt_s, gt_s, eo_s, ig_s,
-):
-    i = pl.program_id(0)
-
-    @pl.when(i == 0)
-    def _():
-        for k, ref in enumerate((own_ref, oth_ref)):
-            x_s[k * ROWS : (k + 1) * ROWS, :] = ref[:, 0].reshape(ROWS, D)
-            g_s[k * ROWS : (k + 1) * ROWS, :] = ref[:, 1].reshape(ROWS, D)
-        xt_s[...] = x_s[...].T
-        gt_s[...] = g_s[...].T
-        eo_s[...] = jnp.zeros_like(eo_s)
-        ig_s[...] = jnp.zeros_like(ig_s)
-
-    wg = jnp.concatenate([wg0[...], wg1[...]], axis=1)
-    wu = jnp.concatenate([wu0[...], wu1[...]], axis=1)
-    wd = jnp.concatenate([wd0[...], wd1[...]], axis=0)
+            ref, at = out_refs[dz], j
+            if split:
+                ref, at = (out_refs[dz], 0) if j == 0 else (out_refs[4 + dz], j - 1)
+            ref[at, 0] = rows[part]
+            ref[at, 1] = grads[part]
+
+
+def dispatch(name, split, me, packed):
+    out = [bf16_like(n, 2, CAP, D) for n in ((1, 2) if split else (3,)) for _ in range(4)]
+    kernel = functools.partial(dispatch_kernel, split)
+    return call(kernel, name, [SMEM, VMEM], out, (me, packed), 3 * 10**6)
+
+
+def join_kernel(count, *refs):
+    ins, out_ref = refs[:SOURCES], refs[-1]
+    for n, ref in enumerate(ins):
+        skip = ref.shape[0] - count
+        for j in range(count):
+            out_ref[j, n] = ref[skip + j if count > 1 else 0]
+
+
+def join(name, count, pieces, after):
+    specs = [VMEM] * SOURCES + [pl.BlockSpec(memory_space=pl.ANY)] * len(after)
+    out = bf16_like(count, SOURCES, 2, CAP, D)
+    return call(functools.partial(join_kernel, count), name, specs, out, (*pieces, *after), 10**6)
+
+
+def share(x_s, g_s, xt_s, gt_s, eo_s, ig_s, weights, homes):
+    wg = jnp.concatenate([weights[0][...], weights[1][...]], axis=1)
+    wu = jnp.concatenate([weights[2][...], weights[3][...]], axis=1)
+    wd = jnp.concatenate([weights[4][...], weights[5][...]], axis=0)
     x = x_s[...]
     g = g_s[...]
     pre_gate = dot(x, wg)
@@ -155,70 +157,106 @@
     hidden = (silu * pre_up).astype(BF16)
     grad_gate = (grad_hidden * pre_up * sig * (1.0 + pre_gate * (1.0 - sig))).astype(BF16)
     grad_up = (grad_hidden * silu).astype(BF16)
-    part_gate = dot(xt_s[...], grad_gate).astype(BF16)
-    part_up = dot(xt_s[...], grad_up).astype(BF16)
-    part_down = dot(gt_s[...], hidden).astype(BF16)
-
-    def keep(ref, lane):
-        for k, part in enumerate((part_gate, part_up, part_down)):
-            ref[k * D : (k + 1) * D, :] = part[:, lane * BLK : (lane + 1) * BLK]
-
-    homes = (far.at[0], far.at[1]), (mid.at[0], mid.at[1]), (near.at[0], near.at[1]), (home0, home1)
-    for step, (a, b) in enumerate(homes):
+    parts = [
+        dot(xt_s[...], grad_gate).astype(BF16),
+        dot(xt_s[...], grad_up).astype(BF16),
+        dot(gt_s[...], hidden).astype(BF16),
+    ]
+    i = pl.program_id(0)
+    for step, pair in enumerate(homes):
 
         @pl.when(i == step)
-        def _(a=a, b=b):
-            keep(a, 0)
-            keep(b, 1)
+        def _(pair=pair):
+            for lane, ref in enumerate(pair):
+                for k, part in enumerate(parts):
+                    ref[k * D : (k + 1) * D, :] = part[:, lane * BLK : (lane + 1) * BLK]
 
     eo_s[...] += dot(hidden, wd)
     ig_s[...] += dot(grad_gate, wg, 1, 1) + dot(grad_up, wu, 1, 1)
 
-    @pl.when(i == 3)
+
+def load_rows(own_ref, oth_ref, x_s, g_s, xt_s, gt_s):
+    for k, ref in enumerate((own_ref, oth_ref)):
+        x_s[k * ROWS : (k + 1) * ROWS, :] = ref[:, 0].reshape(ROWS, D)
+        g_s[k * ROWS : (k + 1) * ROWS, :] = ref[:, 1].reshape(ROWS, D)
+    xt_s[...] = x_s[...].T
+    gt_s[...] = g_s[...].T
+
+
+def first_kernel(n_after, tbl_ref, own_ref, oth_ref, *refs):
+    weights, (far, eo_ref, ig_ref, x_s, g_s, xt_s, gt_s) = refs[:6], refs[6 + n_after :]
+    load_rows(own_ref, oth_ref, x_s, g_s, xt_s, gt_s)
+    eo_ref[...] = jnp.zeros_like(eo_ref)
+    ig_ref[...] = jnp.zeros_like(ig_ref)
+    share(x_s, g_s, xt_s, gt_s, eo_ref, ig_ref, weights, [(far.at[0], far.at[1])])
+
+
+def rest_kernel(n_after, tbl_ref, own_ref, oth_ref, *refs):
+    weights, eo_ref, ig_ref = refs[:6], refs[6], refs[7]
+    mid, near, home0, home1, ret_own, ret_oth, x_s, g_s, xt_s, gt_s, eo_s, ig_s = refs[8 + n_after :]
+    i = pl.program_id(0)
+
+    @pl.when(i == 0)
+    def _():
+        load_rows(own_ref, oth_ref, x_s, g_s, xt_s, gt_s)
+        eo_s[...] = eo_ref[...]
+        ig_s[...] = ig_ref[...]
+
+    homes = [(mid.at[0], mid.at[1]), (near.at[0], near.at[1]), (home0, home1)]
+    share(x_s, g_s, xt_s, gt_s, eo_s, ig_s, weights, homes)
+
+    @pl.when(i == 2)
     def _():
         for k, ref in enumerate((ret_own, ret_oth)):
             ref[0] = eo_s[k * ROWS : (k + 1) * ROWS, :].astype(BF16)
             ref[1] = ig_s[k * ROWS : (k + 1) * ROWS, :].astype(BF16)
 
 
-def expert(j, tbl, own, oth, after, w_gate, w_up, w_down):
+def expert(j, at, tbl, own, oth, weights, sums=None, after=()):
     rows = 2 * ROWS
+    steps = (0,) if sums is None else (1, 2, 3)
 
     def fixed(shape):
         return pl.BlockSpec(shape, lambda i, tbl: (0,) * len(shape))
 
     def columns(k):
-        return pl.BlockSpec((None, D, BLK), lambda i, tbl: (j, 0, tbl[2 * i + k]))
+        return pl.BlockSpec((None, D, BLK), lambda i, tbl: (j, 0, tbl[2 * (i + steps[0]) + k]))
 
     def lines(k):
-        return pl.BlockSpec((None, BLK, D), lambda i, tbl: (j, tbl[2 * i + k], 0))
-
-    chunk, ret = (3 * D, BLK), (2, ROWS, D)
-    out_shapes = [(2,) + chunk] * 3 + [chunk] * 2 + [ret] * 2
+        return pl.BlockSpec((None, BLK, D), lambda i, tbl: (j, tbl[2 * (i + steps[0]) + k], 0))
+
+    joined = pl.BlockSpec((None, SOURCES, 2, CAP, D), lambda i, tbl: (at, 0, 0, 0, 0))
+    chunk, ret, sum_like = (3 * D, BLK), (2, ROWS, D), jax.ShapeDtypeStruct((rows, D), F32)
+    scratch = [pltpu.VMEM((rows, D), BF16)] * 2 + [pltpu.VMEM((D, rows), BF16)] * 2
+    if sums is None:
+        kernel, name, sums = first_kernel, f"expert{j}_first", ()
+        out = [bf16_like(2, *chunk), sum_like, sum_like]
+    else:
+        kernel, name = rest_kernel, f"expert{j}_rest"
+        out = [bf16_like(*s) for s in ((2,) + chunk, (2,) + chunk, chunk, chunk, ret, ret)]
+        scratch = scratch + [pltpu.VMEM((rows, D), F32)] * 2
+    w_gate, w_up, w_down = weights
     return pl.pallas_call(
-        expert_kernel,
+        functools.partial(kernel, len(after)),
         grid_spec=pltpu.PrefetchScalarGridSpec(
             num_scalar_prefetch=1,
-            grid=(4,),
-            in_specs=[fixed(own.shape), fixed(oth.shape), pl.BlockSpec(memory_space=pl.ANY)]
-            + [columns(0), columns(1), columns(0), columns(1), lines(0), lines(1)],
-            out_specs=[fixed(s) for s in out_shapes],
-            scratch_shapes=[
-                pltpu.VMEM((rows, D), BF16),
-                pltpu.VMEM((rows, D), BF16),
-                pltpu.VMEM((D, rows), BF16),
-                pltpu.VMEM((D, rows), BF16),
-                pltpu.VMEM((rows, D), F32),
-                pltpu.VMEM((rows, D), F32),
-            ],
+            grid=(len(steps),),
+            in_specs=[joined, joined]
+            + [columns(0), columns(1), columns(0), columns(1), lines(0), lines(1)]
+            + [fixed((rows, D))] * len(sums)
+            + [pl.BlockSpec(memory_space=pl.ANY)] * len(after),
+            out_specs=[fixed(s.shape) for s in out],
+            scratch_shapes=scratch,
         ),
-        out_shape=[bf16_like(*s) for s in out_shapes],
+        out_shape=out,
         compiler_params=pltpu.CompilerParams(
             dimension_semantics=("arbitrary",), vmem_limit_bytes=VMEM_LIMIT
         ),
-        cost_estimate=pl.CostEstimate(flops=0, bytes_accessed=2 * 10**6, transcendentals=0),
-        name=f"expert{j}",
-    )(tbl, own, oth, after, w_gate, w_gate, w_up, w_up, w_down, w_down)
+        cost_estimate=pl.CostEstimate(
+            flops=len(steps) * 18 * rows * D * 256, bytes_accessed=10**6, transcendentals=0
+        ),
+        name=name,
+    )(tbl, own, oth, w_gate, w_gate, w_up, w_up, w_down, w_down, *sums, *after)
 
 
 def back_kernel(count, *refs):
@@ -314,34 +352,51 @@
     packed = call(
         pack_kernel,
         "pack",
-        [VMEM] * 4,
+        [pl.BlockSpec(memory_space=pltpu.HBM)] * 4,
         bf16_like(2 * TOK + META, D),
         (tokens, cotangent, expert_ids.T, gates.T),
+        scratch=[
+            pltpu.VMEM((2, TOK), jnp.int32),
+            pltpu.VMEM((2, TOK), F32),
+            pltpu.SemaphoreType.DMA((4,)),
+        ],
     )
     partner = lax.ppermute(packed, "expert", PARTNER)
-    firsts, rests = [], []
-    for name, source in (("own_slots", packed), ("partner_slots", partner)):
-        sent = dispatch(name, me, source)
-        firsts += [sent[0]] + [to_z(sent[dz], dz) for dz in range(1, 4)]
-        rests += [sent[4]] + [to_z(sent[4 + dz], dz) for dz in range(1, 4)]
-    joined = bf16_like(SOURCES, 2, CAP, D)
-    received = [call(join_first_kernel, "join0", [VMEM] * 8, joined, firsts)]
-    received += call(join_rest_kernel, "join12", [VMEM] * 8, [joined] * 2, rests)
+    sent = dispatch("own_slots", False, me, packed)
+    from_own = [sent[0]] + [to_z(sent[dz], dz) for dz in range(1, 4)]
+    sent = dispatch("partner_slots", True, me, partner)
+    firsts = [sent[0]] + [to_z(sent[dz], dz) for dz in range(1, 4)]
+    rests = [sent[4]] + [to_z(sent[4 + dz], dz) for dz in range(1, 4)]
+
+    weights = (w_gate, w_up, w_down)
+    own0 = join("join0", 1, from_own + firsts, ())
+    oth0 = over_replica(own0, CORE)
+    far0, eo, ig = expert(0, 0, tbl, own0, oth0, weights)
+    own12 = join("join12", 2, from_own + rests, (far0,))
+    oth12 = over_replica(own12, CORE)
+    second0 = over_replica(far0, RING)
+    mid0, near0, *kept0 = expert(0, 0, tbl, own0, oth0, weights, (eo, ig), (own12,))
+    second0 = add(mid0, second0)
+    third0 = over_replica(second0, RING)
+    far1, eo, ig = expert(1, 0, tbl, own12, oth12, weights, None, (second0,))
+    second1 = over_replica(far1, RING)
+    mid1, near1, *kept1 = expert(1, 0, tbl, own12, oth12, weights, (eo, ig))
+    third0 = add(near0, third0)
+    home0 = over_replica(third0, RING)
+    second1 = add(mid1, second1)
+    third1 = over_replica(second1, RING)
+    far2, eo, ig = expert(2, 1, tbl, own12, oth12, weights, None, (third0, second1))
+    second2 = over_replica(far2, RING)
+    mid2, near2, *kept2 = expert(2, 1, tbl, own12, oth12, weights, (eo, ig))
+    second2 = add(mid2, second2)
+    third2 = over_replica(second2, RING)
+    home1 = over_replica(add(near1, third1), RING)
+    home2 = over_replica(add(near2, third2), RING)
 
     parts, pairs = [], []
-    after = me
-    for j in range(LOCAL):
-        own = received[j]
-        oth = over_replica(own, CORE)
-        far, mid, near, home0, home1, ret_own, ret_oth = expert(
-            j, tbl, own, oth, after, w_gate, w_up, w_down
-        )
-        after = home0
-        total = over_replica(far, RING)
-        total = over_replica(add(mid, total), RING)
-        total = over_replica(add(near, total), RING)
-        across = over_replica(add(home1, total[1]), ACROSS)
-        parts += [add(home0, total[0]), across]
+    for home, (mine, theirs, ret_own, ret_oth) in ((home0, kept0), (home1, kept1), (home2, kept2)):
+        across = over_replica(add(theirs, home[1]), ACROSS)
+        parts += [add(mine, home[0]), across]
         pairs += [ret_own, over_replica(ret_oth, CORE)]
 
     rows = []

time: 191 us -> 171 us (0.90)
  waiting for transfers between devices: 80.3 us -> 58.1 us
  local copies, waits for them, and re-layouts: 3.27 us -> 9.53 us
  other arithmetic: 6.15 us -> 1.87 us
    ppermute x18 -> x15, waiting for transfers between devices: 35 us -> 9.15 us  [to_z(): return lax.ppermute(value, 'expert', along_z(dz))]
    ppermute x1, waiting for transfers between devices: 0.01 us -> 12.8 us  [local(): lax.ppermute(theirs, 'expert', PARTNER)]
    ppermute x18 -> x17, waiting for transfers between devices: 40.3 us -> 31.1 us  [over_replica(): return lax.ppermute(value, 'replica', perm)]
    unnamed x16 -> x36, local copies, waits for them, and re-layouts: 3.27 us -> 9.53 us
    convert_element_type x9, other arithmetic: 6.14 us -> 1.86 us  [add(): functools.reduce(lambda a, b: a + b, [t.astype(F32) for t in terms])]
    pallas_call x3 -> x6, Pallas kernels: 44.5 us -> 45.9 us  [expert(): pl.pallas_call(functools.partial(kernel, len(after)), grid_spec=pltpu.Pre...]
    ppermute x18 -> x15, starting transfers between devices: 26.6 us -> 25.3 us  [to_z(): return lax.ppermute(value, 'expert', along_z(dz))]
    ppermute x18 -> x17, starting transfers between devices: 14.3 us -> 13.9 us  [over_replica(): return lax.ppermute(value, 'replica', perm)]
  transfers between devices with their start and end apart: 38 -> 34, of which waited for: 19 -> 16; matrix products, arithmetic and copies ran while one was open for 3% -> 1% of each run, Pallas kernels for 27% -> 28%
where the time goes in v1:
time: 171 us; the launch traced here: 169 us
  waiting for transfers between devices  58.1 us (34%)
  Pallas kernels  53.1 us (31%)
  starting transfers between devices  45.5 us (27%)
  local copies, waits for them, and re-layouts  9.53 us (6%)
  other arithmetic  1.87 us (1%)
    pallas_call x6, Pallas kernels, expert(): pl.pallas_call(functools.partial(kernel, len(after)), grid_spec=pltpu.Pre...  45.9 us
    ppermute x17, waiting for transfers between devices, over_replica(): return lax.ppermute(value, 'replica', perm)  31.1 us
    ppermute x15, starting transfers between devices, to_z(): return lax.ppermute(value, 'expert', along_z(dz))  25.3 us
    ppermute x17, starting transfers between devices, over_replica(): return lax.ppermute(value, 'replica', perm)  13.9 us
    ppermute x1, waiting for transfers between devices, local(): lax.ppermute(theirs, 'expert', PARTNER)  12.8 us
    unnamed x36, local copies, waits for them, and re-layouts  9.53 us
    ppermute x15, waiting for transfers between devices, to_z(): return lax.ppermute(value, 'expert', along_z(dz))  9.15 us
    pallas_call x10, Pallas kernels, call(): pl.pallas_call(kernel, in_specs=in_specs, out_specs=jax.tree.map(lambda _...  7.14 us
  transfers between devices with their start and end apart: 34, of which 16 were waited for; matrix products, arithmetic and copies ran while one was open for 1% of the time, Pallas kernels for 28%

profile of v1, /device:TPU:0, one launch (start us, length us, event | category | flops | bytes accessed | tf_op | source)
XLA Modules:
  0.0 169.0 jit_solution(6231603903348367936)
XLA Ops:
  0.6 0.9 copy-done.7
  1.6 0.9 copy-done.8
  2.5 0.7 copy-done.11
  3.2 0.7 copy-done.12
  4.0 3.2 %collective-permute-start = (bf16[528,512]{1,0:T(8,128)(2,1)S(1)}, bf16[528,512]{1,0:T(8,128)(2,1)S(1)}, u32[]{:S(2)}, u32[]{:S(2)}) collective-permute-start(bf16[528,512]{1,0:T(8,128)(2,1)S(1)} %pack.1.packed_ref), channel_id=1, source_target_pairs={{0,16},{16,0},{32,48},{48,32},{64,80},{80,64},{96,112},{112,96},{1... | collective-permute-start | bytes 1622024 | tf_op jit(solution)/shard_map/ppermute | solution.py:364
  7.2 0.7 own_slots.1
  7.9 2.0 %collective-permute-start.1 = (bf16[3,2,48,512]{3,2,1,0:T(8,128)(2,1)S(1)}, bf16[3,2,48,512]{3,2,1,0:T(8,128)(2,1)S(1)}, u32[]{:S(2)}, u32[]{:S(2)}) collective-permute-start(bf16[3,2,48,512]{3,2,1,0:T(8,128)(2,1)S(1)} %get-tuple-element.58), channel_id=1, source_target_pairs={{0,32},{16,48},{32,64},{48,80},{64,96},{80,112},{96,0},{112,16},{1... | collective-permute-start | bytes 884744 | tf_op jit(solution)/shard_map/ppermute | solution.py:350
  9.9 3.6 %collective-permute-start.2 = (bf16[3,2,48,512]{3,2,1,0:T(8,128)(2,1)S(1)}, bf16[3,2,48,512]{3,2,1,0:T(8,128)(2,1)S(1)}, u32[]{:S(2)}, u32[]{:S(2)}) collective-permute-start(bf16[3,2,48,512]{3,2,1,0:T(8,128)(2,1)S(1)} %get-tuple-element.59), channel_id=1, source_target_pairs={{0,64},{16,80},{32,96},{48,112},{64,0},{80,16},{96,32},{112,48},{1... | collective-permute-start | bytes 884744 | tf_op jit(solution)/shard_map/ppermute | solution.py:350
  13.5 1.0 collective-permute-start.3
  14.5 5.0 %collective-permute-done.packed_ref = bf16[528,512]{1,0:T(8,128)(2,1)S(1)} collective-permute-done((bf16[528,512]{1,0:T(8,128)(2,1)S(1)}, bf16[528,512]{1,0:T(8,128)(2,1)S(1)}, u32[]{:S(2)}, u32[]{:S(2)}) %collective-permute-start) | collective-permute-done | bytes 540704 | tf_op jit(solution)/shard_map/ppermute | solution.py:364
  19.5 0.7 partner_slots.1
  20.2 0.7 copy-done.15
  20.9 2.1 %collective-permute-start.4 = (bf16[1,2,48,512]{3,2,1,0:T(8,128)(2,1)S(1)}, bf16[1,2,48,512]{3,2,1,0:T(8,128)(2,1)S(1)}, u32[]{:S(2)}, u32[]{:S(2)}) collective-permute-start(bf16[1,2,48,512]{3,2,1,0:T(8,128)(2,1)S(1)} %get-tuple-element.62), channel_id=1, source_target_pairs={{0,32},{16,48},{32,64},{48,80},{64,96},{80,112},{96,0},{112,16},{1... | collective-permute-start | bytes 294920 | tf_op jit(solution)/shard_map/ppermute | solution.py:350
  23.0 3.6 %collective-permute-start.5 = (bf16[1,2,48,512]{3,2,1,0:T(8,128)(2,1)S(1)}, bf16[1,2,48,512]{3,2,1,0:T(8,128)(2,1)S(1)}, u32[]{:S(2)}, u32[]{:S(2)}) collective-permute-start(bf16[1,2,48,512]{3,2,1,0:T(8,128)(2,1)S(1)} %get-tuple-element.63), channel_id=1, source_target_pairs={{0,64},{16,80},{32,96},{48,112},{64,0},{80,16},{96,32},{112,48},{1... | collective-permute-start | bytes 294920 | tf_op jit(solution)/shard_map/ppermute | solution.py:350
  26.6 1.0 collective-permute-start.6
  27.6 1.8 %collective-permute-done.4.refs_5_ = bf16[1,2,48,512]{3,2,1,0:T(8,128)(2,1)S(1)} collective-permute-done((bf16[1,2,48,512]{3,2,1,0:T(8,128)(2,1)S(1)}, bf16[1,2,48,512]{3,2,1,0:T(8,128)(2,1)S(1)}, u32[]{:S(2)}, u32[]{:S(2)}) %collective-permute-start.4) | collective-permute-done | bytes 98336 | tf_op jit(solution)/shard_map/ppermute | solution.py:350
  29.4 1.1 collective-permute-done.5.refs_6_
  30.5 0.8 collective-permute-done.6.refs_7_
  31.4 0.6 collective-permute-start.8
  32.0 3.1 %collective-permute-start.9 = (bf16[2,2,48,512]{3,2,1,0:T(8,128)(2,1)}, bf16[2,2,48,512]{3,2,1,0:T(8,128)(2,1)S(1)}, u32[]{:S(2)}, u32[]{:S(2)}) collective-permute-start(bf16[2,2,48,512]{3,2,1,0:T(8,128)(2,1)} %copy-done.14), channel_id=1, source_target_pairs={{0,64},{16,80},{32,96},{48,112},{64,0},{80,16},{96,32},{112,48},{1... | collective-permute-start | bytes 589832 | tf_op jit(solution)/shard_map/ppermute | solution.py:350
  35.1 0.5 collective-permute-start.10
  35.7 2.8 %copy-done = bf16[3,512,2048]{2,1,0:T(8,128)(2,1)S(1)} copy-done((bf16[3,512,2048]{2,1,0:T(8,128)(2,1)S(1)}, bf16[3,512,2048]{2,1,0:T(8,128)(2,1)}, u32[]{:S(2)}) %copy-start) | copy-done | bytes 6291480
  38.4 2.8 %copy-done.2 = bf16[3,512,2048]{2,1,0:T(8,128)(2,1)S(1)} copy-done((bf16[3,512,2048]{2,1,0:T(8,128)(2,1)S(1)}, bf16[3,512,2048]{2,1,0:T(8,128)(2,1)}, u32[]{:S(2)}) %copy-start.2) | copy-done | bytes 6291480
  41.2 4.7 %expert0_first.1 = (bf16[2,1536,128]{2,1,0:T(8,128)(2,1)S(1)}, f32[768,512]{1,0:T(8,128)S(1)}, f32[768,512]{1,0:T(8,128)S(1)}) custom-call(s32[8]{0:T(128)S(1)} %add_add_fusion.tbl_ref, bf16[1,8,2,48,512]{4,3,2,1,0:T(8,128)(2,1)S(1)} %join0.1.own_ref, bf16[1,8,2,48,512]{4,3,2,1,0:T(8,128)(2,1)S(1)} %collective-permute-done.7.oth_ref, ...), custom_call_target="tpu_custom_call" | custom-call | flops 1811939328 | bytes 1000000 | tf_op jit(solution)/shard_map/expert0_first/pallas_call | solution.py:239
  46.2 1.7 collective-permute-start.13
  47.9 11.2 %expert0_rest.1 = (bf16[2,1536,128]{2,1,0:T(8,128)(2,1)S(1)}, bf16[2,1536,128]{2,1,0:T(8,128)(2,1)S(1)}, bf16[1536,128]{1,0:T(8,128)(2,1)S(1)}, bf16[1536,128]{1...) custom-call(s32[8]{0:T(128)S(1)} %add_add_fusion.tbl_ref, ...), custom_call_target="tpu_custom_call" | custom-call | flops 5435817984 | bytes 1000000 | tf_op jit(solution)/shard_map/expert0_rest/pallas_call | solution.py:239
  59.1 0.4 collective-permute-done.13
  59.5 0.2 add_convert_fusion.5.refs_6_
  59.7 1.5 collective-permute-start.18
  61.2 4.2 %expert1_first.1 = (bf16[2,1536,128]{2,1,0:T(8,128)(2,1)S(1)}, f32[768,512]{1,0:T(8,128)S(1)}, f32[768,512]{1,0:T(8,128)S(1)}) custom-call(s32[8]{0:T(128)S(1)} %add_add_fusion.tbl_ref, bf16[2,8,2,48,512]{4,3,2,1,0:T(8,128)(2,1)S(1)} %join12.1.refs_8_.own_ref, bf16[2,8,2,48,512]{4,3,2,1,0:T(8,128)(2,1)S(1)} %collective-permute-done.12.oth_ref, ...), custom_call_target="tpu_custom_call" | custom-call | flops 1811939328 | bytes 1000000 | tf_op jit(solution)/shard_map/expert1_first/pallas_call | solution.py:239
  65.3 1.4 collective-permute-start.19
  66.7 10.8 %expert1_rest.1 = (bf16[2,1536,128]{2,1,0:T(8,128)(2,1)S(1)}, bf16[2,1536,128]{2,1,0:T(8,128)(2,1)S(1)}, bf16[1536,128]{1,0:T(8,128)(2,1)S(1)}, bf16[1536,128]{1...) custom-call(s32[8]{0:T(128)S(1)} %add_add_fusion.tbl_ref, ...), custom_call_target="tpu_custom_call" | custom-call | flops 5435817984 | bytes 1000000 | tf_op jit(solution)/shard_map/expert1_rest/pallas_call | solution.py:239
  77.6 0.2 add_convert_fusion.4.refs_6_
  77.8 3.8 %collective-permute-done.19 = bf16[2,1536,128]{2,1,0:T(8,128)(2,1)S(1)} collective-permute-done((bf16[2,1536,128]{2,1,0:T(8,128)(2,1)S(1)}, bf16[2,1536,128]{2,1,0:T(8,128)(2,1)S(1)}, u32[]{:S(2)}, u32[]{:S(2)}) %collective-permute-start.19) | collective-permute-done | bytes 786464 | tf_op jit(solution)/shard_map/ppermute | solution.py:347
  81.8 4.2 %expert2_first.1 = (bf16[2,1536,128]{2,1,0:T(8,128)(2,1)S(1)}, f32[768,512]{1,0:T(8,128)S(1)}, f32[768,512]{1,0:T(8,128)S(1)}) custom-call(s32[8]{0:T(128)S(1)} %add_add_fusion.tbl_ref, bf16[2,8,2,48,512]{4,3,2,1,0:T(8,128)(2,1)S(1)} %join12.1.refs_8_.own_ref, bf16[2,8,2,48,512]{4,3,2,1,0:T(8,128)(2,1)S(1)} %collective-permute-done.12.oth_ref, ...), custom_call_target="tpu_custom_call" | custom-call | flops 1811939328 | bytes 1000000 | tf_op jit(solution)/shard_map/expert2_first/pallas_call | solution.py:239
  86.0 0.9 collective-permute-start.11
  86.9 0.9 collective-permute-start.27
  87.8 10.8 %expert2_rest.1 = (bf16[2,1536,128]{2,1,0:T(8,128)(2,1)S(1)}, bf16[2,1536,128]{2,1,0:T(8,128)(2,1)S(1)}, bf16[1536,128]{1,0:T(8,128)(2,1)S(1)}, bf16[1536,128]{1...) custom-call(s32[8]{0:T(128)S(1)} %add_add_fusion.tbl_ref, ...), custom_call_target="tpu_custom_call" | custom-call | flops 5435817984 | bytes 1000000 | tf_op jit(solution)/shard_map/expert2_rest/pallas_call | solution.py:239
  98.7 1.7 %collective-permute-start.20 = (bf16[2,384,512]{2,1,0:T(8,128)(2,1)S(1)}, bf16[2,384,512]{2,1,0:T(8,128)(2,1)S(1)}, u32[]{:S(2)}, u32[]{:S(2)}) collective-permute-start(bf16[2,384,512]{2,1,0:T(8,128)(2,1)S(1)} %get-tuple-element.89), channel_id=1, source_target_pairs={{0,1},{1,0},{2,3},{3,2},{4,5},{5,4},{6,7},{7,6},{8,9},{9,8},{10,11... | collective-permute-start | bytes 2359304 | tf_op jit(solution)/shard_map/ppermute | solution.py:347
  100.7 1.7 %collective-permute-start.25 = (bf16[2,1536,128]{2,1,0:T(8,128)(2,1)S(1)}, bf16[2,1536,128]{2,1,0:T(8,128)(2,1)S(1)}, u32[]{:S(2)}, u32[]{:S(2)}) collective-permute-start(bf16[2,1536,128]{2,1,0:T(8,128)(2,1)S(1)} %add_convert_fusion.4.refs_6_), channel_id=1, source_target_pairs={{0,4},{1,13},{2,6},{3,15},{4,8},{5,1},{6,10},{7,3},{8,12},{9,5},{1... | collective-permute-start | bytes 2359304 | tf_op jit(solution)/shard_map/ppermute | solution.py:347
  102.4 0.4 back01.1
  102.8 1.6 collective-permute-start.15
  104.5 3.2 %collective-permute-done.27 = bf16[2,1536,128]{2,1,0:T(8,128)(2,1)S(1)} collective-permute-done((bf16[2,1536,128]{2,1,0:T(8,128)(2,1)S(1)}, bf16[2,1536,128]{2,1,0:T(8,128)(2,1)S(1)}, u32[]{:S(2)}, u32[]{:S(2)}) %collective-permute-start.27) | collective-permute-done | bytes 786464 | tf_op jit(solution)/shard_map/ppermute | solution.py:347
  107.7 2.0 %collective-permute-start.16 = (bf16[2,2,2,48,512]{4,3,2,1,0:T(8,128)(2,1)S(1)}, bf16[2,2,2,48,512]{4,3,2,1,0:T(8,128)(2,1)S(1)}, u32[]{:S(2)}, u32[]{:S(2)}) collective-permute-start(bf16[2,2,2,48,512]{4,3,2,1,0:T(8,128)(2,1)S(1)} %get-tuple-element.81), channel_id=1, source_target_pairs={{0,64},{16,80},{32,96},{48,112},{64,0},{80,16},{96,32},{112,48},{1... | collective-permute-start | bytes 1179656 | tf_op jit(solution)/shard_map/ppermute | solution.py:350
  109.9 0.5 collective-permute-start.17
  110.6 5.5 %collective-permute-done.31 = bf16[2,1536,128]{2,1,0:T(8,128)(2,1)S(1)} collective-permute-done((bf16[2,1536,128]{2,1,0:T(8,128)(2,1)S(1)}, bf16[2,1536,128]{2,1,0:T(8,128)(2,1)S(1)}, u32[]{:S(2)}, u32[]{:S(2)}) %collective-permute-start.31) | collective-permute-done | bytes 786464 | tf_op jit(solution)/shard_map/ppermute | solution.py:347
  116.3 8.2 %collective-permute-done.25 = bf16[2,1536,128]{2,1,0:T(8,128)(2,1)S(1)} collective-permute-done((bf16[2,1536,128]{2,1,0:T(8,128)(2,1)S(1)}, bf16[2,1536,128]{2,1,0:T(8,128)(2,1)S(1)}, u32[]{:S(2)}, u32[]{:S(2)}) %collective-permute-start.25) | collective-permute-done | bytes 786464 | tf_op jit(solution)/shard_map/ppermute | solution.py:347
  124.5 1.6 collective-permute-start.21
  126.1 2.0 %collective-permute-start.22 = (bf16[1,2,2,48,512]{4,3,2,1,0:T(8,128)(2,1)S(1)}, bf16[1,2,2,48,512]{4,3,2,1,0:T(8,128)(2,1)S(1)}, u32[]{:S(2)}, u32[]{:S(2)}) collective-permute-start(bf16[1,2,2,48,512]{4,3,2,1,0:T(8,128)(2,1)S(1)} %get-tuple-element.92), channel_id=1, source_target_pairs={{0,64},{16,80},{32,96},{48,112},{64,0},{80,16},{96,32},{112,48},{1... | collective-permute-start | bytes 589832 | tf_op jit(solution)/shard_map/ppermute | solution.py:350
  128.2 0.2 fusion.4
  128.4 2.1 %collective-permute-done.21.refs_5_ = bf16[1,2,2,48,512]{4,3,2,1,0:T(8,128)(2,1)S(1)} collective-permute-done((bf16[1,2,2,48,512]{4,3,2,1,0:T(8,128)(2,1)S(1)}, bf16[1,2,2,48,512]{4,3,2,1,0:T(8,128)(2,1)S(1)}, u32[]{:S(2)}, u32[]{:S(2)}) %collective-permute-start.21) | collective-permute-done | bytes 196640 | tf_op jit(solution)/shard_map/ppermute | solution.py:350
  130.6 1.5 collective-permute-start.26
  132.0 1.3 collective-permute-done.22.refs_6_
  133.4 2.1 %collective-permute-done.23.refs_7_ = bf16[1,2,2,48,512]{4,3,2,1,0:T(8,128)(2,1)S(1)} collective-permute-done((bf16[1,2,2,48,512]{4,3,2,1,0:T(8,128)(2,1)S(1)}, bf16[1,2,2,48,512]{4,3,2,1,0:T(8,128)(2,1)S(1)}, u32[]{:S(2)}, u32[]{:S(2)}) %collective-permute-start.23) | collective-permute-done | bytes 196640 | tf_op jit(solution)/shard_map/ppermute | solution.py:350
  135.4 1.4 partner_sums.1
  136.9 3.1 %collective-permute-start.24 = (bf16[2,256,512]{2,1,0:T(8,128)(2,1)S(1)}, bf16[2,256,512]{2,1,0:T(8,128)(2,1)S(1)}, u32[]{:S(2)}, u32[]{:S(2)}) collective-permute-start(bf16[2,256,512]{2,1,0:T(8,128)(2,1)S(1)} %partner_sums.1), channel_id=1, source_target_pairs={{0,16},{16,0},{32,48},{48,32},{64,80},{80,64},{96,112},{112,96},{1... | collective-permute-start | bytes 1572872 | tf_op jit(solution)/shard_map/ppermute | solution.py:413
  140.2 0.7 collective-permute-start.29
  140.9 0.5 collective-permute-done.32
  141.6 1.6 collective-permute-start.33
  143.2 12.8 %collective-permute-done.24.other_ref = bf16[2,256,512]{2,1,0:T(8,128)(2,1)S(1)} collective-permute-done((bf16[2,256,512]{2,1,0:T(8,128)(2,1)S(1)}, bf16[2,256,512]{2,1,0:T(8,128)(2,1)S(1)}, u32[]{:S(2)}, u32[]{:S(2)}) %collective-permute-start.24) | collective-permute-done | bytes 524320 | tf_op jit(solution)/shard_map/ppermute | solution.py:413
  156.0 2.2 %combine.1 = (bf16[256,512]{1,0:T(8,128)(2,1)}, bf16[256,512]{1,0:T(8,128)(2,1)}) custom-call(s32[1]{0:T(128)} %bitcast.me_ref, bf16[528,512]{1,0:T(8,128)(2,1)S(1)} %pack.1.packed_ref, bf16[2,256,512]{2,1,0:T(8,128)(2,1)S(1)} %collective-permute-done.24.other_ref, bf16[2,2,2,48,512]{4,3,2,1,0:T(8,128)(2,1)S(1)} %get-tuple-element.79.refs_0_, ...), custom_call_target="tpu_custom_call" | custom-call | bytes 3000000 | tf_op jit(solution)/shard_map/combine/pallas_call | solution.py:34
  158.2 3.7 %collective-permute-done.29.refs_3_ = bf16[1536,128]{1,0:T(8,128)(2,1)S(1)} collective-permute-done((bf16[1536,128]{1,0:T(8,128)(2,1)S(1)}, bf16[1536,128]{1,0:T(8,128)(2,1)S(1)}, u32[]{:S(2)}, u32[]{:S(2)}) %collective-permute-start.29) | collective-permute-done | bytes 393248 | tf_op jit(solution)/shard_map/ppermute | solution.py:347
  161.9 5.9 %collective-permute-done.33.refs_5_ = bf16[1536,128]{1,0:T(8,128)(2,1)S(1)} collective-permute-done((bf16[1536,128]{1,0:T(8,128)(2,1)S(1)}, bf16[1536,128]{1,0:T(8,128)(2,1)S(1)}, u32[]{:S(2)}, u32[]{:S(2)}) %collective-permute-start.33) | collective-permute-done | bytes 393248 | tf_op jit(solution)/shard_map/ppermute | solution.py:347
  167.8 1.3 finish.1
  (67 shorter events, 2.2 us)
Async XLA Ops:
  0.6 1.0 copy-start.7
  1.6 0.9 copy-start.8
  2.5 0.7 copy-start.11
  3.2 0.7 copy-start.12
  4.0 15.5 %collective-permute-start = (bf16[528,512]{1,0:T(8,128)(2,1)S(1)}, bf16[528,512]{1,0:T(8,128)(2,1)S(1)}, u32[]{:S(2)}, u32[]{:S(2)}) collective-permute-start(bf16[528,512]{1,0:T(8,128)(2,1)S(1)} %pack.1.packed_ref), channel_id=1, source_target_pairs={{0,16},{16,0},{32,48},{48,32},{64,80},{80,64},{96,112},{112,96},{1... | collective-permute-start | bytes 1622024 | tf_op jit(solution)/shard_map/ppermute | solution.py:364
  7.9 18.7 %collective-permute-start.1 = (bf16[3,2,48,512]{3,2,1,0:T(8,128)(2,1)S(1)}, bf16[3,2,48,512]{3,2,1,0:T(8,128)(2,1)S(1)}, u32[]{:S(2)}, u32[]{:S(2)}) collective-permute-start(bf16[3,2,48,512]{3,2,1,0:T(8,128)(2,1)S(1)} %get-tuple-element.58), channel_id=1, source_target_pairs={{0,32},{16,48},{32,64},{48,80},{64,96},{80,112},{96,0},{112,16},{1... | collective-permute-start | bytes 884744 | tf_op jit(solution)/shard_map/ppermute | solution.py:350
  9.9 17.7 %collective-permute-start.2 = (bf16[3,2,48,512]{3,2,1,0:T(8,128)(2,1)S(1)}, bf16[3,2,48,512]{3,2,1,0:T(8,128)(2,1)S(1)}, u32[]{:S(2)}, u32[]{:S(2)}) collective-permute-start(bf16[3,2,48,512]{3,2,1,0:T(8,128)(2,1)S(1)} %get-tuple-element.59), channel_id=1, source_target_pairs={{0,64},{16,80},{32,96},{48,112},{64,0},{80,16},{96,32},{112,48},{1... | collective-permute-start | bytes 884744 | tf_op jit(solution)/shard_map/ppermute | solution.py:350
  13.5 14.1 %collective-permute-start.3 = (bf16[3,2,48,512]{3,2,1,0:T(8,128)(2,1)S(1)}, bf16[3,2,48,512]{3,2,1,0:T(8,128)(2,1)S(1)}, u32[]{:S(2)}, u32[]{:S(2)}) collective-permute-start(bf16[3,2,48,512]{3,2,1,0:T(8,128)(2,1)S(1)} %get-tuple-element.60), channel_id=1, source_target_pairs={{0,96},{16,112},{32,0},{48,16},{64,32},{80,48},{96,64},{112,80},{1... | collective-permute-start | bytes 884744 | tf_op jit(solution)/shard_map/ppermute | solution.py:350
  19.5 11.8 %copy-start.5 = (bf16[528,512]{1,0:T(8,128)(2,1)}, bf16[528,512]{1,0:T(8,128)(2,1)S(1)}, u32[]{:S(2)}) copy-start(bf16[528,512]{1,0:T(8,128)(2,1)S(1)} %collective-permute-done.packed_ref) | copy-start | bytes 1622020
  20.2 0.7 copy-start.15
  20.9 10.4 %copy-start.13 = (bf16[2,2,48,512]{3,2,1,0:T(8,128)(2,1)}, bf16[2,2,48,512]{3,2,1,0:T(8,128)(2,1)S(1)}, u32[]{:S(2)}) copy-start(bf16[2,2,48,512]{3,2,1,0:T(8,128)(2,1)S(1)} %get-tuple-element.70) | copy-start | bytes 589828
  20.9 10.4 %copy-start.9 = (bf16[2,2,48,512]{3,2,1,0:T(8,128)(2,1)}, bf16[2,2,48,512]{3,2,1,0:T(8,128)(2,1)S(1)}, u32[]{:S(2)}) copy-start(bf16[2,2,48,512]{3,2,1,0:T(8,128)(2,1)S(1)} %get-tuple-element.67.refs_4_) | copy-start | bytes 589828
  20.9 10.4 %copy-start.14 = (bf16[2,2,48,512]{3,2,1,0:T(8,128)(2,1)}, bf16[2,2,48,512]{3,2,1,0:T(8,128)(2,1)S(1)}, u32[]{:S(2)}) copy-start(bf16[2,2,48,512]{3,2,1,0:T(8,128)(2,1)S(1)} %get-tuple-element.69) | copy-start | bytes 589828
  20.9 8.5 %collective-permute-start.4 = (bf16[1,2,48,512]{3,2,1,0:T(8,128)(2,1)S(1)}, bf16[1,2,48,512]{3,2,1,0:T(8,128)(2,1)S(1)}, u32[]{:S(2)}, u32[]{:S(2)}) collective-permute-start(bf16[1,2,48,512]{3,2,1,0:T(8,128)(2,1)S(1)} %get-tuple-element.62), channel_id=1, source_target_pairs={{0,32},{16,48},{32,64},{48,80},{64,96},{80,112},{96,0},{112,16},{1... | collective-permute-start | bytes 294920 | tf_op jit(solution)/shard_map/ppermute | solution.py:350
  23.0 7.4 %collective-permute-start.5 = (bf16[1,2,48,512]{3,2,1,0:T(8,128)(2,1)S(1)}, bf16[1,2,48,512]{3,2,1,0:T(8,128)(2,1)S(1)}, u32[]{:S(2)}, u32[]{:S(2)}) collective-permute-start(bf16[1,2,48,512]{3,2,1,0:T(8,128)(2,1)S(1)} %get-tuple-element.63), channel_id=1, source_target_pairs={{0,64},{16,80},{32,96},{48,112},{64,0},{80,16},{96,32},{112,48},{1... | collective-permute-start | bytes 294920 | tf_op jit(solution)/shard_map/ppermute | solution.py:350
  26.6 4.6 %collective-permute-start.6 = (bf16[1,2,48,512]{3,2,1,0:T(8,128)(2,1)S(1)}, bf16[1,2,48,512]{3,2,1,0:T(8,128)(2,1)S(1)}, u32[]{:S(2)}, u32[]{:S(2)}) collective-permute-start(bf16[1,2,48,512]{3,2,1,0:T(8,128)(2,1)S(1)} %get-tuple-element.64), channel_id=1, source_target_pairs={{0,96},{16,112},{32,0},{48,16},{64,32},{80,48},{96,64},{112,80},{1... | collective-permute-start | bytes 294920 | tf_op jit(solution)/shard_map/ppermute | solution.py:350
  31.3 4.4 %collective-permute-start.7 = (bf16[1,8,2,48,512]{4,3,2,1,0:T(8,128)(2,1)S(1)}, bf16[1,8,2,48,512]{4,3,2,1,0:T(8,128)(2,1)S(1)}, u32[]{:S(2)}, u32[]{:S(2)}) collective-permute-start(bf16[1,8,2,48,512]{4,3,2,1,0:T(8,128)(2,1)S(1)} %join0.1.own_ref), channel_id=1, source_target_pairs={{0,1},{1,0},{2,3},{3,2},{4,5},{5,4},{6,7},{7,6},{8,9},{9,8},{10,11... | collective-permute-start | bytes 2359304 | tf_op jit(solution)/shard_map/ppermute | solution.py:347
  31.4 14.6 %collective-permute-start.8 = (bf16[2,2,48,512]{3,2,1,0:T(8,128)(2,1)}, bf16[2,2,48,512]{3,2,1,0:T(8,128)(2,1)S(1)}, u32[]{:S(2)}, u32[]{:S(2)}) collective-permute-start(bf16[2,2,48,512]{3,2,1,0:T(8,128)(2,1)} %copy-done.15), channel_id=1, source_target_pairs={{0,32},{16,48},{32,64},{48,80},{64,96},{80,112},{96,0},{112,16},{1... | collective-permute-start | bytes 589832 | tf_op jit(solution)/shard_map/ppermute | solution.py:350
  32.0 14.0 %collective-permute-start.9 = (bf16[2,2,48,512]{3,2,1,0:T(8,128)(2,1)}, bf16[2,2,48,512]{3,2,1,0:T(8,128)(2,1)S(1)}, u32[]{:S(2)}, u32[]{:S(2)}) collective-permute-start(bf16[2,2,48,512]{3,2,1,0:T(8,128)(2,1)} %copy-done.14), channel_id=1, source_target_pairs={{0,64},{16,80},{32,96},{48,112},{64,0},{80,16},{96,32},{112,48},{1... | collective-permute-start | bytes 589832 | tf_op jit(solution)/shard_map/ppermute | solution.py:350
  35.1 10.8 %collective-permute-start.10 = (bf16[2,2,48,512]{3,2,1,0:T(8,128)(2,1)}, bf16[2,2,48,512]{3,2,1,0:T(8,128)(2,1)S(1)}, u32[]{:S(2)}, u32[]{:S(2)}) collective-permute-start(bf16[2,2,48,512]{3,2,1,0:T(8,128)(2,1)} %copy-done.13), channel_id=1, source_target_pairs={{0,96},{16,112},{32,0},{48,16},{64,32},{80,48},{96,64},{112,80},{1... | collective-permute-start | bytes 589832 | tf_op jit(solution)/shard_map/ppermute | solution.py:350
  35.7 2.8 %copy-start = (bf16[3,512,2048]{2,1,0:T(8,128)(2,1)S(1)}, bf16[3,512,2048]{2,1,0:T(8,128)(2,1)}, u32[]{:S(2)}) copy-start(bf16[3,512,2048]{2,1,0:T(8,128)(2,1)} %refs_1_.11) | copy-start | bytes 18874372
  38.4 2.8 %copy-start.2 = (bf16[3,512,2048]{2,1,0:T(8,128)(2,1)S(1)}, bf16[3,512,2048]{2,1,0:T(8,128)(2,1)}, u32[]{:S(2)}) copy-start(bf16[3,512,2048]{2,1,0:T(8,128)(2,1)} %refs_3_.11) | copy-start | bytes 18874372
  41.2 4.7 %copy-start.3 = (bf16[1,8,2,48,512]{4,3,2,1,0:T(8,128)(2,1)}, bf16[1,8,2,48,512]{4,3,2,1,0:T(8,128)(2,1)S(1)}, u32[]{:S(2)}) copy-start(bf16[1,8,2,48,512]{4,3,2,1,0:T(8,128)(2,1)S(1)} %collective-permute-done.7.oth_ref) | copy-start | bytes 2359300
  41.2 4.8 %copy-start.10 = (bf16[2,2,48,512]{3,2,1,0:T(8,128)(2,1)S(1)}, bf16[2,2,48,512]{3,2,1,0:T(8,128)(2,1)}, u32[]{:S(2)}) copy-start(bf16[2,2,48,512]{3,2,1,0:T(8,128)(2,1)} %copy-done.9) | copy-start | bytes 589828
  41.2 6.6 %copy-start.1 = (bf16[3,512,2048]{2,1,0:T(8,128)(2,1)S(1)}, bf16[3,512,2048]{2,1,0:T(8,128)(2,1)}, u32[]{:S(2)}) copy-start(bf16[3,512,2048]{2,1,0:T(8,128)(2,1)} %refs_1_.11) | copy-start | bytes 18874372
  46.0 1.9 %copy-start.4 = (bf16[1,8,2,48,512]{4,3,2,1,0:T(8,128)(2,1)S(1)}, bf16[1,8,2,48,512]{4,3,2,1,0:T(8,128)(2,1)}, u32[]{:S(2)}) copy-start(bf16[1,8,2,48,512]{4,3,2,1,0:T(8,128)(2,1)} %copy-done.3) | copy-start | bytes 2359300
  46.1 15.0 %collective-permute-start.12 = (bf16[2,8,2,48,512]{4,3,2,1,0:T(8,128)(2,1)S(1)}, bf16[2,8,2,48,512]{4,3,2,1,0:T(8,128)(2,1)S(1)}, u32[]{:S(2)}, u32[]{:S(2)}) collective-permute-start(bf16[2,8,2,48,512]{4,3,2,1,0:T(8,128)(2,1)S(1)} %join12.1.refs_8_.own_ref), channel_id=1, source_target_pairs={{0,1},{1,0},{2,3},{3,2},{4,5},{5,4},{6,7},{7,6},{8,9},{9,8},{10,11... | collective-permute-start | bytes 4718600 | tf_op jit(solution)/shard_map/ppermute | solution.py:347
  46.2 13.3 %collective-permute-start.13 = (bf16[2,1536,128]{2,1,0:T(8,128)(2,1)S(1)}, bf16[2,1536,128]{2,1,0:T(8,128)(2,1)S(1)}, u32[]{:S(2)}, u32[]{:S(2)}) collective-permute-start(bf16[2,1536,128]{2,1,0:T(8,128)(2,1)S(1)} %get-tuple-element.71.refs_8_), channel_id=1, source_target_pairs={{0,4},{1,13},{2,6},{3,15},{4,8},{5,1},{6,10},{7,3},{8,12},{9,5},{1... | collective-permute-start | bytes 2359304 | tf_op jit(solution)/shard_map/ppermute | solution.py:347
  47.9 13.3 %slice-start = ((s8[6291456]{0:T(1024)(128)(4,1)}), s8[4194304]{0:T(1024)(128)(4,1)S(1)}, s32[]{:S(2)}) async-start(s8[6291456]{0:T(1024)(128)(4,1)} %bitcast.33), calls=%async_computation | async-start | bytes 8388608
  47.9 13.3 %slice-start.1 = ((s8[6291456]{0:T(1024)(128)(4,1)}), s8[2097152]{0:T(1024)(128)(4,1)S(1)}, s32[]{:S(2)}) async-start(s8[6291456]{0:T(1024)(128)(4,1)} %bitcast.33), calls=%async_computation.1 | async-start | bytes 4194304
  59.7 17.9 %collective-permute-start.18 = (bf16[2,1536,128]{2,1,0:T(8,128)(2,1)S(1)}, bf16[2,1536,128]{2,1,0:T(8,128)(2,1)S(1)}, u32[]{:S(2)}, u32[]{:S(2)}) collective-permute-start(bf16[2,1536,128]{2,1,0:T(8,128)(2,1)S(1)} %add_convert_fusion.5.refs_6_), channel_id=1, source_target_pairs={{0,4},{1,13},{2,6},{3,15},{4,8},{5,1},{6,10},{7,3},{8,12},{9,5},{1... | collective-permute-start | bytes 2359304 | tf_op jit(solution)/shard_map/ppermute | solution.py:347
  65.3 16.2 %collective-permute-start.19 = (bf16[2,1536,128]{2,1,0:T(8,128)(2,1)S(1)}, bf16[2,1536,128]{2,1,0:T(8,128)(2,1)S(1)}, u32[]{:S(2)}, u32[]{:S(2)}) collective-permute-start(bf16[2,1536,128]{2,1,0:T(8,128)(2,1)S(1)} %get-tuple-element.85), channel_id=1, source_target_pairs={{0,4},{1,13},{2,6},{3,15},{4,8},{5,1},{6,10},{7,3},{8,12},{9,5},{1... | collective-permute-start | bytes 2359304 | tf_op jit(solution)/shard_map/ppermute | solution.py:347
  86.0 14.5 %collective-permute-start.30 = (bf16[2,1536,128]{2,1,0:T(8,128)(2,1)S(1)}, bf16[2,1536,128]{2,1,0:T(8,128)(2,1)S(1)}, u32[]{:S(2)}, u32[]{:S(2)}) collective-permute-start(bf16[2,1536,128]{2,1,0:T(8,128)(2,1)S(1)} %get-tuple-element.104), channel_id=1, source_target_pairs={{0,4},{1,13},{2,6},{3,15},{4,8},{5,1},{6,10},{7,3},{8,12},{9,5},{1... | collective-permute-start | bytes 2359304 | tf_op jit(solution)/shard_map/ppermute | solution.py:347
  86.0 14.7 %collective-permute-start.11 = (bf16[2,384,512]{2,1,0:T(8,128)(2,1)S(1)}, bf16[2,384,512]{2,1,0:T(8,128)(2,1)S(1)}, u32[]{:S(2)}, u32[]{:S(2)}) collective-permute-start(bf16[2,384,512]{2,1,0:T(8,128)(2,1)S(1)} %get-tuple-element.73), channel_id=1, source_target_pairs={{0,1},{1,0},{2,3},{3,2},{4,5},{5,4},{6,7},{7,6},{8,9},{9,8},{10,11... | collective-permute-start | bytes 2359304 | tf_op jit(solution)/shard_map/ppermute | solution.py:347
  86.9 15.5 %collective-permute-start.14 = (bf16[2,384,512]{2,1,0:T(8,128)(2,1)S(1)}, bf16[2,384,512]{2,1,0:T(8,128)(2,1)S(1)}, u32[]{:S(2)}, u32[]{:S(2)}) collective-permute-start(bf16[2,384,512]{2,1,0:T(8,128)(2,1)S(1)} %get-tuple-element.78), channel_id=1, source_target_pairs={{0,1},{1,0},{2,3},{3,2},{4,5},{5,4},{6,7},{7,6},{8,9},{9,8},{10,11... | collective-permute-start | bytes 2359304 | tf_op jit(solution)/shard_map/ppermute | solution.py:347
  86.9 20.8 %collective-permute-start.27 = (bf16[2,1536,128]{2,1,0:T(8,128)(2,1)S(1)}, bf16[2,1536,128]{2,1,0:T(8,128)(2,1)S(1)}, u32[]{:S(2)}, u32[]{:S(2)}) collective-permute-start(bf16[2,1536,128]{2,1,0:T(8,128)(2,1)S(1)} %add_convert_fusion.3.refs_7_), channel_id=1, source_target_pairs={{0,4},{1,13},{2,6},{3,15},{4,8},{5,1},{6,10},{7,3},{8,12},{9,5},{1... | collective-permute-start | bytes 2359304 | tf_op jit(solution)/shard_map/ppermute | solution.py:347
  98.7 11.2 %collective-permute-start.20 = (bf16[2,384,512]{2,1,0:T(8,128)(2,1)S(1)}, bf16[2,384,512]{2,1,0:T(8,128)(2,1)S(1)}, u32[]{:S(2)}, u32[]{:S(2)}) collective-permute-start(bf16[2,384,512]{2,1,0:T(8,128)(2,1)S(1)} %get-tuple-element.89), channel_id=1, source_target_pairs={{0,1},{1,0},{2,3},{3,2},{4,5},{5,4},{6,7},{7,6},{8,9},{9,8},{10,11... | collective-permute-start | bytes 2359304 | tf_op jit(solution)/shard_map/ppermute | solution.py:347
  100.6 15.5 %collective-permute-start.31 = (bf16[2,1536,128]{2,1,0:T(8,128)(2,1)S(1)}, bf16[2,1536,128]{2,1,0:T(8,128)(2,1)S(1)}, u32[]{:S(2)}, u32[]{:S(2)}) collective-permute-start(bf16[2,1536,128]{2,1,0:T(8,128)(2,1)S(1)} %add_convert_fusion.1), channel_id=1, source_target_pairs={{0,4},{1,13},{2,6},{3,15},{4,8},{5,1},{6,10},{7,3},{8,12},{9,5},{1... | collective-permute-start | bytes 2359304 | tf_op jit(solution)/shard_map/ppermute | solution.py:347
  100.7 23.8 %collective-permute-start.25 = (bf16[2,1536,128]{2,1,0:T(8,128)(2,1)S(1)}, bf16[2,1536,128]{2,1,0:T(8,128)(2,1)S(1)}, u32[]{:S(2)}, u32[]{:S(2)}) collective-permute-start(bf16[2,1536,128]{2,1,0:T(8,128)(2,1)S(1)} %add_convert_fusion.4.refs_6_), channel_id=1, source_target_pairs={{0,4},{1,13},{2,6},{3,15},{4,8},{5,1},{6,10},{7,3},{8,12},{9,5},{1... | collective-permute-start | bytes 2359304 | tf_op jit(solution)/shard_map/ppermute | solution.py:347
  102.8 23.3 %collective-permute-start.15 = (bf16[2,2,2,48,512]{4,3,2,1,0:T(8,128)(2,1)S(1)}, bf16[2,2,2,48,512]{4,3,2,1,0:T(8,128)(2,1)S(1)}, u32[]{:S(2)}, u32[]{:S(2)}) collective-permute-start(bf16[2,2,2,48,512]{4,3,2,1,0:T(8,128)(2,1)S(1)} %get-tuple-element.80), channel_id=1, source_target_pairs={{0,96},{16,112},{32,0},{48,16},{64,32},{80,48},{96,64},{112,80},{1... | collective-permute-start | bytes 1179656 | tf_op jit(solution)/shard_map/ppermute | solution.py:350
  107.7 20.5 %collective-permute-start.16 = (bf16[2,2,2,48,512]{4,3,2,1,0:T(8,128)(2,1)S(1)}, bf16[2,2,2,48,512]{4,3,2,1,0:T(8,128)(2,1)S(1)}, u32[]{:S(2)}, u32[]{:S(2)}) collective-permute-start(bf16[2,2,2,48,512]{4,3,2,1,0:T(8,128)(2,1)S(1)} %get-tuple-element.81), channel_id=1, source_target_pairs={{0,64},{16,80},{32,96},{48,112},{64,0},{80,16},{96,32},{112,48},{1... | collective-permute-start | bytes 1179656 | tf_op jit(solution)/shard_map/ppermute | solution.py:350
  109.9 18.3 %collective-permute-start.17 = (bf16[2,2,2,48,512]{4,3,2,1,0:T(8,128)(2,1)S(1)}, bf16[2,2,2,48,512]{4,3,2,1,0:T(8,128)(2,1)S(1)}, u32[]{:S(2)}, u32[]{:S(2)}) collective-permute-start(bf16[2,2,2,48,512]{4,3,2,1,0:T(8,128)(2,1)S(1)} %get-tuple-element.82), channel_id=1, source_target_pairs={{0,32},{16,48},{32,64},{48,80},{64,96},{80,112},{96,0},{112,16},{1... | collective-permute-start | bytes 1179656 | tf_op jit(solution)/shard_map/ppermute | solution.py:350
  116.1 23.9 %collective-permute-start.28 = (bf16[2,1536,128]{2,1,0:T(8,128)(2,1)S(1)}, bf16[2,1536,128]{2,1,0:T(8,128)(2,1)S(1)}, u32[]{:S(2)}, u32[]{:S(2)}) collective-permute-start(bf16[2,1536,128]{2,1,0:T(8,128)(2,1)S(1)} %add_convert_fusion.2), channel_id=1, source_target_pairs={{0,4},{1,13},{2,6},{3,15},{4,8},{5,1},{6,10},{7,3},{8,12},{9,5},{1... | collective-permute-start | bytes 2359304 | tf_op jit(solution)/shard_map/ppermute | solution.py:347
  116.3 19.1 %copy-start.6 = (bf16[528,512]{1,0:T(8,128)(2,1)S(1)}, bf16[528,512]{1,0:T(8,128)(2,1)}, u32[]{:S(2)}) copy-start(bf16[528,512]{1,0:T(8,128)(2,1)} %copy-done.5) | copy-start | bytes 1622020
  124.5 6.1 %collective-permute-start.21 = (bf16[1,2,2,48,512]{4,3,2,1,0:T(8,128)(2,1)S(1)}, bf16[1,2,2,48,512]{4,3,2,1,0:T(8,128)(2,1)S(1)}, u32[]{:S(2)}, u32[]{:S(2)}) collective-permute-start(bf16[1,2,2,48,512]{4,3,2,1,0:T(8,128)(2,1)S(1)} %get-tuple-element.91), channel_id=1, source_target_pairs={{0,96},{16,112},{32,0},{48,16},{64,32},{80,48},{96,64},{112,80},{1... | collective-permute-start | bytes 589832 | tf_op jit(solution)/shard_map/ppermute | solution.py:350
  126.1 7.3 %collective-permute-start.22 = (bf16[1,2,2,48,512]{4,3,2,1,0:T(8,128)(2,1)S(1)}, bf16[1,2,2,48,512]{4,3,2,1,0:T(8,128)(2,1)S(1)}, u32[]{:S(2)}, u32[]{:S(2)}) collective-permute-start(bf16[1,2,2,48,512]{4,3,2,1,0:T(8,128)(2,1)S(1)} %get-tuple-element.92), channel_id=1, source_target_pairs={{0,64},{16,80},{32,96},{48,112},{64,0},{80,16},{96,32},{112,48},{1... | collective-permute-start | bytes 589832 | tf_op jit(solution)/shard_map/ppermute | solution.py:350
  128.1 7.3 %collective-permute-start.23 = (bf16[1,2,2,48,512]{4,3,2,1,0:T(8,128)(2,1)S(1)}, bf16[1,2,2,48,512]{4,3,2,1,0:T(8,128)(2,1)S(1)}, u32[]{:S(2)}, u32[]{:S(2)}) collective-permute-start(bf16[1,2,2,48,512]{4,3,2,1,0:T(8,128)(2,1)S(1)} %get-tuple-element.93), channel_id=1, source_target_pairs={{0,32},{16,48},{32,64},{48,80},{64,96},{80,112},{96,0},{112,16},{1... | collective-permute-start | bytes 589832 | tf_op jit(solution)/shard_map/ppermute | solution.py:350
  128.1 13.3 %collective-permute-start.32 = (bf16[2,1536,128]{2,1,0:T(8,128)(2,1)S(1)}, bf16[2,1536,128]{2,1,0:T(8,128)(2,1)S(1)}, u32[]{:S(2)}, u32[]{:S(2)}) collective-permute-start(bf16[2,1536,128]{2,1,0:T(8,128)(2,1)S(1)} %add_convert_fusion), channel_id=1, source_target_pairs={{0,4},{1,13},{2,6},{3,15},{4,8},{5,1},{6,10},{7,3},{8,12},{9,5},{1... | collective-permute-start | bytes 2359304 | tf_op jit(solution)/shard_map/ppermute | solution.py:347
  130.6 27.7 %collective-permute-start.26 = (bf16[1536,128]{1,0:T(8,128)(2,1)S(1)}, bf16[1536,128]{1,0:T(8,128)(2,1)S(1)}, u32[]{:S(2)}, u32[]{:S(2)}) collective-permute-start(bf16[1536,128]{1,0:T(8,128)(2,1)S(1)} %get-tuple-element.113), channel_id=1, source_target_pairs={{0,2},{1,3},{2,0},{3,1},{4,6},{5,7},{6,4},{7,5},{8,10},{9,11},{10,... | collective-permute-start | bytes 1179656 | tf_op jit(solution)/shard_map/ppermute | solution.py:347
  136.9 19.2 %collective-permute-start.24 = (bf16[2,256,512]{2,1,0:T(8,128)(2,1)S(1)}, bf16[2,256,512]{2,1,0:T(8,128)(2,1)S(1)}, u32[]{:S(2)}, u32[]{:S(2)}) collective-permute-start(bf16[2,256,512]{2,1,0:T(8,128)(2,1)S(1)} %partner_sums.1), channel_id=1, source_target_pairs={{0,16},{16,0},{32,48},{48,32},{64,80},{80,64},{96,112},{112,96},{1... | collective-permute-start | bytes 1572872 | tf_op jit(solution)/shard_map/ppermute | solution.py:413
  140.2 21.7 %collective-permute-start.29 = (bf16[1536,128]{1,0:T(8,128)(2,1)S(1)}, bf16[1536,128]{1,0:T(8,128)(2,1)S(1)}, u32[]{:S(2)}, u32[]{:S(2)}) collective-permute-start(bf16[1536,128]{1,0:T(8,128)(2,1)S(1)} %get-tuple-element.111), channel_id=1, source_target_pairs={{0,2},{1,3},{2,0},{3,1},{4,6},{5,7},{6,4},{7,5},{8,10},{9,11},{10,... | collective-permute-start | bytes 1179656 | tf_op jit(solution)/shard_map/ppermute | solution.py:347
  141.6 26.1 %collective-permute-start.33 = (bf16[1536,128]{1,0:T(8,128)(2,1)S(1)}, bf16[1536,128]{1,0:T(8,128)(2,1)S(1)}, u32[]{:S(2)}, u32[]{:S(2)}) collective-permute-start(bf16[1536,128]{1,0:T(8,128)(2,1)S(1)} %get-tuple-element.109), channel_id=1, source_target_pairs={{0,2},{1,3},{2,0},{3,1},{4,6},{5,7},{6,4},{7,5},{8,10},{9,11},{10,... | collective-permute-start | bytes 1179656 | tf_op jit(solution)/shard_map/ppermute | solution.py:347

commit v2 on v1

--- a/solution.py
+++ b/solution.py
@@ -17,7 +17,15 @@
 META = 16
 F32 = jnp.float32
 BF16 = jnp.bfloat16
-VMEM_LIMIT = 34 * 1024 * 1024
+VMEM_LIMIT = 32 * 1024 * 1024
+EXPERT_LIMIT = 44 * 1024 * 1024
+COST = {
+    "expert0_first": 20,
+    "expert0_rest": 20,
+    "expert1": 20,
+    "expert2_first": 20,
+    "expert2_rest": 10,
+}
 VMEM = pl.BlockSpec(memory_space=pltpu.VMEM)
 SMEM = pl.BlockSpec(memory_space=pltpu.SMEM)
 
@@ -30,14 +38,14 @@
     return jax.ShapeDtypeStruct(shape, BF16)
 
 
-def call(kernel, name, in_specs, out_shape, args, nbytes=10**6, scratch=()):
+def call(kernel, name, in_specs, out_shape, args, nbytes=10**6, scratch=(), limit=VMEM_LIMIT):
     return pl.pallas_call(
         kernel,
         in_specs=in_specs,
         out_specs=jax.tree.map(lambda _: VMEM, out_shape),
         out_shape=out_shape,
         scratch_shapes=list(scratch),
-        compiler_params=pltpu.CompilerParams(vmem_limit_bytes=VMEM_LIMIT),
+        compiler_params=pltpu.CompilerParams(vmem_limit_bytes=limit),
         cost_estimate=pl.CostEstimate(flops=0, bytes_accessed=nbytes, transcendentals=0),
         name=name,
     )(*args)
@@ -175,72 +183,66 @@
     ig_s[...] += dot(grad_gate, wg, 1, 1) + dot(grad_up, wu, 1, 1)
 
 
-def load_rows(own_ref, oth_ref, x_s, g_s, xt_s, gt_s):
-    for k, ref in enumerate((own_ref, oth_ref)):
-        x_s[k * ROWS : (k + 1) * ROWS, :] = ref[:, 0].reshape(ROWS, D)
-        g_s[k * ROWS : (k + 1) * ROWS, :] = ref[:, 1].reshape(ROWS, D)
-    xt_s[...] = x_s[...].T
-    gt_s[...] = g_s[...].T
-
-
-def first_kernel(n_after, tbl_ref, own_ref, oth_ref, *refs):
-    weights, (far, eo_ref, ig_ref, x_s, g_s, xt_s, gt_s) = refs[:6], refs[6 + n_after :]
-    load_rows(own_ref, oth_ref, x_s, g_s, xt_s, gt_s)
-    eo_ref[...] = jnp.zeros_like(eo_ref)
-    ig_ref[...] = jnp.zeros_like(ig_ref)
-    share(x_s, g_s, xt_s, gt_s, eo_ref, ig_ref, weights, [(far.at[0], far.at[1])])
-
-
-def rest_kernel(n_after, tbl_ref, own_ref, oth_ref, *refs):
-    weights, eo_ref, ig_ref = refs[:6], refs[6], refs[7]
-    mid, near, home0, home1, ret_own, ret_oth, x_s, g_s, xt_s, gt_s, eo_s, ig_s = refs[8 + n_after :]
+def expert_kernel(has_sums, ends, n_after, counts, tbl_ref, own_ref, oth_ref, *refs):
+    weights, refs = refs[:6], refs[6:]
+    if has_sums:
+        sums, refs = refs[:2], refs[2:]
+    refs = refs[n_after:]
+    chunks, refs = refs[: len(counts)], refs[len(counts) :]
+    results, (x_s, g_s, xt_s, gt_s, *acc) = refs[:2], refs[2:]
+    eo_s, ig_s = acc if ends else results
     i = pl.program_id(0)
+    flat = [ref.at[n] for ref, count in zip(chunks, counts) for n in range(count)]
+    steps = len(flat) // 2
 
     @pl.when(i == 0)
     def _():
-        load_rows(own_ref, oth_ref, x_s, g_s, xt_s, gt_s)
-        eo_s[...] = eo_ref[...]
-        ig_s[...] = ig_ref[...]
-
-    homes = [(mid.at[0], mid.at[1]), (near.at[0], near.at[1]), (home0, home1)]
+        for k, ref in enumerate((own_ref, oth_ref)):
+            x_s[k * ROWS : (k + 1) * ROWS, :] = ref[:, 0].reshape(ROWS, D)
+            g_s[k * ROWS : (k + 1) * ROWS, :] = ref[:, 1].reshape(ROWS, D)
+        xt_s[...] = x_s[...].T
+        gt_s[...] = g_s[...].T
+        eo_s[...] = sums[0][...] if has_sums else jnp.zeros_like(eo_s)
+        ig_s[...] = sums[1][...] if has_sums else jnp.zeros_like(ig_s)
+
+    homes = [flat[2 * n : 2 * n + 2] for n in range(steps)]
     share(x_s, g_s, xt_s, gt_s, eo_s, ig_s, weights, homes)
-
-    @pl.when(i == 2)
-    def _():
-        for k, ref in enumerate((ret_own, ret_oth)):
-            ref[0] = eo_s[k * ROWS : (k + 1) * ROWS, :].astype(BF16)
-            ref[1] = ig_s[k * ROWS : (k + 1) * ROWS, :].astype(BF16)
-
-
-def expert(j, at, tbl, own, oth, weights, sums=None, after=()):
+    if ends:
+
+        @pl.when(i == steps - 1)
+        def _():
+            for k, ref in enumerate(results):
+                ref[0] = eo_s[k * ROWS : (k + 1) * ROWS, :].astype(BF16)
+                ref[1] = ig_s[k * ROWS : (k + 1) * ROWS, :].astype(BF16)
+
+
+def expert(name, j, at, tbl, base, counts, ends, own, oth, weights, sums=(), after=()):
     rows = 2 * ROWS
-    steps = (0,) if sums is None else (1, 2, 3)
+    steps = sum(counts) // 2
 
     def fixed(shape):
         return pl.BlockSpec(shape, lambda i, tbl: (0,) * len(shape))
 
     def columns(k):
-        return pl.BlockSpec((None, D, BLK), lambda i, tbl: (j, 0, tbl[2 * (i + steps[0]) + k]))
+        return pl.BlockSpec((None, D, BLK), lambda i, tbl: (j, 0, tbl[base + 2 * i + k]))
 
     def lines(k):
-        return pl.BlockSpec((None, BLK, D), lambda i, tbl: (j, tbl[2 * (i + steps[0]) + k], 0))
+        return pl.BlockSpec((None, BLK, D), lambda i, tbl: (j, tbl[base + 2 * i + k], 0))
 
     joined = pl.BlockSpec((None, SOURCES, 2, CAP, D), lambda i, tbl: (at, 0, 0, 0, 0))
-    chunk, ret, sum_like = (3 * D, BLK), (2, ROWS, D), jax.ShapeDtypeStruct((rows, D), F32)
+    out = [bf16_like(count, 3 * D, BLK) for count in counts]
     scratch = [pltpu.VMEM((rows, D), BF16)] * 2 + [pltpu.VMEM((D, rows), BF16)] * 2
-    if sums is None:
-        kernel, name, sums = first_kernel, f"expert{j}_first", ()
-        out = [bf16_like(2, *chunk), sum_like, sum_like]
+    if ends:
+        out += [bf16_like(2, ROWS, D)] * 2
+        scratch += [pltpu.VMEM((rows, D), F32)] * 2
     else:
-        kernel, name = rest_kernel, f"expert{j}_rest"
-        out = [bf16_like(*s) for s in ((2,) + chunk, (2,) + chunk, chunk, chunk, ret, ret)]
-        scratch = scratch + [pltpu.VMEM((rows, D), F32)] * 2
+        out += [jax.ShapeDtypeStruct((rows, D), F32)] * 2
     w_gate, w_up, w_down = weights
     return pl.pallas_call(
-        functools.partial(kernel, len(after)),
+        functools.partial(expert_kernel, bool(sums), ends, len(after), counts),
         grid_spec=pltpu.PrefetchScalarGridSpec(
             num_scalar_prefetch=1,
-            grid=(len(steps),),
+            grid=(steps,),
             in_specs=[joined, joined]
             + [columns(0), columns(1), columns(0), columns(1), lines(0), lines(1)]
             + [fixed((rows, D))] * len(sums)
@@ -250,17 +252,17 @@
         ),
         out_shape=out,
         compiler_params=pltpu.CompilerParams(
-            dimension_semantics=("arbitrary",), vmem_limit_bytes=VMEM_LIMIT
+            dimension_semantics=("arbitrary",), vmem_limit_bytes=EXPERT_LIMIT
         ),
         cost_estimate=pl.CostEstimate(
-            flops=len(steps) * 18 * rows * D * 256, bytes_accessed=10**6, transcendentals=0
+            flops=COST[name] * 10**9, bytes_accessed=10**6, transcendentals=0
         ),
         name=name,
     )(tbl, own, oth, w_gate, w_gate, w_up, w_up, w_down, w_down, *sums, *after)
 
 
-def back_kernel(count, *refs):
-    ins, outs = refs[: 2 * count], refs[2 * count :]
+def back_kernel(count, n_after, *refs):
+    ins, outs = refs[: 2 * count], refs[2 * count + n_after :]
     for j in range(count):
         own_ref, oth_ref = ins[2 * j : 2 * j + 2]
         for n in range(SOURCES):
@@ -270,12 +272,12 @@
                 outs[n & 3][j, n >> 2, k] = total.astype(BF16)
 
 
-def back(name, pairs):
+def back(name, pairs, after=()):
     count = len(pairs) // 2
     out = [bf16_like(count, 2, 2, CAP, D)] * 4
-    return call(
-        functools.partial(back_kernel, count), name, [VMEM] * len(pairs), out, pairs, 3 * 10**6
-    )
+    specs = [VMEM] * len(pairs) + [pl.BlockSpec(memory_space=pl.ANY)] * len(after)
+    kernel = functools.partial(back_kernel, count, len(after))
+    return call(kernel, name, specs, out, (*pairs, *after), 10**6)
 
 
 def token_sums(side, me_ref, packed_ref, rows, out_s, in_s):
@@ -339,15 +341,18 @@
     me = lax.axis_index("expert").astype(jnp.int32).reshape(1)
     rep = lax.axis_index("replica").astype(jnp.int32)
     y, x, core = rep >> 2, (rep >> 1) & 1, rep & 1
-    step = jnp.arange(8, dtype=jnp.int32)
-    away = (3 - (step >> 1)) * (1 - 2 * core)
-    tbl = ((y + away) & 3) * 4 + (x ^ (step & 1)) * 2 + core
-
-    def over_replica(value, perm):
-        return lax.ppermute(value, "replica", perm)
-
-    def to_z(value, dz):
-        return lax.ppermute(value, "expert", along_z(dz))
+    step = jnp.arange(16, dtype=jnp.int32)
+    hop = jnp.where(step < 8, step >> 1, step & 3)
+    flip = jnp.where(step < 8, step & 1, (step < 12).astype(jnp.int32))
+    tbl = ((y + (3 - hop) * (1 - 2 * core)) & 3) * 4 + (x ^ flip) * 2 + core
+
+    def over_replica(label, value, perm):
+        with jax.named_scope(label):
+            return lax.ppermute(value, "replica", perm)
+
+    def to_z(label, value, dz):
+        with jax.named_scope(label):
+            return lax.ppermute(value, "expert", along_z(dz))
 
     packed = call(
         pack_kernel,
@@ -360,57 +365,81 @@
             pltpu.VMEM((2, TOK), F32),
             pltpu.SemaphoreType.DMA((4,)),
         ],
-    )
-    partner = lax.ppermute(packed, "expert", PARTNER)
+        limit=63 * 1024 * 1024,
+    )
+    with jax.named_scope("packed"):
+        partner = lax.ppermute(packed, "expert", PARTNER)
     sent = dispatch("own_slots", False, me, packed)
-    from_own = [sent[0]] + [to_z(sent[dz], dz) for dz in range(1, 4)]
+    from_own = [sent[0]] + [to_z("own_rows", sent[dz], dz) for dz in range(1, 4)]
     sent = dispatch("partner_slots", True, me, partner)
-    firsts = [sent[0]] + [to_z(sent[dz], dz) for dz in range(1, 4)]
-    rests = [sent[4]] + [to_z(sent[4 + dz], dz) for dz in range(1, 4)]
+    firsts = [sent[0]] + [to_z("partner_rows0", sent[dz], dz) for dz in range(1, 4)]
+    rests = [sent[4]] + [to_z("partner_rows12", sent[4 + dz], dz) for dz in range(1, 4)]
 
     weights = (w_gate, w_up, w_down)
     own0 = join("join0", 1, from_own + firsts, ())
-    oth0 = over_replica(own0, CORE)
-    far0, eo, ig = expert(0, 0, tbl, own0, oth0, weights)
+    oth0 = over_replica("core_rows0", own0, CORE)
+    far0, *sums = expert("expert0_first", 0, 0, tbl, 0, (2,), False, own0, oth0, weights)
+    second0 = over_replica("ring0_1", far0, RING)
     own12 = join("join12", 2, from_own + rests, (far0,))
-    oth12 = over_replica(own12, CORE)
-    second0 = over_replica(far0, RING)
-    mid0, near0, *kept0 = expert(0, 0, tbl, own0, oth0, weights, (eo, ig), (own12,))
+    oth12 = over_replica("core_rows12", own12, CORE)
+    mid0, near0, home0, ret0, swap0 = expert(
+        "expert0_rest", 0, 0, tbl, 2, (2, 2, 2), True, own0, oth0, weights, sums, (own12,)
+    )
+    mid0, swap0, second0 = lax.optimization_barrier((mid0, swap0, second0))
     second0 = add(mid0, second0)
-    third0 = over_replica(second0, RING)
-    far1, eo, ig = expert(1, 0, tbl, own12, oth12, weights, None, (second0,))
-    second1 = over_replica(far1, RING)
-    mid1, near1, *kept1 = expert(1, 0, tbl, own12, oth12, weights, (eo, ig))
+    third0 = over_replica("ring0_2", second0, RING)
+    swap0 = over_replica("core_back0", swap0, CORE)
+    cross1a, cross1b, all1, ret1, swap1 = expert(
+        "expert1", 1, 0, tbl, 8, (2, 2, 4), True, own12, oth12, weights, (), (second0,)
+    )
+    cross1a, swap1, third0 = lax.optimization_barrier((cross1a, swap1, third0))
     third0 = add(near0, third0)
-    home0 = over_replica(third0, RING)
-    second1 = add(mid1, second1)
-    third1 = over_replica(second1, RING)
-    far2, eo, ig = expert(2, 1, tbl, own12, oth12, weights, None, (third0, second1))
-    second2 = over_replica(far2, RING)
-    mid2, near2, *kept2 = expert(2, 1, tbl, own12, oth12, weights, (eo, ig))
+    last0 = over_replica("ring0_3", third0, RING)
+    crossed1a = over_replica("cross1a", cross1a, ACROSS)
+    swap1 = over_replica("core_back1", swap1, CORE)
+    far2, *sums = expert(
+        "expert2_first", 2, 1, tbl, 0, (2,), False, own12, oth12, weights, (), (third0, ret1)
+    )
+    second2 = over_replica("ring2_1", far2, RING)
+    back01 = back("back01", (ret0, swap0, ret1, swap1), (far2,))
+    mid2, near2, home2, ret2, swap2 = expert(
+        "expert2_rest", 2, 1, tbl, 2, (2, 2, 2), True, own12, oth12, weights, sums, (back01[0],)
+    )
+    mid2, swap2, second2, last0, crossed1a = lax.optimization_barrier(
+        (mid2, swap2, second2, last0, crossed1a)
+    )
+    ring1 = over_replica("ring1_1", add(all1[0], crossed1a[0]), RING)
+    crossed1b = over_replica("cross1b", cross1b, ACROSS)
     second2 = add(mid2, second2)
-    third2 = over_replica(second2, RING)
-    home1 = over_replica(add(near1, third1), RING)
-    home2 = over_replica(add(near2, third2), RING)
-
-    parts, pairs = [], []
-    for home, (mine, theirs, ret_own, ret_oth) in ((home0, kept0), (home1, kept1), (home2, kept2)):
-        across = over_replica(add(theirs, home[1]), ACROSS)
-        parts += [add(mine, home[0]), across]
-        pairs += [ret_own, over_replica(ret_oth, CORE)]
-
-    rows = []
-    for name, some in (("back01", pairs[:4]), ("back2", pairs[4:])):
-        sums = back(name, some)
-        rows += [sums[0]] + [to_z(sums[dz], 4 - dz) for dz in range(1, 4)]
+    third2 = over_replica("ring2_2", second2, RING)
+    across0 = add(home0[1], last0[1])
+    across0_out = over_replica("across0", across0, ACROSS)
+    swap2 = over_replica("core_back2", swap2, CORE)
+    rows = [back01[0]] + [to_z("rows_back01", back01[dz], 4 - dz) for dz in range(1, 4)]
+    back2 = back("back2", (ret2, swap2), (second2, across0, *rows[1:]))
+    third2, ring1, local2 = lax.optimization_barrier((third2, ring1, back2[0]))
+    ring1 = over_replica("ring1_2", add(all1[1], crossed1a[1], ring1), RING)
+    third2 = add(near2, third2)
+    last2 = over_replica("ring2_3", third2, RING)
+    rows += [local2] + [to_z("rows_back2", back2[dz], 4 - dz) for dz in range(1, 4)]
+    crossed1b, ring1, across0_out, last2, *rows = lax.optimization_barrier(
+        (crossed1b, ring1, across0_out, last2, *rows)
+    )
+    ring1 = over_replica("ring1_3", add(all1[2], crossed1b[0], ring1), RING)
+    across2 = over_replica("across2", add(home2[1], last2[1]), ACROSS)
     scratch = [pltpu.VMEM((4 * LOCAL * CAP, D), BF16)] * 2
     theirs = call(
         partner_kernel, "partner_sums", [SMEM] + [VMEM] * 9, bf16_like(2, TOK, D),
         (me, partner, *rows), 3 * 10**6, scratch,
     )
+    parts = [add(home0[0], last0[0]), across0_out]
+    parts += [add(all1[3], crossed1b[1]), ring1]
+    parts += [add(home2[0], last2[0]), across2]
+    with jax.named_scope("partner_out"):
+        others = lax.ppermute(theirs, "expert", PARTNER)
     mixed, token_grad = call(
         combine_kernel, "combine", [SMEM] + [VMEM] * 10, [bf16_like(TOK, D)] * 2,
-        (me, packed, lax.ppermute(theirs, "expert", PARTNER), *rows), 3 * 10**6, scratch,
+        (me, packed, others, *rows), 3 * 10**6, scratch,
     )
     gate_grad, up_grad, down_grad = call(
         finish_kernel, "finish", [VMEM] * len(parts),

time: 171 us -> 168 us (0.982)
  local copies, waits for them, and re-layouts: 9.53 us -> 2.92 us
  starting transfers between devices: 45.5 us -> 48.5 us
    ppermute x15, waiting for transfers between devices: 9.15 us -> 23.9 us  [to_z(): return lax.ppermute(value, 'expert', along_z(dz))]
    ppermute x1, waiting for transfers between devices: 12.8 us -> 0.01 us  [local(): others = lax.ppermute(theirs, 'expert', PARTNER)]
    unnamed x36 -> x12, local copies, waits for them, and re-layouts: 9.53 us -> 2.92 us
    ppermute x15, starting transfers between devices: 25.3 us -> 27.1 us  [to_z(): return lax.ppermute(value, 'expert', along_z(dz))]
    pallas_call x10, Pallas kernels: 7.14 us -> 8.9 us  [call(): pl.pallas_call(kernel, in_specs=in_specs, out_specs=jax.tree.map(lambda _...]
    ppermute x17 -> x18, starting transfers between devices: 13.9 us -> 15.3 us  [over_replica(): return lax.ppermute(value, 'replica', perm)]
    pallas_call x6 -> x5, Pallas kernels: 45.9 us -> 44.6 us  [expert(): pl.pallas_call(functools.partial(expert_kernel, bool(sums), ends, len(aft...]
    ppermute x17 -> x18, waiting for transfers between devices: 31.1 us -> 30.8 us  [over_replica(): return lax.ppermute(value, 'replica', perm)]
  transfers between devices with their start and end apart: 34 -> 35, of which waited for: 16 -> 14; matrix products, arithmetic and copies ran while one was open for 1% -> 1% of each run, Pallas kernels for 28% -> 30%
where the time goes in v2:
time: 168 us; the launch traced here: 166 us
  waiting for transfers between devices  58.8 us (35%)
  Pallas kernels  53.5 us (32%)
  starting transfers between devices  48.5 us (29%)
  local copies, waits for them, and re-layouts  2.92 us (2%)
  other arithmetic  1.77 us (1%)
    pallas_call x5, Pallas kernels, expert(): pl.pallas_call(functools.partial(expert_kernel, bool(sums), ends, len(aft...  44.6 us
    ppermute x18, waiting for transfers between devices, over_replica(): return lax.ppermute(value, 'replica', perm)  30.8 us
    ppermute x15, starting transfers between devices, to_z(): return lax.ppermute(value, 'expert', along_z(dz))  27.1 us
    ppermute x15, waiting for transfers between devices, to_z(): return lax.ppermute(value, 'expert', along_z(dz))  23.9 us
    ppermute x18, starting transfers between devices, over_replica(): return lax.ppermute(value, 'replica', perm)  15.3 us
    pallas_call x10, Pallas kernels, call(): pl.pallas_call(kernel, in_specs=in_specs, out_specs=jax.tree.map(lambda _...  8.9 us
    ppermute x1, waiting for transfers between devices, local(): partner = lax.ppermute(packed, 'expert', PARTNER)  4.11 us
  transfers between devices with their start and end apart: 35, of which 14 were waited for; matrix products, arithmetic and copies ran while one was open for 1% of the time, Pallas kernels for 30%

profile of v2, /device:TPU:0, one launch (start us, length us, event | category | flops | bytes accessed | tf_op | source)
XLA Modules:
  0.0 166.4 jit_solution(11773524075342345077)
XLA Ops:
  0.6 1.9 %pack.1.packed_ref = bf16[528,512]{1,0:T(8,128)(2,1)} custom-call(bf16[256,512]{1,0:T(8,128)(2,1)} %tokens_ref.1, bf16[256,512]{1,0:T(8,128)(2,1)} %cot_ref.1, s32[2,256]{1,0:T(2,128)} %bitcast.23, f32[2,256]{1,0:T(2,128)} %bitcast.24), custom_call_target="tpu_custom_call" | custom-call | bytes 1000000 | tf_op jit(solution)/shard_map/pack/pallas_call | solution.py:42
  2.5 3.2 %collective-permute-start = (bf16[528,512]{1,0:T(8,128)(2,1)}, bf16[528,512]{1,0:T(8,128)(2,1)S(1)}, u32[]{:S(2)}, u32[]{:S(2)}) collective-permute-start(bf16[528,512]{1,0:T(8,128)(2,1)} %pack.1.packed_ref), channel_id=1, source_target_pairs={{0,16},{16,0},{32,48},{48,32},{64,80},{80,64},{96,112},{112,96},{1... | collective-permute-start | bytes 1622024 | tf_op jit(solution)/shard_map/packed/ppermute | solution.py:371
  5.7 1.1 copy-done
  6.8 0.7 own_slots.1
  7.5 2.0 %collective-permute-start.1 = (bf16[3,2,48,512]{3,2,1,0:T(8,128)(2,1)S(1)}, bf16[3,2,48,512]{3,2,1,0:T(8,128)(2,1)S(1)}, u32[]{:S(2)}, u32[]{:S(2)}) collective-permute-start(bf16[3,2,48,512]{3,2,1,0:T(8,128)(2,1)S(1)} %get-tuple-element.78), channel_id=1, source_target_pairs={{0,32},{16,48},{32,64},{48,80},{64,96},{80,112},{96,0},{112,16},{1... | collective-permute-start | bytes 884744 | tf_op jit(solution)/shard_map/own_rows/ppermute | solution.py:355
  9.5 3.6 %collective-permute-start.2 = (bf16[3,2,48,512]{3,2,1,0:T(8,128)(2,1)S(1)}, bf16[3,2,48,512]{3,2,1,0:T(8,128)(2,1)S(1)}, u32[]{:S(2)}, u32[]{:S(2)}) collective-permute-start(bf16[3,2,48,512]{3,2,1,0:T(8,128)(2,1)S(1)} %get-tuple-element.79), channel_id=1, source_target_pairs={{0,64},{16,80},{32,96},{48,112},{64,0},{80,16},{96,32},{112,48},{1... | collective-permute-start | bytes 884744 | tf_op jit(solution)/shard_map/own_rows/ppermute | solution.py:355
  13.1 1.0 collective-permute-start.3
  14.1 4.1 %collective-permute-done.packed_ref = bf16[528,512]{1,0:T(8,128)(2,1)S(1)} collective-permute-done((bf16[528,512]{1,0:T(8,128)(2,1)}, bf16[528,512]{1,0:T(8,128)(2,1)S(1)}, u32[]{:S(2)}, u32[]{:S(2)}) %collective-permute-start) | collective-permute-done | bytes 540704 | tf_op jit(solution)/shard_map/packed/ppermute | solution.py:371
  18.2 0.7 partner_slots.1
  18.9 0.7 copy-done.5
  19.6 2.1 %collective-permute-start.7 = (bf16[1,2,48,512]{3,2,1,0:T(8,128)(2,1)S(1)}, bf16[1,2,48,512]{3,2,1,0:T(8,128)(2,1)S(1)}, u32[]{:S(2)}, u32[]{:S(2)}) collective-permute-start(bf16[1,2,48,512]{3,2,1,0:T(8,128)(2,1)S(1)} %get-tuple-element.86), channel_id=1, source_target_pairs={{0,32},{16,48},{32,64},{48,80},{64,96},{80,112},{96,0},{112,16},{1... | collective-permute-start | bytes 294920 | tf_op jit(solution)/shard_map/partner_rows0/ppermute | solution.py:355
  21.7 3.6 %collective-permute-start.8 = (bf16[1,2,48,512]{3,2,1,0:T(8,128)(2,1)S(1)}, bf16[1,2,48,512]{3,2,1,0:T(8,128)(2,1)S(1)}, u32[]{:S(2)}, u32[]{:S(2)}) collective-permute-start(bf16[1,2,48,512]{3,2,1,0:T(8,128)(2,1)S(1)} %get-tuple-element.87), channel_id=1, source_target_pairs={{0,64},{16,80},{32,96},{48,112},{64,0},{80,16},{96,32},{112,48},{1... | collective-permute-start | bytes 294920 | tf_op jit(solution)/shard_map/partner_rows0/ppermute | solution.py:355
  25.3 1.0 collective-permute-start.9
  26.3 0.4 collective-permute-done.2.refs_2_
  26.8 2.2 %collective-permute-done.7.refs_5_ = bf16[1,2,48,512]{3,2,1,0:T(8,128)(2,1)S(1)} collective-permute-done((bf16[1,2,48,512]{3,2,1,0:T(8,128)(2,1)S(1)}, bf16[1,2,48,512]{3,2,1,0:T(8,128)(2,1)S(1)}, u32[]{:S(2)}, u32[]{:S(2)}) %collective-permute-start.7) | collective-permute-done | bytes 98336 | tf_op jit(solution)/shard_map/partner_rows0/ppermute | solution.py:355
  29.0 1.1 collective-permute-done.8.refs_6_
  30.2 1.3 collective-permute-start.4
  31.5 2.4 %collective-permute-start.5 = (bf16[2,2,48,512]{3,2,1,0:T(8,128)(2,1)}, bf16[2,2,48,512]{3,2,1,0:T(8,128)(2,1)S(1)}, u32[]{:S(2)}, u32[]{:S(2)}) collective-permute-start(bf16[2,2,48,512]{3,2,1,0:T(8,128)(2,1)} %copy-done.4), channel_id=1, source_target_pairs={{0,64},{16,80},{32,96},{48,112},{64,0},{80,16},{96,32},{112,48},{1... | collective-permute-start | bytes 589832 | tf_op jit(solution)/shard_map/partner_rows12/ppermute | solution.py:355
  33.9 1.3 collective-permute-start.6
  35.2 4.2 %expert0_first.1 = (bf16[2,1536,128]{2,1,0:T(8,128)(2,1)S(1)}, f32[768,512]{1,0:T(8,128)S(1)}, f32[768,512]{1,0:T(8,128)S(1)}) custom-call(s32[16]{0:T(128)S(1)} %fusion.14.tbl_ref, bf16[1,8,2,48,512]{4,3,2,1,0:T(8,128)(2,1)S(1)} %join0.1.own_ref, bf16[1,8,2,48,512]{4,3,2,1,0:T(8,128)(2,1)S(1)} %collective-permute-done.10.oth_ref, ...), custom_call_target="tpu_custom_call" | custom-call | flops 20000000000 | bytes 1000000 | tf_op jit(solution)/shard_map/expert0_first/pallas_call | solution.py:241
  39.4 1.6 collective-permute-start.12
  41.1 2.6 %collective-permute-done.5.refs_6_ = bf16[2,2,48,512]{3,2,1,0:T(8,128)(2,1)S(1)} collective-permute-done((bf16[2,2,48,512]{3,2,1,0:T(8,128)(2,1)}, bf16[2,2,48,512]{3,2,1,0:T(8,128)(2,1)S(1)}, u32[]{:S(2)}, u32[]{:S(2)}) %collective-permute-start.5) | collective-permute-done | bytes 196640 | tf_op jit(solution)/shard_map/partner_rows12/ppermute | solution.py:355
  43.6 0.2 collective-permute-done.6.refs_7_
  44.1 10.9 %expert0_rest.1 = (bf16[2,1536,128]{2,1,0:T(8,128)(2,1)S(1)}, bf16[2,1536,128]{2,1,0:T(8,128)(2,1)S(1)}, bf16[2,1536,128]{2,1,0:T(8,128)(2,1)S(1)}, bf16[2,384,5...) custom-call(s32[16]{0:T(128)S(1)} %fusion.14.tbl_ref, bf16[1,8,2,48,512]{4,3,2,1,0:T(8,128)(2,1)S(1)} %join0.1.own_ref, ...), custom_call_target="tpu_custom_call" | custom-call | flops 20000000000 | bytes 1000000 | tf_op jit(solution)/shard_map/expert0_rest/pallas_call | solution.py:241
  55.0 0.2 add_convert_fusion.3.refs_6_
  55.2 1.6 collective-permute-start.14
  56.8 1.6 collective-permute-start.15
  58.5 13.7 %expert1.1 = (bf16[2,1536,128]{2,1,0:T(8,128)(2,1)S(1)}, bf16[2,1536,128]{2,1,0:T(8,128)(2,1)S(1)}, bf16[4,1536,128]{2,1,0:T(8,128)(2,1)S(1)}, bf16[2,384,512]{2,1,0:T(8,128)(2,1)S(1)}, bf16[2,384,512]{2,1,0:T(8,128)(2,1)S(1)}) custom-call(s32[16]{0:T(128)S(1)} %fusion.14.tbl_ref, bf16[2,8,2,48,512]{4,3,2,1,0:T(8,128)(2,1)S(1)} %join12.1.refs_8_.own_ref, ...), custom_call_target="tpu_custom_call" | custom-call | flops 20000000000 | bytes 1000000 | tf_op jit(solution)/shard_map/expert1/pallas_call | solution.py:241
  72.2 0.2 add_convert_fusion.2.refs_6_
  72.5 0.5 collective-permute-start.16
  73.0 1.4 collective-permute-start.19
  74.3 4.3 %expert2_first.1 = (bf16[2,1536,128]{2,1,0:T(8,128)(2,1)S(1)}, f32[768,512]{1,0:T(8,128)S(1)}, f32[768,512]{1,0:T(8,128)S(1)}) custom-call(s32[16]{0:T(128)S(1)} %fusion.14.tbl_ref, bf16[2,8,2,48,512]{4,3,2,1,0:T(8,128)(2,1)S(1)} %join12.1.refs_8_.own_ref, bf16[2,8,2,48,512]{4,3,2,1,0:T(8,128)(2,1)S(1)} %collective-permute-done.11.oth_ref, ...), custom_call_target="tpu_custom_call" | custom-call | flops 20000000000 | bytes 1000000 | tf_op jit(solution)/shard_map/expert2_first/pallas_call | solution.py:241
  78.6 1.2 copy-done.2
  79.8 1.3 collective-permute-start.17
  81.1 0.4 back01.1
  81.4 2.7 %collective-permute-start.23 = (bf16[2,2,2,48,512]{4,3,2,1,0:T(8,128)(2,1)S(1)}, bf16[2,2,2,48,512]{4,3,2,1,0:T(8,128)(2,1)S(1)}, u32[]{:S(2)}, u32[]{:S(2)}) collective-permute-start(bf16[2,2,2,48,512]{4,3,2,1,0:T(8,128)(2,1)S(1)} %get-tuple-element.120), channel_id=1, source_target_pairs={{0,96},{16,112},{32,0},{48,16},{64,32},{80,48},{96,64},{112,80},{1... | collective-permute-start | bytes 1179656 | tf_op jit(solution)/shard_map/rows_back01/ppermute | solution.py:355
  84.1 0.3 collective-permute-start.24
  84.5 11.5 %expert2_rest.1 = (bf16[2,1536,128]{2,1,0:T(8,128)(2,1)S(1)}, bf16[2,1536,128]{2,1,0:T(8,128)(2,1)S(1)}, bf16[2,1536,128]{2,1,0:T(8,128)(2,1)S(1)}, bf16[2,384,5...) custom-call(s32[16]{0:T(128)S(1)} %fusion.14.tbl_ref, bf16[2,8,2,48,512]{4,3,2,1,0:T(8,128)(2,1)S(1)} %join12.1.refs_8_.own_ref, ...), custom_call_target="tpu_custom_call" | custom-call | flops 10000000000 | bytes 1000000 | tf_op jit(solution)/shard_map/expert2_rest/pallas_call | solution.py:241
  96.0 0.7 collective-permute-start.25
  96.7 0.2 add_convert_fusion.1.refs_2_
  97.0 0.5 collective-permute-start.20
  97.5 0.5 collective-permute-start.22
  98.1 3.5 %collective-permute-done.23.refs_4_.refs_1_ = bf16[2,2,2,48,512]{4,3,2,1,0:T(8,128)(2,1)S(1)} collective-permute-done((bf16[2,2,2,48,512]{4,3,2,1,0:T(8,128)(2,1)S(1)}, bf16[2,2,2,48,512]{4,3,2,1,0:T(8,128)(2,1)S(1)}, u32[]{:S(2)}, u32[]{:S(2)}) %collective-permute-start.23) | collective-permute-done | bytes 393248 | tf_op jit(solution)/shard_map/rows_back01/ppermute | solution.py:355
  101.6 0.2 fusion.4
  101.8 0.7 collective-permute-start.13
  102.5 6.7 %collective-permute-done.25.refs_6_.refs_3_ = bf16[2,2,2,48,512]{4,3,2,1,0:T(8,128)(2,1)S(1)} collective-permute-done((bf16[2,2,2,48,512]{4,3,2,1,0:T(8,128)(2,1)S(1)}, bf16[2,2,2,48,512]{4,3,2,1,0:T(8,128)(2,1)S(1)}, u32[]{:S(2)}, u32[]{:S(2)}) %collective-permute-start.25) | collective-permute-done | bytes 393248 | tf_op jit(solution)/shard_map/rows_back01/ppermute | solution.py:355
  109.2 1.3 collective-permute-start.27
  110.8 3.7 %collective-permute-done.21 = bf16[1536,128]{1,0:T(8,128)(2,1)S(1)} collective-permute-done((bf16[1536,128]{1,0:T(8,128)(2,1)S(1)}, bf16[1536,128]{1,0:T(8,128)(2,1)S(1)}, u32[]{:S(2)}, u32[]{:S(2)}) %collective-permute-start.21) | collective-permute-done | bytes 393248 | tf_op jit(solution)/shard_map/ring1_1/ppermute | solution.py:351
  114.4 0.2 add_convert_fusion
  114.9 1.7 %collective-permute-start.26 = (bf16[1536,128]{1,0:T(8,128)(2,1)S(1)}, bf16[1536,128]{1,0:T(8,128)(2,1)S(1)}, u32[]{:S(2)}, u32[]{:S(2)}) collective-permute-start(bf16[1536,128]{1,0:T(8,128)(2,1)S(1)} %fusion.1), channel_id=1, source_target_pairs={{0,4},{1,13},{2,6},{3,15},{4,8},{5,1},{6,10},{7,3},{8,12},{9,5},{1... | collective-permute-start | bytes 1179656 | tf_op jit(solution)/shard_map/ring1_2/ppermute | solution.py:351
  116.6 2.6 %collective-permute-start.29 = (bf16[1,2,2,48,512]{4,3,2,1,0:T(8,128)(2,1)S(1)}, bf16[1,2,2,48,512]{4,3,2,1,0:T(8,128)(2,1)S(1)}, u32[]{:S(2)}, u32[]{:S(2)}) collective-permute-start(bf16[1,2,2,48,512]{4,3,2,1,0:T(8,128)(2,1)S(1)} %get-tuple-element.128), channel_id=1, source_target_pairs={{0,96},{16,112},{32,0},{48,16},{64,32},{80,48},{96,64},{112,80},{1... | collective-permute-start | bytes 589832 | tf_op jit(solution)/shard_map/rows_back2/ppermute | solution.py:355
  119.3 3.0 %collective-permute-done.13 = bf16[2,1536,128]{2,1,0:T(8,128)(2,1)S(1)} collective-permute-done((bf16[2,1536,128]{2,1,0:T(8,128)(2,1)S(1)}, bf16[2,1536,128]{2,1,0:T(8,128)(2,1)S(1)}, u32[]{:S(2)}, u32[]{:S(2)}) %collective-permute-start.13) | collective-permute-done | bytes 786464 | tf_op jit(solution)/shard_map/cross1b/ppermute | solution.py:351
  122.3 1.3 collective-permute-start.30
  123.6 6.8 %collective-permute-done.27.refs_1_ = bf16[1536,128]{1,0:T(8,128)(2,1)S(1)} collective-permute-done((bf16[1536,128]{1,0:T(8,128)(2,1)S(1)}, bf16[1536,128]{1,0:T(8,128)(2,1)S(1)}, u32[]{:S(2)}, u32[]{:S(2)}) %collective-permute-start.27) | collective-permute-done | bytes 393248 | tf_op jit(solution)/shard_map/across0/ppermute | solution.py:351
  130.4 1.2 collective-permute-start.31
  131.6 7.2 %collective-permute-done.31.refs_7_ = bf16[1,2,2,48,512]{4,3,2,1,0:T(8,128)(2,1)S(1)} collective-permute-done((bf16[1,2,2,48,512]{4,3,2,1,0:T(8,128)(2,1)S(1)}, bf16[1,2,2,48,512]{4,3,2,1,0:T(8,128)(2,1)S(1)}, u32[]{:S(2)}, u32[]{:S(2)}) %collective-permute-start.31) | collective-permute-done | bytes 196640 | tf_op jit(solution)/shard_map/rows_back2/ppermute | solution.py:355
  139.0 1.8 %collective-permute-start.33 = (bf16[1536,128]{1,0:T(8,128)(2,1)S(1)}, bf16[1536,128]{1,0:T(8,128)(2,1)S(1)}, u32[]{:S(2)}, u32[]{:S(2)}) collective-permute-start(bf16[1536,128]{1,0:T(8,128)(2,1)S(1)} %fusion), channel_id=1, source_target_pairs={{0,4},{1,13},{2,6},{3,15},{4,8},{5,1},{6,10},{7,3},{8,12},{9,5},{1... | collective-permute-start | bytes 1179656 | tf_op jit(solution)/shard_map/ring1_3/ppermute | solution.py:351
  140.8 1.4 partner_sums.1
  142.3 2.8 %collective-permute-start.32 = (bf16[2,256,512]{2,1,0:T(8,128)(2,1)S(1)}, bf16[2,256,512]{2,1,0:T(8,128)(2,1)S(1)}, u32[]{:S(2)}, u32[]{:S(2)}) collective-permute-start(bf16[2,256,512]{2,1,0:T(8,128)(2,1)S(1)} %partner_sums.1), channel_id=1, source_target_pairs={{0,16},{16,0},{32,48},{48,32},{64,80},{80,64},{96,112},{112,96},{1... | collective-permute-start | bytes 1572872 | tf_op jit(solution)/shard_map/partner_out/ppermute | solution.py:439
  145.3 0.3 collective-permute-start.34
  145.7 2.4 %collective-permute-done.33.refs_3_ = bf16[1536,128]{1,0:T(8,128)(2,1)S(1)} collective-permute-done((bf16[1536,128]{1,0:T(8,128)(2,1)S(1)}, bf16[1536,128]{1,0:T(8,128)(2,1)S(1)}, u32[]{:S(2)}, u32[]{:S(2)}) %collective-permute-start.33) | collective-permute-done | bytes 393248 | tf_op jit(solution)/shard_map/ring1_3/ppermute | solution.py:351
  148.1 14.9 %collective-permute-done.34.refs_5_ = bf16[1536,128]{1,0:T(8,128)(2,1)S(1)} collective-permute-done((bf16[1536,128]{1,0:T(8,128)(2,1)S(1)}, bf16[1536,128]{1,0:T(8,128)(2,1)S(1)}, u32[]{:S(2)}, u32[]{:S(2)}) %collective-permute-start.34) | collective-permute-done | bytes 393248 | tf_op jit(solution)/shard_map/across2/ppermute | solution.py:351
  163.0 1.2 finish.1
  164.2 2.2 %combine.1 = (bf16[256,512]{1,0:T(8,128)(2,1)}, bf16[256,512]{1,0:T(8,128)(2,1)}) custom-call(s32[1]{0:T(128)} %bitcast.me_ref, bf16[528,512]{1,0:T(8,128)(2,1)S(1)} %copy-done.1, bf16[2,256,512]{2,1,0:T(8,128)(2,1)S(1)} %collective-permute-done.32.other_ref, bf16[2,2,2,48,512]{4,3,2,1,0:T(8,128)(2,1)S(1)} %get-tuple-element.131.refs_8_.refs_0_, ...), custom_call_target="tpu_custom_call" | custom-call | bytes 3000000 | tf_op jit(solution)/shard_map/combine/pallas_call | solution.py:42
  (44 shorter events, 1.5 us)
Async XLA Ops:
  2.5 15.7 %collective-permute-start = (bf16[528,512]{1,0:T(8,128)(2,1)}, bf16[528,512]{1,0:T(8,128)(2,1)S(1)}, u32[]{:S(2)}, u32[]{:S(2)}) collective-permute-start(bf16[528,512]{1,0:T(8,128)(2,1)} %pack.1.packed_ref), channel_id=1, source_target_pairs={{0,16},{16,0},{32,48},{48,32},{64,80},{80,64},{96,112},{112,96},{1... | collective-permute-start | bytes 1622024 | tf_op jit(solution)/shard_map/packed/ppermute | solution.py:371
  5.7 1.1 copy-start
  7.5 17.8 %collective-permute-start.1 = (bf16[3,2,48,512]{3,2,1,0:T(8,128)(2,1)S(1)}, bf16[3,2,48,512]{3,2,1,0:T(8,128)(2,1)S(1)}, u32[]{:S(2)}, u32[]{:S(2)}) collective-permute-start(bf16[3,2,48,512]{3,2,1,0:T(8,128)(2,1)S(1)} %get-tuple-element.78), channel_id=1, source_target_pairs={{0,32},{16,48},{32,64},{48,80},{64,96},{80,112},{96,0},{112,16},{1... | collective-permute-start | bytes 884744 | tf_op jit(solution)/shard_map/own_rows/ppermute | solution.py:355
  9.5 17.3 %collective-permute-start.2 = (bf16[3,2,48,512]{3,2,1,0:T(8,128)(2,1)S(1)}, bf16[3,2,48,512]{3,2,1,0:T(8,128)(2,1)S(1)}, u32[]{:S(2)}, u32[]{:S(2)}) collective-permute-start(bf16[3,2,48,512]{3,2,1,0:T(8,128)(2,1)S(1)} %get-tuple-element.79), channel_id=1, source_target_pairs={{0,64},{16,80},{32,96},{48,112},{64,0},{80,16},{96,32},{112,48},{1... | collective-permute-start | bytes 884744 | tf_op jit(solution)/shard_map/own_rows/ppermute | solution.py:355
  13.1 13.7 %collective-permute-start.3 = (bf16[3,2,48,512]{3,2,1,0:T(8,128)(2,1)S(1)}, bf16[3,2,48,512]{3,2,1,0:T(8,128)(2,1)S(1)}, u32[]{:S(2)}, u32[]{:S(2)}) collective-permute-start(bf16[3,2,48,512]{3,2,1,0:T(8,128)(2,1)S(1)} %get-tuple-element.80), channel_id=1, source_target_pairs={{0,96},{16,112},{32,0},{48,16},{64,32},{80,48},{96,64},{112,80},{1... | collective-permute-start | bytes 884744 | tf_op jit(solution)/shard_map/own_rows/ppermute | solution.py:355
  18.9 0.7 copy-start.5
  19.6 10.5 %copy-start.3 = (bf16[2,2,48,512]{3,2,1,0:T(8,128)(2,1)}, bf16[2,2,48,512]{3,2,1,0:T(8,128)(2,1)S(1)}, u32[]{:S(2)}) copy-start(bf16[2,2,48,512]{3,2,1,0:T(8,128)(2,1)S(1)} %get-tuple-element.84) | copy-start | bytes 589828
  19.6 10.5 %copy-start.4 = (bf16[2,2,48,512]{3,2,1,0:T(8,128)(2,1)}, bf16[2,2,48,512]{3,2,1,0:T(8,128)(2,1)S(1)}, u32[]{:S(2)}) copy-start(bf16[2,2,48,512]{3,2,1,0:T(8,128)(2,1)S(1)} %get-tuple-element.83) | copy-start | bytes 589828
  19.6 9.4 %collective-permute-start.7 = (bf16[1,2,48,512]{3,2,1,0:T(8,128)(2,1)S(1)}, bf16[1,2,48,512]{3,2,1,0:T(8,128)(2,1)S(1)}, u32[]{:S(2)}, u32[]{:S(2)}) collective-permute-start(bf16[1,2,48,512]{3,2,1,0:T(8,128)(2,1)S(1)} %get-tuple-element.86), channel_id=1, source_target_pairs={{0,32},{16,48},{32,64},{48,80},{64,96},{80,112},{96,0},{112,16},{1... | collective-permute-start | bytes 294920 | tf_op jit(solution)/shard_map/partner_rows0/ppermute | solution.py:355
  21.7 8.3 %collective-permute-start.8 = (bf16[1,2,48,512]{3,2,1,0:T(8,128)(2,1)S(1)}, bf16[1,2,48,512]{3,2,1,0:T(8,128)(2,1)S(1)}, u32[]{:S(2)}, u32[]{:S(2)}) collective-permute-start(bf16[1,2,48,512]{3,2,1,0:T(8,128)(2,1)S(1)} %get-tuple-element.87), channel_id=1, source_target_pairs={{0,64},{16,80},{32,96},{48,112},{64,0},{80,16},{96,32},{112,48},{1... | collective-permute-start | bytes 294920 | tf_op jit(solution)/shard_map/partner_rows0/ppermute | solution.py:355
  25.3 4.7 %collective-permute-start.9 = (bf16[1,2,48,512]{3,2,1,0:T(8,128)(2,1)S(1)}, bf16[1,2,48,512]{3,2,1,0:T(8,128)(2,1)S(1)}, u32[]{:S(2)}, u32[]{:S(2)}) collective-permute-start(bf16[1,2,48,512]{3,2,1,0:T(8,128)(2,1)S(1)} %get-tuple-element.88), channel_id=1, source_target_pairs={{0,96},{16,112},{32,0},{48,16},{64,32},{80,48},{96,64},{112,80},{1... | collective-permute-start | bytes 294920 | tf_op jit(solution)/shard_map/partner_rows0/ppermute | solution.py:355
  30.1 5.1 %collective-permute-start.10 = (bf16[1,8,2,48,512]{4,3,2,1,0:T(8,128)(2,1)S(1)}, bf16[1,8,2,48,512]{4,3,2,1,0:T(8,128)(2,1)S(1)}, u32[]{:S(2)}, u32[]{:S(2)}) collective-permute-start(bf16[1,8,2,48,512]{4,3,2,1,0:T(8,128)(2,1)S(1)} %join0.1.own_ref), channel_id=1, source_target_pairs={{0,1},{1,0},{2,3},{3,2},{4,5},{5,4},{6,7},{7,6},{8,9},{9,8},{10,11... | collective-permute-start | bytes 2359304 | tf_op jit(solution)/shard_map/core_rows0/ppermute | solution.py:351
  30.2 10.8 %collective-permute-start.4 = (bf16[2,2,48,512]{3,2,1,0:T(8,128)(2,1)}, bf16[2,2,48,512]{3,2,1,0:T(8,128)(2,1)S(1)}, u32[]{:S(2)}, u32[]{:S(2)}) collective-permute-start(bf16[2,2,48,512]{3,2,1,0:T(8,128)(2,1)} %copy-done.5), channel_id=1, source_target_pairs={{0,32},{16,48},{32,64},{48,80},{64,96},{80,112},{96,0},{112,16},{1... | collective-permute-start | bytes 589832 | tf_op jit(solution)/shard_map/partner_rows12/ppermute | solution.py:355
  31.5 12.1 %collective-permute-start.5 = (bf16[2,2,48,512]{3,2,1,0:T(8,128)(2,1)}, bf16[2,2,48,512]{3,2,1,0:T(8,128)(2,1)S(1)}, u32[]{:S(2)}, u32[]{:S(2)}) collective-permute-start(bf16[2,2,48,512]{3,2,1,0:T(8,128)(2,1)} %copy-done.4), channel_id=1, source_target_pairs={{0,64},{16,80},{32,96},{48,112},{64,0},{80,16},{96,32},{112,48},{1... | collective-permute-start | bytes 589832 | tf_op jit(solution)/shard_map/partner_rows12/ppermute | solution.py:355
  33.9 9.9 %collective-permute-start.6 = (bf16[2,2,48,512]{3,2,1,0:T(8,128)(2,1)}, bf16[2,2,48,512]{3,2,1,0:T(8,128)(2,1)S(1)}, u32[]{:S(2)}, u32[]{:S(2)}) collective-permute-start(bf16[2,2,48,512]{3,2,1,0:T(8,128)(2,1)} %copy-done.3), channel_id=1, source_target_pairs={{0,96},{16,112},{32,0},{48,16},{64,32},{80,48},{96,64},{112,80},{1... | collective-permute-start | bytes 589832 | tf_op jit(solution)/shard_map/partner_rows12/ppermute | solution.py:355
  39.4 15.6 %collective-permute-start.12 = (bf16[2,1536,128]{2,1,0:T(8,128)(2,1)S(1)}, bf16[2,1536,128]{2,1,0:T(8,128)(2,1)S(1)}, u32[]{:S(2)}, u32[]{:S(2)}) collective-permute-start(bf16[2,1536,128]{2,1,0:T(8,128)(2,1)S(1)} %get-tuple-element.89.refs_8_), channel_id=1, source_target_pairs={{0,4},{1,13},{2,6},{3,15},{4,8},{5,1},{6,10},{7,3},{8,12},{9,5},{1... | collective-permute-start | bytes 2359304 | tf_op jit(solution)/shard_map/ring0_1/ppermute | solution.py:351
  44.0 14.5 %collective-permute-start.11 = (bf16[2,8,2,48,512]{4,3,2,1,0:T(8,128)(2,1)S(1)}, bf16[2,8,2,48,512]{4,3,2,1,0:T(8,128)(2,1)S(1)}, u32[]{:S(2)}, u32[]{:S(2)}) collective-permute-start(bf16[2,8,2,48,512]{4,3,2,1,0:T(8,128)(2,1)S(1)} %join12.1.refs_8_.own_ref), channel_id=1, source_target_pairs={{0,1},{1,0},{2,3},{3,2},{4,5},{5,4},{6,7},{7,6},{8,9},{9,8},{10,11... | collective-permute-start | bytes 4718600 | tf_op jit(solution)/shard_map/core_rows12/ppermute | solution.py:351
  55.2 17.0 %collective-permute-start.14 = (bf16[2,1536,128]{2,1,0:T(8,128)(2,1)S(1)}, bf16[2,1536,128]{2,1,0:T(8,128)(2,1)S(1)}, u32[]{:S(2)}, u32[]{:S(2)}) collective-permute-start(bf16[2,1536,128]{2,1,0:T(8,128)(2,1)S(1)} %add_convert_fusion.3.refs_6_), channel_id=1, source_target_pairs={{0,4},{1,13},{2,6},{3,15},{4,8},{5,1},{6,10},{7,3},{8,12},{9,5},{1... | collective-permute-start | bytes 2359304 | tf_op jit(solution)/shard_map/ring0_2/ppermute | solution.py:351
  56.8 24.2 %collective-permute-start.15 = (bf16[2,384,512]{2,1,0:T(8,128)(2,1)S(1)}, bf16[2,384,512]{2,1,0:T(8,128)(2,1)S(1)}, u32[]{:S(2)}, u32[]{:S(2)}) collective-permute-start(bf16[2,384,512]{2,1,0:T(8,128)(2,1)S(1)} %get-tuple-element.106), channel_id=1, source_target_pairs={{0,1},{1,0},{2,3},{3,2},{4,5},{5,4},{6,7},{7,6},{8,9},{9,8},{10,11... | collective-permute-start | bytes 2359304 | tf_op jit(solution)/shard_map/core_back0/ppermute | solution.py:351
  72.4 23.6 %collective-permute-start.18 = (bf16[2,1536,128]{2,1,0:T(8,128)(2,1)S(1)}, bf16[2,1536,128]{2,1,0:T(8,128)(2,1)S(1)}, u32[]{:S(2)}, u32[]{:S(2)}) collective-permute-start(bf16[2,1536,128]{2,1,0:T(8,128)(2,1)S(1)} %add_convert_fusion.2.refs_6_), channel_id=1, source_target_pairs={{0,4},{1,13},{2,6},{3,15},{4,8},{5,1},{6,10},{7,3},{8,12},{9,5},{1... | collective-permute-start | bytes 2359304 | tf_op jit(solution)/shard_map/ring0_3/ppermute | solution.py:351
  72.5 8.5 %collective-permute-start.16 = (bf16[2,384,512]{2,1,0:T(8,128)(2,1)S(1)}, bf16[2,384,512]{2,1,0:T(8,128)(2,1)S(1)}, u32[]{:S(2)}, u32[]{:S(2)}) collective-permute-start(bf16[2,384,512]{2,1,0:T(8,128)(2,1)S(1)} %get-tuple-element.107), channel_id=1, source_target_pairs={{0,1},{1,0},{2,3},{3,2},{4,5},{5,4},{6,7},{7,6},{8,9},{9,8},{10,11... | collective-permute-start | bytes 2359304 | tf_op jit(solution)/shard_map/core_back1/ppermute | solution.py:351
  73.0 23.8 %collective-permute-start.19 = (bf16[2,1536,128]{2,1,0:T(8,128)(2,1)S(1)}, bf16[2,1536,128]{2,1,0:T(8,128)(2,1)S(1)}, u32[]{:S(2)}, u32[]{:S(2)}) collective-permute-start(bf16[2,1536,128]{2,1,0:T(8,128)(2,1)S(1)} %get-tuple-element.112), channel_id=1, source_target_pairs={{0,2},{1,3},{2,0},{3,1},{4,6},{5,7},{6,4},{7,5},{8,10},{9,11},{10,... | collective-permute-start | bytes 2359304 | tf_op jit(solution)/shard_map/cross1a/ppermute | solution.py:351
  78.6 1.2 copy-start.2
  79.8 17.0 %collective-permute-start.17 = (bf16[2,1536,128]{2,1,0:T(8,128)(2,1)S(1)}, bf16[2,1536,128]{2,1,0:T(8,128)(2,1)S(1)}, u32[]{:S(2)}, u32[]{:S(2)}) collective-permute-start(bf16[2,1536,128]{2,1,0:T(8,128)(2,1)S(1)} %get-tuple-element.108.refs_4_), channel_id=1, source_target_pairs={{0,4},{1,13},{2,6},{3,15},{4,8},{5,1},{6,10},{7,3},{8,12},{9,5},{1... | collective-permute-start | bytes 2359304 | tf_op jit(solution)/shard_map/ring2_1/ppermute | solution.py:351
  81.4 20.1 %collective-permute-start.23 = (bf16[2,2,2,48,512]{4,3,2,1,0:T(8,128)(2,1)S(1)}, bf16[2,2,2,48,512]{4,3,2,1,0:T(8,128)(2,1)S(1)}, u32[]{:S(2)}, u32[]{:S(2)}) collective-permute-start(bf16[2,2,2,48,512]{4,3,2,1,0:T(8,128)(2,1)S(1)} %get-tuple-element.120), channel_id=1, source_target_pairs={{0,96},{16,112},{32,0},{48,16},{64,32},{80,48},{96,64},{112,80},{1... | collective-permute-start | bytes 1179656 | tf_op jit(solution)/shard_map/rows_back01/ppermute | solution.py:355
  84.1 17.6 %collective-permute-start.24 = (bf16[2,2,2,48,512]{4,3,2,1,0:T(8,128)(2,1)S(1)}, bf16[2,2,2,48,512]{4,3,2,1,0:T(8,128)(2,1)S(1)}, u32[]{:S(2)}, u32[]{:S(2)}) collective-permute-start(bf16[2,2,2,48,512]{4,3,2,1,0:T(8,128)(2,1)S(1)} %get-tuple-element.121), channel_id=1, source_target_pairs={{0,64},{16,80},{32,96},{48,112},{64,0},{80,16},{96,32},{112,48},{1... | collective-permute-start | bytes 1179656 | tf_op jit(solution)/shard_map/rows_back01/ppermute | solution.py:355
  96.0 13.2 %collective-permute-start.25 = (bf16[2,2,2,48,512]{4,3,2,1,0:T(8,128)(2,1)S(1)}, bf16[2,2,2,48,512]{4,3,2,1,0:T(8,128)(2,1)S(1)}, u32[]{:S(2)}, u32[]{:S(2)}) collective-permute-start(bf16[2,2,2,48,512]{4,3,2,1,0:T(8,128)(2,1)S(1)} %get-tuple-element.122), channel_id=1, source_target_pairs={{0,32},{16,48},{32,64},{48,80},{64,96},{80,112},{96,0},{112,16},{1... | collective-permute-start | bytes 1179656 | tf_op jit(solution)/shard_map/rows_back01/ppermute | solution.py:355
  97.0 17.5 %collective-permute-start.20 = (bf16[2,1536,128]{2,1,0:T(8,128)(2,1)S(1)}, bf16[2,1536,128]{2,1,0:T(8,128)(2,1)S(1)}, u32[]{:S(2)}, u32[]{:S(2)}) collective-permute-start(bf16[2,1536,128]{2,1,0:T(8,128)(2,1)S(1)} %add_convert_fusion.1.refs_2_), channel_id=1, source_target_pairs={{0,4},{1,13},{2,6},{3,15},{4,8},{5,1},{6,10},{7,3},{8,12},{9,5},{1... | collective-permute-start | bytes 2359304 | tf_op jit(solution)/shard_map/ring2_2/ppermute | solution.py:351
  97.5 13.1 %collective-permute-start.22 = (bf16[2,384,512]{2,1,0:T(8,128)(2,1)S(1)}, bf16[2,384,512]{2,1,0:T(8,128)(2,1)S(1)}, u32[]{:S(2)}, u32[]{:S(2)}) collective-permute-start(bf16[2,384,512]{2,1,0:T(8,128)(2,1)S(1)} %get-tuple-element.117), channel_id=1, source_target_pairs={{0,1},{1,0},{2,3},{3,2},{4,5},{5,4},{6,7},{7,6},{8,9},{9,8},{10,11... | collective-permute-start | bytes 2359304 | tf_op jit(solution)/shard_map/core_back2/ppermute | solution.py:351
  101.5 12.9 %collective-permute-start.21 = (bf16[1536,128]{1,0:T(8,128)(2,1)S(1)}, bf16[1536,128]{1,0:T(8,128)(2,1)S(1)}, u32[]{:S(2)}, u32[]{:S(2)}) collective-permute-start(bf16[1536,128]{1,0:T(8,128)(2,1)S(1)} %fusion.2), channel_id=1, source_target_pairs={{0,4},{1,13},{2,6},{3,15},{4,8},{5,1},{6,10},{7,3},{8,12},{9,5},{1... | collective-permute-start | bytes 1179656 | tf_op jit(solution)/shard_map/ring1_1/ppermute | solution.py:351
  101.8 20.5 %collective-permute-start.13 = (bf16[2,1536,128]{2,1,0:T(8,128)(2,1)S(1)}, bf16[2,1536,128]{2,1,0:T(8,128)(2,1)S(1)}, u32[]{:S(2)}, u32[]{:S(2)}) collective-permute-start(bf16[2,1536,128]{2,1,0:T(8,128)(2,1)S(1)} %get-tuple-element.96), channel_id=1, source_target_pairs={{0,2},{1,3},{2,0},{3,1},{4,6},{5,7},{6,4},{7,5},{8,10},{9,11},{10,... | collective-permute-start | bytes 2359304 | tf_op jit(solution)/shard_map/cross1b/ppermute | solution.py:351
  109.2 21.2 %collective-permute-start.27 = (bf16[1536,128]{1,0:T(8,128)(2,1)S(1)}, bf16[1536,128]{1,0:T(8,128)(2,1)S(1)}, u32[]{:S(2)}, u32[]{:S(2)}) collective-permute-start(bf16[1536,128]{1,0:T(8,128)(2,1)S(1)} %get-tuple-element.152.refs_3_), channel_id=1, source_target_pairs={{0,2},{1,3},{2,0},{3,1},{4,6},{5,7},{6,4},{7,5},{8,10},{9,11},{10,... | collective-permute-start | bytes 1179656 | tf_op jit(solution)/shard_map/across0/ppermute | solution.py:351
  114.6 24.2 %collective-permute-start.28 = (bf16[2,1536,128]{2,1,0:T(8,128)(2,1)S(1)}, bf16[2,1536,128]{2,1,0:T(8,128)(2,1)S(1)}, u32[]{:S(2)}, u32[]{:S(2)}) collective-permute-start(bf16[2,1536,128]{2,1,0:T(8,128)(2,1)S(1)} %add_convert_fusion), channel_id=1, source_target_pairs={{0,4},{1,13},{2,6},{3,15},{4,8},{5,1},{6,10},{7,3},{8,12},{9,5},{1... | collective-permute-start | bytes 2359304 | tf_op jit(solution)/shard_map/ring2_3/ppermute | solution.py:351
  114.9 24.0 %collective-permute-start.26 = (bf16[1536,128]{1,0:T(8,128)(2,1)S(1)}, bf16[1536,128]{1,0:T(8,128)(2,1)S(1)}, u32[]{:S(2)}, u32[]{:S(2)}) collective-permute-start(bf16[1536,128]{1,0:T(8,128)(2,1)S(1)} %fusion.1), channel_id=1, source_target_pairs={{0,4},{1,13},{2,6},{3,15},{4,8},{5,1},{6,10},{7,3},{8,12},{9,5},{1... | collective-permute-start | bytes 1179656 | tf_op jit(solution)/shard_map/ring1_2/ppermute | solution.py:351
  116.6 15.0 %collective-permute-start.29 = (bf16[1,2,2,48,512]{4,3,2,1,0:T(8,128)(2,1)S(1)}, bf16[1,2,2,48,512]{4,3,2,1,0:T(8,128)(2,1)S(1)}, u32[]{:S(2)}, u32[]{:S(2)}) collective-permute-start(bf16[1,2,2,48,512]{4,3,2,1,0:T(8,128)(2,1)S(1)} %get-tuple-element.128), channel_id=1, source_target_pairs={{0,96},{16,112},{32,0},{48,16},{64,32},{80,48},{96,64},{112,80},{1... | collective-permute-start | bytes 589832 | tf_op jit(solution)/shard_map/rows_back2/ppermute | solution.py:355
  122.3 9.3 %collective-permute-start.30 = (bf16[1,2,2,48,512]{4,3,2,1,0:T(8,128)(2,1)S(1)}, bf16[1,2,2,48,512]{4,3,2,1,0:T(8,128)(2,1)S(1)}, u32[]{:S(2)}, u32[]{:S(2)}) collective-permute-start(bf16[1,2,2,48,512]{4,3,2,1,0:T(8,128)(2,1)S(1)} %get-tuple-element.129), channel_id=1, source_target_pairs={{0,64},{16,80},{32,96},{48,112},{64,0},{80,16},{96,32},{112,48},{1... | collective-permute-start | bytes 589832 | tf_op jit(solution)/shard_map/rows_back2/ppermute | solution.py:355
  130.4 8.5 %collective-permute-start.31 = (bf16[1,2,2,48,512]{4,3,2,1,0:T(8,128)(2,1)S(1)}, bf16[1,2,2,48,512]{4,3,2,1,0:T(8,128)(2,1)S(1)}, u32[]{:S(2)}, u32[]{:S(2)}) collective-permute-start(bf16[1,2,2,48,512]{4,3,2,1,0:T(8,128)(2,1)S(1)} %get-tuple-element.130), channel_id=1, source_target_pairs={{0,32},{16,48},{32,64},{48,80},{64,96},{80,112},{96,0},{112,16},{1... | collective-permute-start | bytes 589832 | tf_op jit(solution)/shard_map/rows_back2/ppermute | solution.py:355
  139.0 9.1 %collective-permute-start.33 = (bf16[1536,128]{1,0:T(8,128)(2,1)S(1)}, bf16[1536,128]{1,0:T(8,128)(2,1)S(1)}, u32[]{:S(2)}, u32[]{:S(2)}) collective-permute-start(bf16[1536,128]{1,0:T(8,128)(2,1)S(1)} %fusion), channel_id=1, source_target_pairs={{0,4},{1,13},{2,6},{3,15},{4,8},{5,1},{6,10},{7,3},{8,12},{9,5},{1... | collective-permute-start | bytes 1179656 | tf_op jit(solution)/shard_map/ring1_3/ppermute | solution.py:351
  142.3 22.0 %collective-permute-start.32 = (bf16[2,256,512]{2,1,0:T(8,128)(2,1)S(1)}, bf16[2,256,512]{2,1,0:T(8,128)(2,1)S(1)}, u32[]{:S(2)}, u32[]{:S(2)}) collective-permute-start(bf16[2,256,512]{2,1,0:T(8,128)(2,1)S(1)} %partner_sums.1), channel_id=1, source_target_pairs={{0,16},{16,0},{32,48},{48,32},{64,80},{80,64},{96,112},{112,96},{1... | collective-permute-start | bytes 1572872 | tf_op jit(solution)/shard_map/partner_out/ppermute | solution.py:439
  145.3 18.9 %copy-start.1 = (bf16[528,512]{1,0:T(8,128)(2,1)S(1)}, bf16[528,512]{1,0:T(8,128)(2,1)}, u32[]{:S(2)}) copy-start(bf16[528,512]{1,0:T(8,128)(2,1)} %pack.1.packed_ref) | copy-start | bytes 1622020
  145.3 17.7 %collective-permute-start.34 = (bf16[1536,128]{1,0:T(8,128)(2,1)S(1)}, bf16[1536,128]{1,0:T(8,128)(2,1)S(1)}, u32[]{:S(2)}, u32[]{:S(2)}) collective-permute-start(bf16[1536,128]{1,0:T(8,128)(2,1)S(1)} %get-tuple-element.149), channel_id=1, source_target_pairs={{0,2},{1,3},{2,0},{3,1},{4,6},{5,7},{6,4},{7,5},{8,10},{9,11},{10,... | collective-permute-start | bytes 1179656 | tf_op jit(solution)/shard_map/across2/ppermute | solution.py:351
